TPU v7x, 128 devices: a whole 4x4x4 slice. The times are simulated.
128 devices in a mesh: dp: 8 (over x, core), seq: 16 (over z, y).
Axes of the slice: x: 4, y: 4, z: 4, core: 2. Of those that a mesh axis runs over, the one named last changes fastest.
Arguments:
- tokens: bfloat16 [8, 2048, 768], P('dp', 'seq'), may hold values from -6 to 6
- params: bfloat16 [7094272], P(('dp', 'seq')), may hold values from -6 to 6, as said below
- out_grad: bfloat16 [8, 2048, 768], P('dp', 'seq'), may hold values from -6 to 6
Outputs:
- layer_out: bfloat16 [8, 2048, 768], P('dp', 'seq')
- input_grad: float32 [8, 2048, 768], P('dp', 'seq')
- param_grad: float32 [7094272], P(('dp', 'seq'))
Inputs may be any that keep to these rules, and one draw needn't show every extreme that they name: `params`: gains lie near 1.
All inputs are finite; a program needn't handle non-finite values.
Results may differ from a plain program's by a relative error of at most 0.0055.
Values may be sent and summed in bfloat16 or wider, within the bound.
A program may use at most 320 MiB of HBM per device.

v0:
```python
import functools

import jax
import jax.numpy as jnp
from jax import lax
from jax.experimental import pallas as pl
from jax.experimental.pallas import tpu as pltpu
from jax.sharding import Mesh
from jax.sharding import PartitionSpec as P

DP_SEQ = ("dp_0", "dp_1", "seq_0", "seq_1")
SEQ = ("seq_0", "seq_1")
DP = ("dp_0", "dp_1")
MESH = pl.DeviceIdType.MESH
ROWS = 448
PARTS = ((0, 144, (0, 2, 1)), (144, 144, (2, 1, 0)), (288, 160, (1, 0, 2)))


def place():
    return [lax.axis_index("dp_0"), lax.axis_index("seq_0"), lax.axis_index("seq_1")], lax.axis_index("dp_1")


def device(pos, core):
    return (pos[0], core, pos[1], pos[2])


def moved(pos, axis, by):
    out = list(pos)
    out[axis] = lax.rem(pos[axis] + by, 4)
    return out


def greet(pos, core, sibling=True):
    barrier = pltpu.get_barrier_semaphore()
    others = [device(moved(pos, a, by), core) for a in range(3) for by in (1, 3)]
    if sibling:
        others.append(device(pos, 1 - core))
    for other in others:
        pl.semaphore_signal(barrier, inc=1, device_id=other, device_id_type=MESH)
    pl.semaphore_wait(barrier, len(others))


def gather_kernel(own_ref, out_ref, send, recv, sib_send, sib_recv, local):
    pos, core = place()
    greet(pos, core)

    def region(part, where, c, start, size):
        idx = [slice(None) if w is None else w for w in where]
        return out_ref.at[idx[0], c, idx[1], idx[2], pl.ds(start, size), :]

    own = pltpu.make_async_copy(own_ref, out_ref.at[pos[0], core, pos[1], pos[2]], local)
    own.start()
    own.wait()
    sibs = []

    def to_sibling(number, part, where):
        start, size, _ = PARTS[part]
        ref = region(part, where, core, start, size)
        copy = pltpu.make_async_remote_copy(ref, ref, sib_send.at[part, number], sib_recv.at[part, number],
                                            device_id=device(pos, 1 - core), device_id_type=MESH)
        copy.start()
        sibs.append(copy)

    def push(part, phase, number, where, start, size, axis, by):
        ref = region(part, where, core, start, size)
        copy = pltpu.make_async_remote_copy(ref, ref, send.at[part, phase, number], recv.at[part, phase, number],
                                            device_id=device(moved(pos, axis, by), core), device_id_type=MESH)
        copy.start()
        return copy

    def before(order, phase):
        where = [pos[0], pos[1], pos[2]]
        for a in order[:phase]:
            where[a] = None
        return where

    for part in range(3):
        to_sibling(0, part, before(PARTS[part][2], 0))
    for phase in range(3):
        firsts, seconds = [], []
        for part in range(3):
            start, size, order = PARTS[part]
            axis = order[phase]
            where = before(order, phase)
            firsts.append((push(part, phase, 0, where, start, size, axis, 1), push(part, phase, 1, where, start, size, axis, 3)))
        for part in range(3):
            start, size, order = PARTS[part]
            axis = order[phase]
            up, down = firsts[part]
            half = size // 32 * 16
            left = before(order, phase)
            left[axis] = lax.rem(pos[axis] + 3, 4)
            right = before(order, phase)
            right[axis] = lax.rem(pos[axis] + 1, 4)
            up.wait_recv()
            one = push(part, phase, 2, left, start, half, axis, 1)
            to_sibling(1 + 3 * phase, part, left)
            down.wait_recv()
            two = push(part, phase, 3, right, start + half, size - half, axis, 3)
            to_sibling(2 + 3 * phase, part, right)
            seconds.append((one, two))
        for part in range(3):
            start, size, order = PARTS[part]
            axis = order[phase]
            one, two = seconds[part]
            one.wait_recv()
            two.wait_recv()
            far = before(order, phase)
            far[axis] = lax.rem(pos[axis] + 2, 4)
            to_sibling(3 + 3 * phase, part, far)
        for copy in [c for pair in firsts + seconds for c in pair]:
            copy.wait_send()
    for copy in sibs:
        copy.wait_send()
        copy.wait_recv()


def gather(own):
    return pl.pallas_call(
        gather_kernel,
        out_shape=jax.ShapeDtypeStruct((4, 2, 4, 4, ROWS, 128), jnp.bfloat16),
        in_specs=[pl.BlockSpec(memory_space=pl.ANY)],
        out_specs=pl.BlockSpec(memory_space=pl.ANY),
        scratch_shapes=[pltpu.SemaphoreType.DMA((3, 3, 4)), pltpu.SemaphoreType.DMA((3, 3, 4)),
                        pltpu.SemaphoreType.DMA((3, 10)), pltpu.SemaphoreType.DMA((3, 10)), pltpu.SemaphoreType.DMA],
        compiler_params=pltpu.CompilerParams(collective_id=0, has_side_effects=True),
    )(own)


EIGHTH = 16 * 433
W_QKV = (24, 768, 18)
W_OUT = (13866, 768, 6)
W_UP = (18480, 768, 24)
W_DOWN = (36936, 3072, 6)
VECTORS = {"ln1_gain": (0, 6), "ln1_shift": (6, 6), "ln2_gain": (12, 6), "ln2_shift": (18, 6),
           "b_qkv": (13848, 18), "b_out": (18474, 6), "b_up": (36912, 24), "b_down": (55368, 6)}


HEADS = 12
TILE = 1024
KEYS = 1024


def exchange_kernel(to_heads, in_ref, out_ref, send, recv, local):
    x, core = lax.axis_index("dp_0"), lax.axis_index("dp_1")
    me = lax.axis_index("seq_0") * 4 + lax.axis_index("seq_1")
    barrier = pltpu.get_barrier_semaphore()
    others = [lax.rem(me + k, 16) for k in range(1, 16)]
    where = lambda t: (x, core, lax.div(t, 4), lax.rem(t, 4))
    for t in others:
        pl.semaphore_signal(barrier, inc=1, device_id=where(t), device_id_type=MESH)
    pl.semaphore_wait(barrier, 15)

    def copy(t):
        return pltpu.make_async_remote_copy(in_ref.at[t], out_ref.at[me], send.at[t], recv.at[me],
                                            device_id=where(t), device_id_type=MESH)

    def arrival(t):
        return pltpu.make_async_remote_copy(out_ref.at[t], out_ref.at[t], send.at[t], recv.at[t],
                                            device_id=where(t), device_id_type=MESH)

    own = pltpu.make_async_copy(in_ref.at[me], out_ref.at[me], local)
    if to_heads:
        for t in others:
            pl.when(t < HEADS)(lambda t=t: copy(t).start())

        @pl.when(me < HEADS)
        def _():
            own.start()
            for t in others:
                arrival(t).wait_recv()
            own.wait()
        for t in others:
            pl.when(t < HEADS)(lambda t=t: copy(t).wait_send())
    else:
        @pl.when(me < HEADS)
        def _():
            for t in others:
                copy(t).start()
            own.start()
        for t in others:
            pl.when(t < HEADS)(lambda t=t: arrival(t).wait_recv())

        @pl.when(me < HEADS)
        def _():
            for t in others:
                copy(t).wait_send()
            own.wait()


def exchange(blocks, to_heads):
    count = 16 if to_heads else HEADS
    return pl.pallas_call(
        functools.partial(exchange_kernel, to_heads),
        out_shape=jax.ShapeDtypeStruct((count,) + blocks.shape[1:], blocks.dtype),
        in_specs=[pl.BlockSpec(memory_space=pl.ANY)],
        out_specs=pl.BlockSpec(memory_space=pl.ANY),
        scratch_shapes=[pltpu.SemaphoreType.DMA((16,)), pltpu.SemaphoreType.DMA((16,)), pltpu.SemaphoreType.DMA],
        compiler_params=pltpu.CompilerParams(collective_id=2 if to_heads else 3, has_side_effects=True),
    )(blocks)


NT = (((1,), (1,)), ((), ()))


def product(a, b, dims=(((1,), (0,)), ((), ()))):
    return lax.dot_general(a, b, dims, preferred_element_type=jnp.float32)


def head_kernel(in_ref, out_ref, k, v, kt, vt, scores, dk, dv):
    blocks = 2048 // TILE
    per = TILE // 128

    def rows(which, i):
        return jnp.concatenate([in_ref[i * per + p, which] for p in range(per)], 0)

    @pl.loop(0, blocks)
    def _(i):
        at = pl.ds(pl.multiple_of(i * TILE, TILE), TILE)
        key = rows(0, i)[:, 64:]
        value = rows(1, i)[:, :64]
        k[at, :] = key
        v[at, :] = value
        kt[:, at] = key.T
        vt[:, at] = value.T
        dk[at, :] = jnp.zeros((TILE, 64), jnp.float32)
        dv[at, :] = jnp.zeros((TILE, 64), jnp.float32)

    @pl.loop(0, blocks)
    def _(i):
        query = rows(0, i)[:, :64] * jnp.bfloat16(0.125)
        grad = rows(1, i)[:, 64:]

        def tile(j):
            return pl.ds(pl.multiple_of(j * KEYS, KEYS), KEYS)

        last = lax.div(i * TILE, KEYS)

        def first(j, top):
            s = product(k[tile(j), :], query, NT)
            scores[tile(j), :] = s
            return jnp.maximum(top, jnp.max(s, 0, keepdims=True))

        top = lax.fori_loop(0, last, first, jnp.full((1, TILE), -1e30, jnp.float32))
        s = product(k[tile(last), :], query, NT)
        keep = lax.broadcasted_iota(jnp.int32, (KEYS, TILE), 0) - lax.broadcasted_iota(jnp.int32, (KEYS, TILE), 1) <= i * TILE - last * KEYS
        s = jnp.where(keep, s, -1e30)
        scores[tile(last), :] = s
        top = jnp.maximum(top, jnp.max(s, 0, keepdims=True))

        def second(j, carry):
            total, out = carry
            e = jnp.exp(scores[tile(j), :] - top)
            scores[tile(j), :] = e
            return total + jnp.sum(e, 0, keepdims=True), out + product(vt[:, tile(j)], e.astype(jnp.bfloat16))

        total, out = lax.fori_loop(0, last + 1, second, (jnp.zeros((1, TILE), jnp.float32), jnp.zeros((64, TILE), jnp.float32)))
        scale = 1.0 / total
        out = out * scale
        inner = jnp.sum(out * grad.astype(jnp.float32).T, 0, keepdims=True)

        def third(j, dq):
            p = scores[tile(j), :] * scale
            dp = product(v[tile(j), :], grad, NT)
            ds = (p * (dp - inner)).astype(jnp.bfloat16)
            dv[tile(j), :] += product(p.astype(jnp.bfloat16), grad)
            dk[tile(j), :] += product(ds, query)
            return dq + product(kt[:, tile(j)], ds)

        dq = lax.fori_loop(0, last + 1, third, jnp.zeros((64, TILE), jnp.float32)) * 0.125
        both = jnp.concatenate([out, dq], 0).T.astype(jnp.bfloat16)
        for p in range(per):
            out_ref[i * per + p, 0] = both[128 * p:128 * (p + 1)]

    @pl.loop(0, blocks)
    def _(i):
        at = pl.ds(pl.multiple_of(i * TILE, TILE), TILE)
        both = jnp.concatenate([dk[at, :], dv[at, :]], 1).astype(jnp.bfloat16)
        for p in range(per):
            out_ref[i * per + p, 1] = both[128 * p:128 * (p + 1)]


def heads(blocks):
    return pl.pallas_call(
        head_kernel,
        out_shape=jax.ShapeDtypeStruct((16, 2, 128, 128), jnp.bfloat16),
        in_specs=[pl.BlockSpec(memory_space=pltpu.VMEM)],
        out_specs=pl.BlockSpec(memory_space=pltpu.VMEM),
        scratch_shapes=[pltpu.VMEM((2048, 64), jnp.bfloat16), pltpu.VMEM((2048, 64), jnp.bfloat16),
                        pltpu.VMEM((64, 2048), jnp.bfloat16), pltpu.VMEM((64, 2048), jnp.bfloat16),
                        pltpu.VMEM((2048, TILE), jnp.float32),
                        pltpu.VMEM((2048, 64), jnp.float32), pltpu.VMEM((2048, 64), jnp.float32)],
        compiler_params=pltpu.CompilerParams(vmem_limit_bytes=32 * 2**20),
    )(blocks)


EPS = 1e-05
ORDER = ("ln1_gain", "ln1_shift", "ln2_gain", "ln2_shift", "b_qkv", "b_out", "b_up", "b_down")


def widen(g_ref, flat, step):
    @pl.loop(0, 16)
    def _(k):
        base = (step * 16 + k) * 433
        flat[pl.ds(base, 440), :] = g_ref[k, 0:440, :].astype(jnp.float32)


def unpack_matrix(flat, first, where, out, size=64):
    offset, rows, blocks = where
    start = offset - first * EIGHTH

    @pl.loop(0, rows // size)
    def _(i):
        for j in range(blocks):
            piece = flat[pl.ds(start + j + i * (size * blocks), size, stride=blocks), :]
            out[pl.ds(pl.multiple_of(i * size, size), size), 128 * j:128 * (j + 1)] = piece.astype(jnp.bfloat16)


def as_row(ref, start, count):
    return jnp.concatenate([ref[start + n:start + n + 1, :] for n in range(count)], 1)


def to_rows(ref, start, row):
    for n in range(row.shape[1] // 128):
        ref[start + n:start + n + 1, :] = row[:, 128 * n:128 * (n + 1)]


def normalized(values):
    center = jnp.mean(values, -1, keepdims=True)
    centered = values - center
    factor = lax.rsqrt(jnp.mean(centered * centered, -1, keepdims=True) + EPS)
    return centered * factor, factor


def turn(x, tables, sign):
    return x * tables[0] + (pltpu.roll(x, 120, 1) * tables[1] + pltpu.roll(x, 8, 1) * tables[2]) * sign


def first_kernel(g_ref, tokens_ref, grad_ref, tables_ref, w_qkv, w_out, blocks_ref, h1t_ref, h2_ref, h2t_ref, vec_ref, flat, wide):
    step = pl.program_id(0)
    widen(g_ref, flat, step)

    @pl.when(step == 1)
    def _():
        unpack_matrix(flat, 0, W_QKV, w_qkv)

    @pl.when(step == 2)
    def _():
        unpack_matrix(flat, 0, W_OUT, w_out)
        vec_ref[0:24, :] = flat[0:24, :]
        start = VECTORS["b_out"][0]
        vec_ref[24:30, :] = flat[start:start + 6, :]
        normal, _ = normalized(tokens_ref[...].astype(jnp.float32))
        h1 = (normal * as_row(flat, 0, 6) + as_row(flat, 6, 6)).astype(jnp.bfloat16)
        h2 = (normal * as_row(flat, 12, 6) + as_row(flat, 18, 6)).astype(jnp.bfloat16)
        h1t_ref[...] = h1.T
        h2_ref[...] = h2
        h2t_ref[...] = h2.T
        for n in range(9):
            start = VECTORS["b_qkv"][0] + 2 * n
            wide[:, 256 * n:256 * (n + 1)] = product(h1, w_qkv[:, 256 * n:256 * (n + 1)]) + as_row(flat, start, 2)
        low = lax.broadcasted_iota(jnp.int32, (128, 128), 1) < 64
        for m in range(6):
            q, k, v = (wide[:, 768 * p + 128 * m:768 * p + 128 * (m + 1)] for p in range(3))
            q = turn(q, tables_ref, 1.0)
            k = turn(k, tables_ref, 1.0)
            a = product(grad_ref[...], w_out[128 * m:128 * (m + 1), :], NT)
            swap = lambda t: pltpu.roll(t, 64, 1)
            blocks_ref[2 * m, 0] = jnp.where(low, q, swap(k)).astype(jnp.bfloat16)
            blocks_ref[2 * m + 1, 0] = jnp.where(low, swap(q), k).astype(jnp.bfloat16)
            blocks_ref[2 * m, 1] = jnp.where(low, v, swap(a)).astype(jnp.bfloat16)
            blocks_ref[2 * m + 1, 1] = jnp.where(low, swap(v), a).astype(jnp.bfloat16)


def const(*shape):
    return pl.BlockSpec(shape, lambda e: (0,) * len(shape))


def first_part(gathered, tokens, grad, tables):
    bf = lambda *s: jax.ShapeDtypeStruct(s, jnp.bfloat16)
    outs = [bf(768, 2304), bf(768, 768), bf(HEADS, 2, 128, 128), bf(768, 128), bf(128, 768), bf(768, 128),
            jax.ShapeDtypeStruct((32, 128), jnp.float32)]
    return pl.pallas_call(
        first_kernel,
        grid=(3,),
        out_shape=outs,
        in_specs=[pl.BlockSpec((16, 448, 128), lambda e: (e, 0, 0)), const(128, 768), const(128, 768), const(3, 128, 128)],
        out_specs=[const(*o.shape) for o in outs],
        scratch_shapes=[pltpu.VMEM((3 * EIGHTH + 16, 128), jnp.float32), pltpu.VMEM((128, 2304), jnp.float32)],
        compiler_params=pltpu.CompilerParams(vmem_limit_bytes=48 * 2**20),
    )(gathered, tokens, grad, tables)


def gelu_pair(u):
    inside = 0.5 * (1.0 + lax.erf(u * 0.7071067811865476))
    return u * inside, inside + u * jnp.exp(-0.5 * u * u) * 0.3989422804014327


def second_kernel(g_ref, h2_ref, grad_ref, mlp_ref, dh2_ref, act_t_ref, dup_ref, bias_ref, flat, w_up, w_down, act, slope):
    step = pl.program_id(0)
    widen(g_ref, flat, step)

    @pl.when(step == 3)
    def _():
        unpack_matrix(flat, 2, W_UP, w_up)
        start = VECTORS["b_up"][0] - 2 * EIGHTH
        for n in range(12):
            at = slice(256 * n, 256 * (n + 1))
            up = product(h2_ref[...], w_up[:, at]) + as_row(flat, start + 2 * n, 2)
            value, slope[:, at] = gelu_pair(up)
            value = value.astype(jnp.bfloat16)
            act[:, at] = value
            act_t_ref[at, :] = value.T

    @pl.when(step == 5)
    def _():
        unpack_matrix(flat, 2, W_DOWN, w_down, 128)
        start = VECTORS["b_down"][0] - 2 * EIGHTH
        for n in range(3):
            at = slice(256 * n, 256 * (n + 1))
            mlp_ref[:, at] = product(act[...], w_down[:, at]) + as_row(flat, start + 2 * n, 2)
        for n in range(12):
            at = slice(256 * n, 256 * (n + 1))
            dup = (product(grad_ref[...], w_down[at, :], NT) * slope[:, at]).astype(jnp.bfloat16)
            dup_ref[:, at] = dup
            to_rows(bias_ref, 2 * n, jnp.sum(dup.astype(jnp.float32), 0, keepdims=True))
        for n in range(3):
            at = slice(256 * n, 256 * (n + 1))
            dh2_ref[:, at] = product(dup_ref[...], w_up[at, :], NT)


def second_part(gathered, h2, grad):
    bf = lambda *s: jax.ShapeDtypeStruct(s, jnp.bfloat16)
    f32 = lambda *s: jax.ShapeDtypeStruct(s, jnp.float32)
    outs = [f32(128, 768), f32(128, 768), bf(3072, 128), bf(128, 3072), f32(24, 128)]
    return pl.pallas_call(
        second_kernel,
        grid=(6,),
        out_shape=outs,
        in_specs=[pl.BlockSpec((16, 448, 128), lambda e: (e + 2, 0, 0)), const(128, 768), const(128, 768)],
        out_specs=[const(*o.shape) for o in outs],
        scratch_shapes=[pltpu.VMEM((6 * EIGHTH + 16, 128), jnp.float32), pltpu.VMEM((768, 3072), jnp.bfloat16),
                        pltpu.VMEM((3072, 768), jnp.bfloat16), pltpu.VMEM((128, 3072), jnp.bfloat16),
                        pltpu.VMEM((128, 3072), jnp.float32)],
        compiler_params=pltpu.CompilerParams(vmem_limit_bytes=56 * 2**20),
    )(gathered, h2, grad)


def third_kernel(back_ref, tokens_ref, grad_ref, tables_ref, w_qkv, w_out, mlp_ref, dh2_ref, bias_ref, in_vec,
                 layer_ref, input_ref, att_t_ref, dqkv_ref, vec_ref):
    low = lax.broadcasted_iota(jnp.int32, (128, 128), 1) < 64
    swap = lambda t: pltpu.roll(t, 64, 1)
    f32 = lambda t: t.astype(jnp.float32)
    attended = []
    for m in range(6):
        a, b = f32(back_ref[2 * m, 0]), f32(back_ref[2 * m + 1, 0])
        c, d = f32(back_ref[2 * m, 1]), f32(back_ref[2 * m + 1, 1])
        attended.append(jnp.where(low, a, swap(b)).astype(jnp.bfloat16))
        dq = turn(jnp.where(low, swap(a), b), tables_ref, -1.0)
        dk = turn(jnp.where(low, c, swap(d)), tables_ref, -1.0)
        dv = jnp.where(low, swap(c), d)
        for p, part in enumerate((dq, dk, dv)):
            dqkv_ref[:, 768 * p + 128 * m:768 * p + 128 * (m + 1)] = part.astype(jnp.bfloat16)
    attended = jnp.concatenate(attended, 1)
    att_t_ref[...] = attended.T
    tokens = f32(tokens_ref[...])
    grad = f32(grad_ref[...])
    layer_ref[...] = (tokens + (product(attended, w_out[...]) + as_row(in_vec, 24, 6)) + mlp_ref[...]).astype(jnp.bfloat16)
    normal, factor = normalized(tokens)
    total = grad
    row = 0
    for gain_at, dh in ((0, product(dqkv_ref[...], w_qkv[...], NT)), (12, dh2_ref[...])):
        to_rows(vec_ref, row, jnp.sum(dh * normal, 0, keepdims=True))
        to_rows(vec_ref, row + 6, jnp.sum(dh, 0, keepdims=True))
        row += 12
        scaled = dh * as_row(in_vec, gain_at, 6)
        inner = scaled - jnp.mean(scaled, -1, keepdims=True) - normal * jnp.mean(scaled * normal, -1, keepdims=True)
        total = total + factor * inner
    input_ref[...] = total
    to_rows(vec_ref, 24, jnp.sum(f32(dqkv_ref[...]), 0, keepdims=True))
    shift = jnp.sum(grad, 0, keepdims=True)
    to_rows(vec_ref, 42, shift)
    vec_ref[48:72, :] = bias_ref[...]
    to_rows(vec_ref, 72, shift)
    vec_ref[78:80, :] = jnp.zeros((2, 128), jnp.float32)


def third_part(*args):
    bf = lambda *s: jax.ShapeDtypeStruct(s, jnp.bfloat16)
    f32 = lambda *s: jax.ShapeDtypeStruct(s, jnp.float32)
    outs = [bf(128, 768), f32(128, 768), bf(768, 128), bf(128, 2304), f32(80, 128)]
    whole = pl.BlockSpec(memory_space=pltpu.VMEM)
    return pl.pallas_call(
        third_kernel,
        out_shape=outs,
        in_specs=[whole] * len(args),
        out_specs=[whole] * len(outs),
        compiler_params=pltpu.CompilerParams(vmem_limit_bytes=32 * 2**20),
    )(*args)


def rotary_tables(positions):
    lane = jnp.arange(128) % 64
    freq = jnp.tile(10000.0 ** (-jnp.arange(8).astype(jnp.float32) * 2.0 / 16), 16)
    angles = positions.astype(jnp.float32)[:, None] * freq[None, :]
    cosine, sine = jnp.cos(angles), jnp.sin(angles)
    return jnp.stack([jnp.where(lane < 16, cosine, 1.0), jnp.where(lane < 8, -sine, 0.0),
                      jnp.where((lane >= 8) & (lane < 16), sine, 0.0)])


MARGIN = 384
CHUNK = 128


def weight_kernel(core_ref, vec_ref, *refs):
    mine, theirs, (out_ref, flat), pair = refs[:7], refs[7:14], refs[14:16], refs[16:]
    step = pl.program_id(0)
    core = core_ref[0]

    @pl.when(step == 0)
    def _():
        for n in range(7):
            if n < 4:
                pair[n][:, :128] = mine[n][...]
                pair[n][:, 128:] = theirs[n][...]
            else:
                pair[n][:128, :] = mine[n][...]
                pair[n][128:, :] = theirs[n][...]

    h1_ref, att_ref, h2_ref, act_ref, dqkv_ref, g_ref, dup_ref = pair
    pairs = ((W_QKV, h1_ref, dqkv_ref), (W_OUT, att_ref, g_ref), (W_UP, h2_ref, dup_ref), (W_DOWN, act_ref, g_ref))

    def eighth(number):
        low, high = number * EIGHTH, (number + 1) * EIGHTH
        at = MARGIN - low
        for (offset, rows, blocks), left, right in pairs:
            first = max(0, (low - offset) // blocks) // 16 * 16
            last = min(rows, -(-(high - offset) // blocks))
            last = -(-last // 16) * 16
            if last <= first:
                continue
            size = min(CHUNK, last - first)
            count = -(-(last - first) // size)
            base = offset + at

            @pl.loop(0, count)
            def _(i, first=first, last=last, size=size, blocks=blocks, base=base, left=left, right=right):
                row = pl.multiple_of(jnp.minimum(first + i * size, last - size), 16)
                lhs = left[pl.ds(row, size), :]

                @pl.loop(0, blocks // 2, unroll=3)
                def _(j):
                    rhs = right[:, pl.ds(pl.multiple_of(j * 256, 256), 256)]
                    product = jnp.dot(lhs, rhs, preferred_element_type=jnp.float32)
                    start = base + row * blocks + 2 * j
                    flat[pl.ds(start, size, stride=blocks), :] = product[:, :128]
                    flat[pl.ds(start + 1, size, stride=blocks), :] = product[:, 128:]

        row = 0
        for name in ORDER:
            start, count = VECTORS[name]
            lo, hi = max(start, low), min(start + count, high)
            if lo < hi:
                flat[lo + at:hi + at, :] = vec_ref[row + lo - start:row + hi - start, :]
            row += count
        end = 55374
        if high > end:
            flat[end + at:high + at, :] = jnp.zeros((high - end, 128), jnp.float32)

    for t in range(4):
        for c in range(2):
            pl.when((step == t) & (core == c))(lambda number=2 * t + c: eighth(number))

    @pl.loop(0, 16)
    def _(k):
        out_ref[0, k] = flat[pl.ds(MARGIN + 433 * k, 448), :].astype(jnp.bfloat16)


def weight_grads(core, vec, mine, theirs):
    whole = pl.BlockSpec(memory_space=pltpu.VMEM)
    pairs = [(r, 256) for r in (768, 768, 768, 3072)] + [(256, c) for c in (2304, 768, 3072)]
    return pl.pallas_call(
        weight_kernel,
        grid=(4,),
        out_shape=jax.ShapeDtypeStruct((4, 16, 448, 128), jnp.bfloat16),
        in_specs=[pl.BlockSpec(memory_space=pltpu.SMEM)] + [whole] * 15,
        out_specs=pl.BlockSpec((1, 16, 448, 128), lambda e: (e, 0, 0, 0)),
        scratch_shapes=[pltpu.VMEM((EIGHTH + 2 * MARGIN, 128), jnp.float32)] + [pltpu.VMEM(p, jnp.bfloat16) for p in pairs],
        compiler_params=pltpu.CompilerParams(vmem_limit_bytes=48 * 2**20),
    )(core, vec, *mine, *theirs)


def halves(size):
    half = size // 32 * 16
    return half, size - half


def pick(ref, axes, axis, index, start, size):
    idx = tuple(index if a == axis else slice(None) for a in axes)
    return ref.at[idx + (pl.ds(start, size), slice(None))]


def each(count, body):
    if count == 0:
        body(())
        return
    @pl.loop(0, 4 ** count)
    def _(n):
        body(tuple(lax.rem(lax.div(n, 4 ** (count - 1 - d)), 4) for d in range(count)))


def scatter_kernel(in_ref, out_ref, *scratch):
    send, recv = scratch[-2:]
    bufs = list(scratch[:-2])
    pos, core = place()
    greet(pos, core, sibling=False)
    take = iter(bufs)
    got = {}
    for part in range(3):
        for phase in range(3):
            got[part, phase] = [next(take) for _ in range(9 if phase < 2 else 8)]

    def push(part, phase, number, src, dst, axis, by):
        copy = pltpu.make_async_remote_copy(src, dst, send.at[part, phase, number], recv.at[part, phase, number],
                                            device_id=device(moved(pos, axis, by), core), device_id_type=MESH)
        copy.start()
        return copy

    def current(part, phase):
        start, size, order = PARTS[part]
        axes = [0, 1, 2]
        for a in order[::-1][:phase]:
            axes.remove(a)
        if phase == 0:
            return in_ref, axes, start
        return got[part, phase - 1][8], axes, 0

    copies = {}

    def begin(part, phase):
        ref, axes, base = current(part, phase)
        start, size, order = PARTS[part]
        axis = order[2 - phase]
        h0, h1 = halves(size)
        q = pos[axis]
        far, right, left = (lax.rem(q + k, 4) for k in (2, 1, 3))
        b = got[part, phase]
        copies[part, phase] = [
            push(part, phase, 0, pick(ref, axes, axis, far, base, h0), b[0], axis, 1),
            push(part, phase, 1, pick(ref, axes, axis, far, base + h0, h1), b[1], axis, 3),
            push(part, phase, 2, pick(ref, axes, axis, right, base + h0, h1), b[2], axis, 1),
            push(part, phase, 3, pick(ref, axes, axis, left, base, h0), b[3], axis, 3),
        ]

    def add(ref, axes, axis, index, base, size, others, put):
        rest = [a for a in axes if a != axis]

        def body(at):
            full = dict(zip(rest, at))
            idx = tuple(index if a == axis else full[a] for a in axes)
            total = ref[idx + (pl.ds(base, size), slice(None))].astype(jnp.float32)
            for other in others:
                total = total + other[at + (slice(None), slice(None))].astype(jnp.float32)
            put(at, total)

        each(len(rest), body)

    def middle(part, phase):
        ref, axes, base = current(part, phase)
        start, size, order = PARTS[part]
        axis = order[2 - phase]
        h0, h1 = halves(size)
        q = pos[axis]
        right, left = (lax.rem(q + k, 4) for k in (1, 3))
        b = got[part, phase]
        c = copies[part, phase]

        def to(ref):
            def put(at, total):
                ref[at + (slice(None), slice(None))] = total.astype(jnp.bfloat16)
            return put

        c[0].wait_recv()
        add(ref, axes, axis, right, base, h0, [b[0]], to(b[6]))
        c.append(push(part, phase, 4, b[6], b[4], axis, 1))
        c[1].wait_recv()
        add(ref, axes, axis, left, base + h0, h1, [b[1]], to(b[7]))
        c.append(push(part, phase, 5, b[7], b[5], axis, 3))

    def finish(part, phase):
        ref, axes, base = current(part, phase)
        start, size, order = PARTS[part]
        axis = order[2 - phase]
        h0, h1 = halves(size)
        q = pos[axis]
        b = got[part, phase]
        c = copies[part, phase]
        for copy in c[2:]:
            copy.wait_recv()
        for lo, n, others in ((0, h0, [b[3], b[4]]), (h0, h1, [b[2], b[5]])):
            def put(at, total, lo=lo, n=n):
                if phase == 2:
                    out_ref[start + lo:start + lo + n, :] = total
                else:
                    b[8][at + (pl.ds(lo, n), slice(None))] = total.astype(jnp.bfloat16)
            add(ref, axes, axis, q, base + lo, n, others, put)

    for phase in range(3):
        for part in range(3):
            if phase == 0:
                begin(part, 0)
        for part in range(3):
            middle(part, phase)
        for part in range(3):
            finish(part, phase)
            if phase < 2:
                begin(part, phase + 1)
    for c in copies.values():
        for copy in c:
            copy.wait_send()


def scatter(parts):
    scratch = []
    for part in range(3):
        _, size, _ = PARTS[part]
        h0, h1 = halves(size)
        for phase in range(3):
            lead = (4,) * (2 - phase)
            sizes = [h0, h1, h1, h0, h0, h1, h0, h1] + ([size] if phase < 2 else [])
            scratch += [pltpu.VMEM(lead + (n, 128), jnp.bfloat16) for n in sizes]
    scratch += [pltpu.SemaphoreType.DMA((3, 3, 6)), pltpu.SemaphoreType.DMA((3, 3, 6))]
    return pl.pallas_call(
        scatter_kernel,
        out_shape=jax.ShapeDtypeStruct((ROWS, 128), jnp.float32),
        in_specs=[pl.BlockSpec(memory_space=pltpu.VMEM)],
        out_specs=pl.BlockSpec(memory_space=pltpu.VMEM),
        scratch_shapes=scratch,
        compiler_params=pltpu.CompilerParams(collective_id=1, has_side_effects=True, vmem_limit_bytes=40 * 2**20),
    )(parts)


def twin(array):
    return lax.ppermute(array, "dp_1", [(0, 1), (1, 0)])


def body(tokens, params, out_grad):
    piece = tokens.shape[1]
    x, grad = tokens[0], out_grad[0]
    own = jnp.pad(params.reshape(433, 128), ((0, ROWS - 433), (0, 0)))
    gathered = gather(own).reshape(128, ROWS, 128)
    tables = rotary_tables(lax.axis_index(SEQ) * piece + jnp.arange(piece))
    w_qkv, w_out, blocks, h1t, h2, h2t, in_vec = first_part(gathered, x, grad, tables)
    back = exchange(heads(exchange(blocks, True)), False)
    mlp, dh2, act_t, dup, bias = second_part(gathered, h2, grad)
    layer_out, input_grad, att_t, dqkv, vec = third_part(
        back, x, grad, tables, w_qkv, w_out, mlp, dh2, bias, in_vec
    )
    vec = vec + twin(vec)
    core = lax.axis_index("dp_1").astype(jnp.int32).reshape(1)
    mine = (h1t, att_t, h2t, act_t, dqkv, grad, dup)
    halves_sum = weight_grads(core, vec, mine, tuple(twin(a) for a in mine))
    param_grad = scatter(halves_sum.reshape(4, 4, 4, ROWS, 128))[:433].reshape(-1)
    return layer_out[None], input_grad[None], param_grad


def solution(mesh):
    finer = Mesh(mesh.devices.reshape(4, 2, 4, 4), DP_SEQ)
    in_specs = (P(DP, SEQ, None), P(DP_SEQ), P(DP, SEQ, None))
    out_specs = (P(DP, SEQ, None), P(DP, SEQ, None), P(DP_SEQ))
    return jax.shard_map(body, mesh=finer, in_specs=in_specs, out_specs=out_specs, check_vma=False)
```

profile of v0, /device:TPU:0, one launch (start us, length us, event | category | flops | bytes accessed | tf_op | source)
XLA Modules:
  0.0 219.8 jit_solution(4315013361341729647)
XLA Ops:
  0.8 1.6 pad.4.own_ref
  2.3 54.2 %shard_map.58 = bf16[4,2,4,4,448,128]{5,4,3,2,1,0:T(8,128)(2,1)} custom-call(bf16[448,128]{1,0:T(8,128)(2,1)} %pad.4.own_ref), custom_call_target="tpu_custom_call" | custom-call | tf_op jit(solution)/shard_map/pallas_call | solution.py:119
  57.0 7.0 %shard_map.59 = (bf16[768,2304]{1,0:T(8,128)(2,1)}, bf16[768,768]{1,0:T(8,128)(2,1)S(1)}, bf16[12,2,128,128]{3,2,1,0:T(8,128)(2,1)S(1)}, bf16[768,128]{1,0:T(8,1...) custom-call(bf16[128,448,128]{2,1,0:T(8,128)(2,1)} %bitcast.13, ...), custom_call_target="tpu_custom_call" | custom-call | tf_op jit(solution)/shard_map/pallas_call | solution.py:383
  64.0 1.0 copy-done.7
  67.9 15.7 %shard_map.63 = (f32[128,768]{1,0:T(8,128)}, f32[128,768]{1,0:T(8,128)}, bf16[3072,128]{1,0:T(8,128)(2,1)}, bf16[128,3072]{1,0:T(8,128)(2,1)}, f32[24,128]{1,0:T(8,128)}) custom-call(bf16[128,448,128]{2,1,0:T(8,128)(2,1)} %bitcast.14, bf16[128,768]{1,0:T(8,128)(2,1)} %copy-done.16, bf16[128,768]{1,0:T(8,128)(2,1)} %bitcast.3.grad_ref.refs_5_), custom_call_target="tpu_custom_call" | custom-call | tf_op jit(solution)/shard_map/pallas_call | solution.py:436
  84.2 18.7 %shard_map.60.in_ref = bf16[16,2,128,128]{3,2,1,0:T(8,128)(2,1)} custom-call(bf16[12,2,128,128]{3,2,1,0:T(8,128)(2,1)} %copy-done.11), custom_call_target="tpu_custom_call" | custom-call | tf_op jit(solution)/shard_map/pallas_call | solution.py:193
  103.0 1.2 copy-done.1
  104.2 14.0 %shard_map.61.in_ref = bf16[16,2,128,128]{3,2,1,0:T(8,128)(2,1)S(1)} custom-call(bf16[16,2,128,128]{3,2,1,0:T(8,128)(2,1)S(1)} %copy-done.1), custom_call_target="tpu_custom_call" | custom-call | tf_op jit(solution)/shard_map/pallas_call | solution.py:284
  118.2 1.0 copy-done.2
  119.2 19.1 %shard_map.62.back_ref = bf16[12,2,128,128]{3,2,1,0:T(8,128)(2,1)} custom-call(bf16[16,2,128,128]{3,2,1,0:T(8,128)(2,1)} %copy-done.2), custom_call_target="tpu_custom_call" | custom-call | tf_op jit(solution)/shard_map/pallas_call | solution.py:193
  138.3 1.1 copy-done.4
  139.4 0.9 copy-done.6
  140.3 1.3 copy-done.8
  141.6 0.9 copy-done.13
  142.5 1.0 copy-done.14
  143.5 1.0 copy-done.15
  145.2 4.0 %shard_map.64 = (bf16[128,768]{1,0:T(8,128)(2,1)}, f32[128,768]{1,0:T(8,128)}, bf16[768,128]{1,0:T(8,128)(2,1)S(1)}, bf16[128,2304]{1,0:T(8,128)(2,1)}, f32[80,128]{1,0:T(8,128)S(1)}) custom-call(bf16[12,2,128,128]{3,2,1,0:T(8,128)(2,1)S(1)} %copy-done.4, bf16[128,768]{1,0:T(8,128)(2,1)S(1)} %bitcast.12, bf16[128,768]{1,0:T(8,128)(2,1)} %bitcast.3.grad_ref.refs_5_, ...), custom_call_target="tpu_custom_call" | custom-call | tf_op jit(solution)/shard_map/pallas_call | solution.py:493
  154.2 1.1 copy-done.9
  155.3 1.1 copy-done.10
  156.5 0.9 copy-done.18
  157.4 0.9 copy-done.20
  159.2 13.9 %shard_map.65 = bf16[4,16,448,128]{3,2,1,0:T(8,128)(2,1)} custom-call(s32[1]{0:T(128)} %bitcast.6.core_ref, f32[80,128]{1,0:T(8,128)S(1)} %add.32.vec_ref, bf16[768,128]{1,0:T(8,128)(2,1)S(1)} %copy-done.18, bf16[768,128]{1,0:T(8,128)(2,1)S(1)} %copy-done.22, bf16[768,128]{1,0:T(8,128)(2,1)S(1)} %copy-done.20, bf16[3072,128]{1,0:T(8,128)(2,1)S(1)} %copy-done.9, ...), custom_call_target="tpu_custom_call" | custom-call | tf_op jit(solution)/shard_map/pallas_call | solution.py:582
  173.1 3.1 %copy-done = bf16[4,16,448,128]{3,2,1,0:T(8,128)(2,1)S(1)} copy-done((bf16[4,16,448,128]{3,2,1,0:T(8,128)(2,1)S(1)}, bf16[4,16,448,128]{3,2,1,0:T(8,128)(2,1)}, u32[]{:S(2)}) %copy-start) | copy-done | bytes 7340056
  176.2 42.9 %shard_map.66 = f32[448,128]{1,0:T(8,128)S(1)} custom-call(bf16[4,4,4,448,128]{4,3,2,1,0:T(8,128)(2,1)S(1)} %bitcast.10), custom_call_target="tpu_custom_call" | custom-call | tf_op jit(solution)/shard_map/pallas_call | solution.py:733
  (62 shorter events, 11.4 us)
Async XLA Ops:
  2.3 54.6 %copy-start.12 = (bf16[1,128,768]{2,1,0:T(8,128)(2,1)S(1)}, bf16[1,128,768]{2,1,0:T(8,128)(2,1)}, u32[]{:S(2)}) copy-start(bf16[1,128,768]{2,1,0:T(8,128)(2,1)} %param.3) | copy-start | bytes 589828
  56.9 7.0 %copy-start.5 = (f32[3,128,128]{2,1,0:T(8,128)}, f32[3,128,128]{2,1,0:T(8,128)S(1)}, u32[]{:S(2)}) copy-start(f32[3,128,128]{2,1,0:T(8,128)S(1)} %pad_maximum_fusion.tables_ref) | copy-start | bytes 589828
  64.0 1.0 copy-start.7
  67.9 70.3 %copy-start.3 = (bf16[768,2304]{1,0:T(8,128)(2,1)S(1)}, bf16[768,2304]{1,0:T(8,128)(2,1)}, u32[]{:S(2)}) copy-start(bf16[768,2304]{1,0:T(8,128)(2,1)} %get-tuple-element.21.w_qkv) | copy-start | bytes 10616836
  83.6 70.6 %collective-permute-start.4 = (bf16[3072,128]{1,0:T(8,128)(2,1)}, bf16[3072,128]{1,0:T(8,128)(2,1)}, u32[]{:S(2)}, u32[]{:S(2)}) collective-permute-start(bf16[3072,128]{1,0:T(8,128)(2,1)} %get-tuple-element.34.refs_3_), channel_id=1, source_target_pairs={{0,16},{16,0},{1,17},{17,1},{2,18},{18,2},{3,19},{19,3},{4,20},{20... | collective-permute-start | bytes 2359304 | tf_op jit(solution)/shard_map/ppermute | solution.py:744
  83.9 70.3 %collective-permute-start.7 = (bf16[128,3072]{1,0:T(8,128)(2,1)}, bf16[128,3072]{1,0:T(8,128)(2,1)}, u32[]{:S(2)}, u32[]{:S(2)}) collective-permute-start(bf16[128,3072]{1,0:T(8,128)(2,1)} %get-tuple-element.36.refs_6_), channel_id=1, source_target_pairs={{0,16},{16,0},{1,17},{17,1},{2,18},{18,2},{3,19},{19,3},{4,20},{20... | collective-permute-start | bytes 2359304 | tf_op jit(solution)/shard_map/ppermute | solution.py:744
  103.0 1.2 copy-start.1
  118.2 1.0 copy-start.2
  138.2 1.1 copy-start.4
  139.4 0.9 copy-start.6
  140.3 1.3 copy-start.8
  141.6 0.9 copy-start.13
  142.5 1.0 copy-start.14
  143.5 1.0 copy-start.15
  149.2 3.4 %copy-start.23 = (f32[80,128]{1,0:T(8,128)}, f32[80,128]{1,0:T(8,128)S(1)}, u32[]{:S(2)}) copy-start(f32[80,128]{1,0:T(8,128)S(1)} %get-tuple-element.30) | copy-start | bytes 122884
  149.2 5.0 %collective-permute-start.5 = (bf16[128,2304]{1,0:T(8,128)(2,1)}, bf16[128,2304]{1,0:T(8,128)(2,1)S(1)}, u32[]{:S(2)}, u32[]{:S(2)}) collective-permute-start(bf16[128,2304]{1,0:T(8,128)(2,1)} %get-tuple-element.35.refs_4_), channel_id=1, source_target_pairs={{0,16},{16,0},{1,17},{17,1},{2,18},{18,2},{3,19},{19,3},{4,20},{20... | collective-permute-start | bytes 1769480 | tf_op jit(solution)/shard_map/ppermute | solution.py:744
  149.2 1.7 collective-permute-start
  149.7 1.8 collective-permute-start.2
  150.9 1.7 collective-permute-start.1
  151.5 2.2 collective-permute-start.3
  152.5 1.7 collective-permute-start.6
  154.2 1.1 copy-start.9
  155.3 1.1 copy-start.10
  173.1 3.1 %copy-start = (bf16[4,16,448,128]{3,2,1,0:T(8,128)(2,1)S(1)}, bf16[4,16,448,128]{3,2,1,0:T(8,128)(2,1)}, u32[]{:S(2)}) copy-start(bf16[4,16,448,128]{3,2,1,0:T(8,128)(2,1)} %shard_map.65) | copy-start | bytes 22020100
  (9 other events, 7.1 us)
where the time goes:
time: 221 us; the launch traced here: 220 us
  Pallas kernels  189 us (86%)
  local copies, waits for them, and re-layouts  24.2 us (11%)
    pallas_call x1, Pallas kernels, gather(): pl.pallas_call(gather_kernel, out_shape=jax.ShapeDtypeStruct((4, 2, 4, 4,...  54.2 us
    pallas_call x1, Pallas kernels, scatter(): pl.pallas_call(scatter_kernel, out_shape=jax.ShapeDtypeStruct((ROWS, 128)...  42.9 us
    pallas_call x2, Pallas kernels, exchange(): pl.pallas_call(functools.partial(exchange_kernel, to_heads), out_shape=ja...  37.8 us
    unnamed x50, local copies, waits for them, and re-layouts  21.9 us
    pallas_call x1, Pallas kernels, second_part(): pl.pallas_call(second_kernel, grid=(6,), out_shape=outs, in_specs=[pl.Blo...  15.7 us
    pallas_call x1, Pallas kernels, heads(): pl.pallas_call(head_kernel, out_shape=jax.ShapeDtypeStruct((16, 2, 128, 1...  14 us
    pallas_call x1, Pallas kernels, weight_grads(): pl.pallas_call(weight_kernel, grid=(4,), out_shape=jax.ShapeDtypeStruct((...  13.9 us
    pallas_call x1, Pallas kernels, first_part(): pl.pallas_call(first_kernel, grid=(3,), out_shape=outs, in_specs=[pl.Bloc...  6.99 us
  transfers between devices with their start and end apart: 8, of which 4 were waited for; matrix products, arithmetic and copies ran while one was open for 0% of the time, Pallas kernels for 25%

commit v1 on v0

--- a/solution.py
+++ b/solution.py
@@ -11,6 +11,7 @@
 DP_SEQ = ("dp_0", "dp_1", "seq_0", "seq_1")
 SEQ = ("seq_0", "seq_1")
 DP = ("dp_0", "dp_1")
+VMEM_LIMIT = 60 * 2**20
 MESH = pl.DeviceIdType.MESH
 ROWS = 448
 PARTS = ((0, 144, (0, 2, 1)), (144, 144, (2, 1, 0)), (288, 160, (1, 0, 2)))
@@ -141,63 +142,66 @@
 KEYS = 1024
 
 
-def exchange_kernel(to_heads, in_ref, out_ref, send, recv, local):
-    x, core = lax.axis_index("dp_0"), lax.axis_index("dp_1")
-    me = lax.axis_index("seq_0") * 4 + lax.axis_index("seq_1")
-    barrier = pltpu.get_barrier_semaphore()
-    others = [lax.rem(me + k, 16) for k in range(1, 16)]
-    where = lambda t: (x, core, lax.div(t, 4), lax.rem(t, 4))
-    for t in others:
-        pl.semaphore_signal(barrier, inc=1, device_id=where(t), device_id_type=MESH)
-    pl.semaphore_wait(barrier, 15)
-
-    def copy(t):
-        return pltpu.make_async_remote_copy(in_ref.at[t], out_ref.at[me], send.at[t], recv.at[me],
-                                            device_id=where(t), device_id_type=MESH)
-
-    def arrival(t):
-        return pltpu.make_async_remote_copy(out_ref.at[t], out_ref.at[t], send.at[t], recv.at[t],
-                                            device_id=where(t), device_id_type=MESH)
-
-    own = pltpu.make_async_copy(in_ref.at[me], out_ref.at[me], local)
-    if to_heads:
-        for t in others:
-            pl.when(t < HEADS)(lambda t=t: copy(t).start())
-
-        @pl.when(me < HEADS)
-        def _():
-            own.start()
-            for t in others:
-                arrival(t).wait_recv()
-            own.wait()
-        for t in others:
-            pl.when(t < HEADS)(lambda t=t: copy(t).wait_send())
-    else:
-        @pl.when(me < HEADS)
-        def _():
-            for t in others:
-                copy(t).start()
-            own.start()
-        for t in others:
-            pl.when(t < HEADS)(lambda t=t: arrival(t).wait_recv())
-
-        @pl.when(me < HEADS)
-        def _():
-            for t in others:
-                copy(t).wait_send()
-            own.wait()
-
-
-def exchange(blocks, to_heads):
-    count = 16 if to_heads else HEADS
-    return pl.pallas_call(
-        functools.partial(exchange_kernel, to_heads),
-        out_shape=jax.ShapeDtypeStruct((count,) + blocks.shape[1:], blocks.dtype),
-        in_specs=[pl.BlockSpec(memory_space=pl.ANY)],
-        out_specs=pl.BlockSpec(memory_space=pl.ANY),
-        scratch_shapes=[pltpu.SemaphoreType.DMA((16,)), pltpu.SemaphoreType.DMA((16,)), pltpu.SemaphoreType.DMA],
-        compiler_params=pltpu.CompilerParams(collective_id=2 if to_heads else 3, has_side_effects=True),
-    )(blocks)
+class Exchange:
+    scratch = [pltpu.SemaphoreType.DMA((16,)), pltpu.SemaphoreType.DMA((16,)), pltpu.SemaphoreType.DMA]
+
+    def __init__(self, to_heads, in_ref, out_ref, send, recv, local):
+        self.to_heads, self.in_ref, self.out_ref = to_heads, in_ref, out_ref
+        self.send, self.recv, self.local = send, recv, local
+        self.x, self.core = lax.axis_index("dp_0"), lax.axis_index("dp_1")
+        self.me = lax.axis_index("seq_0") * 4 + lax.axis_index("seq_1")
+        self.others = [lax.rem(self.me + k, 16) for k in range(1, 16)]
+
+    def where(self, t):
+        return (self.x, self.core, lax.div(t, 4), lax.rem(t, 4))
+
+    def copy(self, t):
+        return pltpu.make_async_remote_copy(
+            self.in_ref.at[t], self.out_ref.at[self.me], self.send.at[t], self.recv.at[self.me],
+            device_id=self.where(t), device_id_type=MESH)
+
+    def arrival(self, t):
+        return pltpu.make_async_remote_copy(
+            self.out_ref.at[t], self.out_ref.at[t], self.send.at[t], self.recv.at[t],
+            device_id=self.where(t), device_id_type=MESH)
+
+    def own(self):
+        return pltpu.make_async_copy(self.in_ref.at[self.me], self.out_ref.at[self.me], self.local)
+
+    def start(self):
+        barrier = pltpu.get_barrier_semaphore()
+        for t in self.others:
+            pl.semaphore_signal(barrier, inc=1, device_id=self.where(t), device_id_type=MESH)
+        pl.semaphore_wait(barrier, 15)
+        if self.to_heads:
+            for t in self.others:
+                pl.when(t < HEADS)(lambda t=t: self.copy(t).start())
+            pl.when(self.me < HEADS)(lambda: self.own().start())
+        else:
+            @pl.when(self.me < HEADS)
+            def _():
+                for t in self.others:
+                    self.copy(t).start()
+                self.own().start()
+
+    def wait(self):
+        if self.to_heads:
+            @pl.when(self.me < HEADS)
+            def _():
+                for t in self.others:
+                    self.arrival(t).wait_recv()
+                self.own().wait()
+            for t in self.others:
+                pl.when(t < HEADS)(lambda t=t: self.copy(t).wait_send())
+        else:
+            for t in self.others:
+                pl.when(t < HEADS)(lambda t=t: self.arrival(t).wait_recv())
+
+            @pl.when(self.me < HEADS)
+            def _():
+                for t in self.others:
+                    self.copy(t).wait_send()
+                self.own().wait()
 
 
 NT = (((1,), (1,)), ((), ()))
@@ -284,13 +288,14 @@
     return pl.pallas_call(
         head_kernel,
         out_shape=jax.ShapeDtypeStruct((16, 2, 128, 128), jnp.bfloat16),
-        in_specs=[pl.BlockSpec(memory_space=pltpu.VMEM)],
-        out_specs=pl.BlockSpec(memory_space=pltpu.VMEM),
+        grid=(1,),
+        in_specs=[pl.BlockSpec((16, 2, 128, 128), lambda e: (0, 0, 0, 0))],
+        out_specs=pl.BlockSpec((16, 2, 128, 128), lambda e: (0, 0, 0, 0)),
         scratch_shapes=[pltpu.VMEM((2048, 64), jnp.bfloat16), pltpu.VMEM((2048, 64), jnp.bfloat16),
                         pltpu.VMEM((64, 2048), jnp.bfloat16), pltpu.VMEM((64, 2048), jnp.bfloat16),
                         pltpu.VMEM((2048, TILE), jnp.float32),
                         pltpu.VMEM((2048, 64), jnp.float32), pltpu.VMEM((2048, 64), jnp.float32)],
-        compiler_params=pltpu.CompilerParams(vmem_limit_bytes=32 * 2**20),
+        compiler_params=pltpu.CompilerParams(vmem_limit_bytes=VMEM_LIMIT),
     )(blocks)
 
 
@@ -387,7 +392,7 @@
         in_specs=[pl.BlockSpec((16, 448, 128), lambda e: (e, 0, 0)), const(128, 768), const(128, 768), const(3, 128, 128)],
         out_specs=[const(*o.shape) for o in outs],
         scratch_shapes=[pltpu.VMEM((3 * EIGHTH + 16, 128), jnp.float32), pltpu.VMEM((128, 2304), jnp.float32)],
-        compiler_params=pltpu.CompilerParams(vmem_limit_bytes=48 * 2**20),
+        compiler_params=pltpu.CompilerParams(vmem_limit_bytes=VMEM_LIMIT),
     )(gathered, tokens, grad, tables)
 
 
@@ -396,8 +401,11 @@
     return u * inside, inside + u * jnp.exp(-0.5 * u * u) * 0.3989422804014327
 
 
-def second_kernel(g_ref, h2_ref, grad_ref, mlp_ref, dh2_ref, act_t_ref, dup_ref, bias_ref, flat, w_up, w_down, act, slope):
+def second_kernel(g_ref, h2_ref, grad_ref, blocks_ref, mlp_ref, dh2_ref, act_t_ref, dup_ref, bias_ref, heads_ref,
+                  flat, w_up, w_down, act, slope, *sems):
     step = pl.program_id(0)
+    swap = Exchange(True, blocks_ref, heads_ref, *sems)
+    pl.when(step == 0)(swap.start)
     widen(g_ref, flat, step)
 
     @pl.when(step == 3)
@@ -427,23 +435,25 @@
         for n in range(3):
             at = slice(256 * n, 256 * (n + 1))
             dh2_ref[:, at] = product(dup_ref[...], w_up[at, :], NT)
-
-
-def second_part(gathered, h2, grad):
+        swap.wait()
+
+
+def second_part(gathered, h2, grad, blocks):
     bf = lambda *s: jax.ShapeDtypeStruct(s, jnp.bfloat16)
     f32 = lambda *s: jax.ShapeDtypeStruct(s, jnp.float32)
     outs = [f32(128, 768), f32(128, 768), bf(3072, 128), bf(128, 3072), f32(24, 128)]
+    anywhere = pl.BlockSpec(memory_space=pl.ANY)
     return pl.pallas_call(
         second_kernel,
         grid=(6,),
-        out_shape=outs,
-        in_specs=[pl.BlockSpec((16, 448, 128), lambda e: (e + 2, 0, 0)), const(128, 768), const(128, 768)],
-        out_specs=[const(*o.shape) for o in outs],
+        out_shape=outs + [bf(16, 2, 128, 128)],
+        in_specs=[pl.BlockSpec((16, 448, 128), lambda e: (e + 2, 0, 0)), const(128, 768), const(128, 768), anywhere],
+        out_specs=[const(*o.shape) for o in outs] + [anywhere],
         scratch_shapes=[pltpu.VMEM((6 * EIGHTH + 16, 128), jnp.float32), pltpu.VMEM((768, 3072), jnp.bfloat16),
                         pltpu.VMEM((3072, 768), jnp.bfloat16), pltpu.VMEM((128, 3072), jnp.bfloat16),
-                        pltpu.VMEM((128, 3072), jnp.float32)],
-        compiler_params=pltpu.CompilerParams(vmem_limit_bytes=56 * 2**20),
-    )(gathered, h2, grad)
+                        pltpu.VMEM((128, 3072), jnp.float32)] + Exchange.scratch,
+        compiler_params=pltpu.CompilerParams(collective_id=2, has_side_effects=True, vmem_limit_bytes=VMEM_LIMIT),
+    )(gathered, h2, grad, blocks)
 
 
 def third_kernel(back_ref, tokens_ref, grad_ref, tables_ref, w_qkv, w_out, mlp_ref, dh2_ref, bias_ref, in_vec,
@@ -489,13 +499,13 @@
     bf = lambda *s: jax.ShapeDtypeStruct(s, jnp.bfloat16)
     f32 = lambda *s: jax.ShapeDtypeStruct(s, jnp.float32)
     outs = [bf(128, 768), f32(128, 768), bf(768, 128), bf(128, 2304), f32(80, 128)]
-    whole = pl.BlockSpec(memory_space=pltpu.VMEM)
     return pl.pallas_call(
         third_kernel,
+        grid=(1,),
         out_shape=outs,
-        in_specs=[whole] * len(args),
-        out_specs=[whole] * len(outs),
-        compiler_params=pltpu.CompilerParams(vmem_limit_bytes=32 * 2**20),
+        in_specs=[const(*a.shape) for a in args],
+        out_specs=[const(*o.shape) for o in outs],
+        compiler_params=pltpu.CompilerParams(vmem_limit_bytes=VMEM_LIMIT),
     )(*args)
 
 
@@ -512,82 +522,132 @@
 CHUNK = 128
 
 
-def weight_kernel(core_ref, vec_ref, *refs):
-    mine, theirs, (out_ref, flat), pair = refs[:7], refs[7:14], refs[14:16], refs[16:]
-    step = pl.program_id(0)
-    core = core_ref[0]
-
-    @pl.when(step == 0)
-    def _():
-        for n in range(7):
-            if n < 4:
-                pair[n][:, :128] = mine[n][...]
-                pair[n][:, 128:] = theirs[n][...]
-            else:
-                pair[n][:128, :] = mine[n][...]
-                pair[n][128:, :] = theirs[n][...]
-
-    h1_ref, att_ref, h2_ref, act_ref, dqkv_ref, g_ref, dup_ref = pair
-    pairs = ((W_QKV, h1_ref, dqkv_ref), (W_OUT, att_ref, g_ref), (W_UP, h2_ref, dup_ref), (W_DOWN, act_ref, g_ref))
-
-    def eighth(number):
-        low, high = number * EIGHTH, (number + 1) * EIGHTH
-        at = MARGIN - low
-        for (offset, rows, blocks), left, right in pairs:
-            first = max(0, (low - offset) // blocks) // 16 * 16
-            last = min(rows, -(-(high - offset) // blocks))
-            last = -(-last // 16) * 16
-            if last <= first:
-                continue
-            size = min(CHUNK, last - first)
-            count = -(-(last - first) // size)
-            base = offset + at
-
-            @pl.loop(0, count)
-            def _(i, first=first, last=last, size=size, blocks=blocks, base=base, left=left, right=right):
-                row = pl.multiple_of(jnp.minimum(first + i * size, last - size), 16)
-                lhs = left[pl.ds(row, size), :]
-
-                @pl.loop(0, blocks // 2, unroll=3)
-                def _(j):
-                    rhs = right[:, pl.ds(pl.multiple_of(j * 256, 256), 256)]
-                    product = jnp.dot(lhs, rhs, preferred_element_type=jnp.float32)
-                    start = base + row * blocks + 2 * j
-                    flat[pl.ds(start, size, stride=blocks), :] = product[:, :128]
-                    flat[pl.ds(start + 1, size, stride=blocks), :] = product[:, 128:]
-
-        row = 0
-        for name in ORDER:
-            start, count = VECTORS[name]
-            lo, hi = max(start, low), min(start + count, high)
-            if lo < hi:
-                flat[lo + at:hi + at, :] = vec_ref[row + lo - start:row + hi - start, :]
-            row += count
-        end = 55374
-        if high > end:
-            flat[end + at:high + at, :] = jnp.zeros((high - end, 128), jnp.float32)
-
-    for t in range(4):
-        for c in range(2):
-            pl.when((step == t) & (core == c))(lambda number=2 * t + c: eighth(number))
-
+def weight_eighth(number, pairs, vec_ref, flat):
+    low, high = number * EIGHTH, (number + 1) * EIGHTH
+    at = MARGIN - low
+    for (offset, rows, blocks), left, right in pairs:
+        first = max(0, (low - offset) // blocks) // 16 * 16
+        last = min(rows, -(-(high - offset) // blocks))
+        last = -(-last // 16) * 16
+        if last <= first:
+            continue
+        size = min(CHUNK, last - first)
+        count = -(-(last - first) // size)
+        base = offset + at
+
+        @pl.loop(0, count)
+        def _(i, first=first, last=last, size=size, blocks=blocks, base=base, left=left, right=right):
+            row = pl.multiple_of(jnp.minimum(first + i * size, last - size), 16)
+            lhs = left[pl.ds(row, size), :]
+
+            @pl.loop(0, blocks // 2, unroll=3)
+            def _(j):
+                rhs = right[:, pl.ds(pl.multiple_of(j * 256, 256), 256)]
+                result = product(lhs, rhs)
+                start = base + row * blocks + 2 * j
+                flat[pl.ds(start, size, stride=blocks), :] = result[:, :128]
+                flat[pl.ds(start + 1, size, stride=blocks), :] = result[:, 128:]
+
+    row = 0
+    for name in ORDER:
+        start, count = VECTORS[name]
+        lo, hi = max(start, low), min(start + count, high)
+        if lo < hi:
+            flat[lo + at:hi + at, :] = vec_ref[row + lo - start:row + hi - start, :]
+        row += count
+    end = 55374
+    if high > end:
+        flat[end + at:high + at, :] = jnp.zeros((high - end, 128), jnp.float32)
+
+
+def join(pair, mine, theirs, lanes):
+    if lanes:
+        pair[:, :128] = mine[...]
+        pair[:, 128:] = theirs[...]
+    else:
+        pair[:128, :] = mine[...]
+        pair[128:, :] = theirs[...]
+
+
+def pack(flat, out_ref):
     @pl.loop(0, 16)
     def _(k):
         out_ref[0, k] = flat[pl.ds(MARGIN + 433 * k, 448), :].astype(jnp.bfloat16)
 
 
-def weight_grads(core, vec, mine, theirs):
-    whole = pl.BlockSpec(memory_space=pltpu.VMEM)
-    pairs = [(r, 256) for r in (768, 768, 768, 3072)] + [(256, c) for c in (2304, 768, 3072)]
+def eighths(steps, step, core, pairs, vec_ref, flat):
+    for n, t in enumerate(steps):
+        for c in range(2):
+            pl.when((step == n) & (core == c))(lambda number=2 * t + c: weight_eighth(number, pairs, vec_ref, flat))
+
+
+HALVES = jax.ShapeDtypeStruct((4, 16, 448, 128), jnp.bfloat16)
+
+
+def late_kernel(vec_ref, act_ref, act2_ref, g_ref, g2_ref, dup_ref, dup2_ref, h2_ref, h22_ref, heads_ref,
+                out_ref, back_ref, flat, act, g, dup, h2, *sems):
+    step = pl.program_id(0)
+    swap = Exchange(False, heads_ref, back_ref, *sems)
+
+    @pl.when(step == 0)
+    def _():
+        swap.start()
+        join(act, act_ref, act2_ref, True)
+        join(h2, h2_ref, h22_ref, True)
+        join(g, g_ref, g2_ref, False)
+        join(dup, dup_ref, dup2_ref, False)
+
+    eighths((2, 3), step, lax.axis_index("dp_1"), ((W_UP, h2, dup), (W_DOWN, act, g)), vec_ref, flat)
+    pack(flat, out_ref)
+    pl.when(step == 1)(swap.wait)
+
+
+def late_grads(vec, act, act2, g, g2, dup, dup2, h2, h22, heads_out):
+    args = (vec, act, act2, g, g2, dup, dup2, h2, h22)
+    anywhere = pl.BlockSpec(memory_space=pl.ANY)
+    pairs = [(3072, 256), (256, 768), (256, 3072), (768, 256)]
     return pl.pallas_call(
-        weight_kernel,
-        grid=(4,),
-        out_shape=jax.ShapeDtypeStruct((4, 16, 448, 128), jnp.bfloat16),
-        in_specs=[pl.BlockSpec(memory_space=pltpu.SMEM)] + [whole] * 15,
+        late_kernel,
+        grid=(2,),
+        out_shape=[HALVES, jax.ShapeDtypeStruct((HEADS, 2, 128, 128), jnp.bfloat16)],
+        in_specs=[const(*a.shape) for a in args] + [anywhere],
+        out_specs=[pl.BlockSpec((1, 16, 448, 128), lambda e: (e + 2, 0, 0, 0)), anywhere],
+        scratch_shapes=[pltpu.VMEM((EIGHTH + 2 * MARGIN, 128), jnp.float32)]
+        + [pltpu.VMEM(p, jnp.bfloat16) for p in pairs] + Exchange.scratch,
+        compiler_params=pltpu.CompilerParams(collective_id=3, has_side_effects=True, vmem_limit_bytes=VMEM_LIMIT),
+    )(*args, heads_out)
+
+
+def early_kernel(core_ref, vec_ref, h1_ref, h12_ref, att_ref, att2_ref, h2_ref, h22_ref, dqkv_ref, dqkv2_ref,
+                 g_ref, g2_ref, dup_ref, dup2_ref, halves_ref, out_ref, flat, h1, att, h2, dqkv, g, dup):
+    step = pl.program_id(0)
+
+    @pl.when(step == 0)
+    def _():
+        join(h1, h1_ref, h12_ref, True)
+        join(att, att_ref, att2_ref, True)
+        join(h2, h2_ref, h22_ref, True)
+        join(dqkv, dqkv_ref, dqkv2_ref, False)
+        join(g, g_ref, g2_ref, False)
+        join(dup, dup_ref, dup2_ref, False)
+
+    eighths((0, 1), step, core_ref[0], ((W_QKV, h1, dqkv), (W_OUT, att, g), (W_UP, h2, dup)), vec_ref, flat)
+    pack(flat, out_ref)
+
+
+def early_grads(core, vec, h1, h12, att, att2, h2, h22, dqkv, dqkv2, g, g2, dup, dup2, halves):
+    args = (vec, h1, h12, att, att2, h2, h22, dqkv, dqkv2, g, g2, dup, dup2)
+    pairs = [(768, 256)] * 3 + [(256, 2304), (256, 768), (256, 3072)]
+    return pl.pallas_call(
+        early_kernel,
+        grid=(2,),
+        out_shape=HALVES,
+        in_specs=[pl.BlockSpec(memory_space=pltpu.SMEM)] + [const(*a.shape) for a in args] + [pl.BlockSpec(memory_space=pl.ANY)],
         out_specs=pl.BlockSpec((1, 16, 448, 128), lambda e: (e, 0, 0, 0)),
         scratch_shapes=[pltpu.VMEM((EIGHTH + 2 * MARGIN, 128), jnp.float32)] + [pltpu.VMEM(p, jnp.bfloat16) for p in pairs],
-        compiler_params=pltpu.CompilerParams(vmem_limit_bytes=48 * 2**20),
-    )(core, vec, *mine, *theirs)
+        input_output_aliases={14: 0},
+        compiler_params=pltpu.CompilerParams(vmem_limit_bytes=VMEM_LIMIT),
+    )(core, *args, halves)
 
 
 def halves(size):
@@ -733,10 +793,11 @@
     return pl.pallas_call(
         scatter_kernel,
         out_shape=jax.ShapeDtypeStruct((ROWS, 128), jnp.float32),
-        in_specs=[pl.BlockSpec(memory_space=pltpu.VMEM)],
-        out_specs=pl.BlockSpec(memory_space=pltpu.VMEM),
+        grid=(1,),
+        in_specs=[pl.BlockSpec((4, 4, 4, ROWS, 128), lambda e: (0, 0, 0, 0, 0))],
+        out_specs=pl.BlockSpec((ROWS, 128), lambda e: (0, 0)),
         scratch_shapes=scratch,
-        compiler_params=pltpu.CompilerParams(collective_id=1, has_side_effects=True, vmem_limit_bytes=40 * 2**20),
+        compiler_params=pltpu.CompilerParams(collective_id=1, has_side_effects=True, vmem_limit_bytes=VMEM_LIMIT),
     )(parts)
 
 
@@ -751,15 +812,20 @@
     gathered = gather(own).reshape(128, ROWS, 128)
     tables = rotary_tables(lax.axis_index(SEQ) * piece + jnp.arange(piece))
     w_qkv, w_out, blocks, h1t, h2, h2t, in_vec = first_part(gathered, x, grad, tables)
-    back = exchange(heads(exchange(blocks, True)), False)
-    mlp, dh2, act_t, dup, bias = second_part(gathered, h2, grad)
+    mlp, dh2, act_t, dup, bias, at_heads = second_part(gathered, h2, grad, blocks)
+    shift = jnp.sum(grad.astype(jnp.float32), 0).reshape(6, 128)
+    late_vec = jnp.concatenate([jnp.zeros((48, 128), jnp.float32), bias, shift, jnp.zeros((2, 128), jnp.float32)])
+    late_vec = late_vec + twin(late_vec)
+    act2, g2, dup2, h22, h12 = (twin(a) for a in (act_t, grad, dup, h2t, h1t))
+    halves_sum, back = late_grads(late_vec, act_t, act2, grad, g2, dup, dup2, h2t, h22, heads(at_heads))
     layer_out, input_grad, att_t, dqkv, vec = third_part(
         back, x, grad, tables, w_qkv, w_out, mlp, dh2, bias, in_vec
     )
     vec = vec + twin(vec)
     core = lax.axis_index("dp_1").astype(jnp.int32).reshape(1)
-    mine = (h1t, att_t, h2t, act_t, dqkv, grad, dup)
-    halves_sum = weight_grads(core, vec, mine, tuple(twin(a) for a in mine))
+    halves_sum = early_grads(
+        core, vec, h1t, h12, att_t, twin(att_t), h2t, h22, dqkv, twin(dqkv), grad, g2, dup, dup2, halves_sum
+    )
     param_grad = scatter(halves_sum.reshape(4, 4, 4, ROWS, 128))[:433].reshape(-1)
     return layer_out[None], input_grad[None], param_grad
 

time: 221 us -> 202 us (0.914)
  local copies, waits for them, and re-layouts: 24.2 us -> 6.22 us
  other arithmetic: 1.14 us -> 4.67 us
  Pallas kernels: 189 us -> 186 us
    unnamed x50 -> x20, local copies, waits for them, and re-layouts: 21.9 us -> 2.85 us
    pallas_call x5 -> x4, Pallas kernels: 71.3 us -> 60.7 us  [the longest x1 23.8 us: late_grads(): pl.pallas_call(late_kernel, grid=(2,), out_shape=[HALVES, jax.ShapeDtypeS...]
    pallas_call x1, Pallas kernels: 42.9 us -> 46.7 us  [scatter(): pl.pallas_call(scatter_kernel, out_shape=jax.ShapeDtypeStruct((ROWS, 128)...]
    pallas_call x1, Pallas kernels: 14 us -> 16.3 us  [heads(): pl.pallas_call(head_kernel, out_shape=jax.ShapeDtypeStruct((16, 2, 128, 1...]
  transfers between devices with their start and end apart: 8 -> 9, of which waited for: 4 -> 1; matrix products, arithmetic and copies ran while one was open for 0% -> 2% of each run, Pallas kernels for 25% -> 8%
where the time goes in v1:
time: 202 us
  Pallas kernels  186 us (92%)
  local copies, waits for them, and re-layouts  6.22 us (3%)
  other arithmetic  4.67 us (2%)
  starting transfers between devices  2.28 us (1%)
    pallas_call x1, Pallas kernels, gather(): pl.pallas_call(gather_kernel, out_shape=jax.ShapeDtypeStruct((4, 2, 4, 4,...  54.2 us
    pallas_call x1, Pallas kernels, scatter(): pl.pallas_call(scatter_kernel, out_shape=jax.ShapeDtypeStruct((ROWS, 128)...  46.7 us
    pallas_call x1, Pallas kernels, late_grads(): pl.pallas_call(late_kernel, grid=(2,), out_shape=[HALVES, jax.ShapeDtypeS...  23.8 us
    pallas_call x1, Pallas kernels, second_part(): pl.pallas_call(second_kernel, grid=(6,), out_shape=outs + [bf(16, 2, 128,...  22.3 us
    pallas_call x1, Pallas kernels, heads(): pl.pallas_call(head_kernel, out_shape=jax.ShapeDtypeStruct((16, 2, 128, 1...  16.3 us
    pallas_call x1, Pallas kernels, early_grads(): pl.pallas_call(early_kernel, grid=(2,), out_shape=HALVES, in_specs=[pl.Bl...  8.72 us
    pallas_call x1, Pallas kernels, first_part(): pl.pallas_call(first_kernel, grid=(3,), out_shape=outs, in_specs=[pl.Bloc...  7.88 us
    pallas_call x1, Pallas kernels, third_part(): pl.pallas_call(third_kernel, grid=(1,), out_shape=outs, in_specs=[const(*...  5.93 us
  transfers between devices with their start and end apart: 9, of which 1 were waited for; matrix products, arithmetic and copies ran while one was open for 2% of the time, Pallas kernels for 8%

profile of v1, /device:TPU:0, one launch (start us, length us, event | category | flops | bytes accessed | tf_op | source)
XLA Modules:
  0.0 201.6 jit_solution(16938682311184693115)
XLA Ops:
  0.8 1.6 pad.4.own_ref
  2.3 54.2 %shard_map.58 = bf16[4,2,4,4,448,128]{5,4,3,2,1,0:T(8,128)(2,1)} custom-call(bf16[448,128]{1,0:T(8,128)(2,1)} %pad.4.own_ref), custom_call_target="tpu_custom_call" | custom-call | tf_op jit(solution)/shard_map/pallas_call | solution.py:120
  56.6 0.3 fusion.3
  56.9 0.7 pad_maximum_fusion.tables_ref
  57.6 7.9 %shard_map.59 = (bf16[768,2304]{1,0:T(8,128)(2,1)}, bf16[768,768]{1,0:T(8,128)(2,1)}, bf16[12,2,128,128]{3,2,1,0:T(8,128)(2,1)}, bf16[768,128]{1,0:T(8,128)(2,1)...) custom-call(bf16[128,448,128]{2,1,0:T(8,128)(2,1)} %bitcast.12, ...), custom_call_target="tpu_custom_call" | custom-call | tf_op jit(solution)/shard_map/pallas_call | solution.py:388
  65.5 22.3 %shard_map.60 = (f32[128,768]{1,0:T(8,128)}, f32[128,768]{1,0:T(8,128)}, bf16[3072,128]{1,0:T(8,128)(2,1)}, bf16[128,3072]{1,0:T(8,128)(2,1)}, f32[24,128]{1,0:T(8,128)}, /*index=5*/bf16[16,2,128,128]{3,2,1,0:T(8,128)(2,1)}) custom-call(bf16[128,448,128]{2,1,0:T(8,128)(2,1)} %bitcast.13, bf16[128,768]{1,0:T(8,128)(2,1)} %get-tuple-element.23.h2_ref, ...), custom_call_target="tpu_custom_call" | custom-call | tf_op jit(solution)/shard_map/pallas_call | solution.py:446
  88.0 0.5 collective-permute-start.1
  88.5 0.8 maximum_maximum_fusion
  89.5 0.4 collective-permute-start.2
  90.0 16.3 %shard_map.61.heads_ref = bf16[16,2,128,128]{3,2,1,0:T(8,128)(2,1)} custom-call(bf16[16,2,128,128]{3,2,1,0:T(8,128)(2,1)} %get-tuple-element.29.in_ref), custom_call_target="tpu_custom_call" | custom-call | tf_op jit(solution)/shard_map/pallas_call | solution.py:288
  106.3 1.4 fusion.4.vec_ref
  107.8 0.6 copy-done.4
  108.7 0.9 copy-done.5
  109.6 23.8 %shard_map.62 = (bf16[4,16,448,128]{3,2,1,0:T(8,128)(2,1)}, bf16[12,2,128,128]{3,2,1,0:T(8,128)(2,1)}) custom-call(f32[80,128]{1,0:T(8,128)} %fusion.4.vec_ref, bf16[3072,128]{1,0:T(8,128)(2,1)} %get-tuple-element.26.act_ref, bf16[3072,128]{1,0:T(8,128)(2,1)} %copy-done.5, bf16[128,768]{1,0:T(8,128)(2,1)} %bitcast.17, bf16[128,768]{1,0:T(8,128)(2,1)} %copy-done.3, ...), custom_call_target="tpu_custom_call" | custom-call | tf_op jit(solution)/shard_map/pallas_call | solution.py:609
  133.4 5.9 %shard_map.63 = (bf16[128,768]{1,0:T(8,128)(2,1)}, f32[128,768]{1,0:T(8,128)}, bf16[768,128]{1,0:T(8,128)(2,1)}, bf16[128,2304]{1,0:T(8,128)(2,1)}, f32[80,128]{1,0:T(8,128)}) custom-call(bf16[12,2,128,128]{3,2,1,0:T(8,128)(2,1)} %get-tuple-element.30.back_ref, bf16[128,768]{1,0:T(8,128)(2,1)} %bitcast.22, bf16[128,768]{1,0:T(8,128)(2,1)} %bitcast.18, ...), custom_call_target="tpu_custom_call" | custom-call | tf_op jit(solution)/shard_map/pallas_call | solution.py:502
  139.3 0.5 collective-permute-start.6
  139.9 0.4 collective-permute-start.5
  140.4 1.8 collective-permute-done.5
  142.2 1.4 add.36.vec_ref
  143.6 0.6 copy-done.8
  144.3 0.3 copy-done.6
  144.6 8.7 %shard_map.64 = bf16[4,16,448,128]{3,2,1,0:T(8,128)(2,1)} custom-call(s32[1]{0:T(128)} %bitcast.7.core_ref, f32[80,128]{1,0:T(8,128)} %add.36.vec_ref, bf16[768,128]{1,0:T(8,128)(2,1)} %get-tuple-element.39.h1_ref, bf16[768,128]{1,0:T(8,128)(2,1)} %copy-done.8, bf16[768,128]{1,0:T(8,128)(2,1)} %get-tuple-element.40.att_ref, ...), custom_call_target="tpu_custom_call", output_to_operand_aliasing={{}: (14, {})} | custom-call | tf_op jit(solution)/shard_map/pallas_call | solution.py:641
  153.3 46.7 %shard_map.65 = f32[448,128]{1,0:T(8,128)} custom-call(bf16[4,4,4,448,128]{4,3,2,1,0:T(8,128)(2,1)} %bitcast.14), custom_call_target="tpu_custom_call" | custom-call | tf_op jit(solution)/shard_map/pallas_call | solution.py:793
  200.0 1.6 slice_bitcast_fusion
  (40 shorter events, 1.2 us)
Async XLA Ops:
  65.5 23.0 %copy-start = (bf16[1,128,768]{2,1,0:T(8,128)(2,1)S(1)}, bf16[1,128,768]{2,1,0:T(8,128)(2,1)}, u32[]{:S(2)}) copy-start(bf16[1,128,768]{2,1,0:T(8,128)(2,1)} %param.5) | copy-start | bytes 589828
  65.5 24.4 %copy-start.2 = (bf16[768,128]{1,0:T(8,128)(2,1)S(1)}, bf16[768,128]{1,0:T(8,128)(2,1)}, u32[]{:S(2)}) copy-start(bf16[768,128]{1,0:T(8,128)(2,1)} %get-tuple-element.28.h2_ref) | copy-start | bytes 589828
  87.8 51.5 %copy-start.7 = (bf16[768,128]{1,0:T(8,128)(2,1)S(1)}, bf16[768,128]{1,0:T(8,128)(2,1)}, u32[]{:S(2)}) copy-start(bf16[768,128]{1,0:T(8,128)(2,1)} %get-tuple-element.39.h1_ref) | copy-start | bytes 589828
  87.8 19.9 %collective-permute-start.3 = (bf16[128,3072]{1,0:T(8,128)(2,1)}, bf16[128,3072]{1,0:T(8,128)(2,1)S(1)}, u32[]{:S(2)}, u32[]{:S(2)}) collective-permute-start(bf16[128,3072]{1,0:T(8,128)(2,1)} %get-tuple-element.27.dup_ref), channel_id=1, source_target_pairs={{0,16},{16,0},{1,17},{17,1},{2,18},{18,2},{3,19},{19,3},{4,20},{20... | collective-permute-start | bytes 2359304 | tf_op jit(solution)/shard_map/ppermute | solution.py:805
  88.0 19.8 %collective-permute-start.1 = (bf16[3072,128]{1,0:T(8,128)(2,1)}, bf16[3072,128]{1,0:T(8,128)(2,1)S(1)}, u32[]{:S(2)}, u32[]{:S(2)}) collective-permute-start(bf16[3072,128]{1,0:T(8,128)(2,1)} %get-tuple-element.26.act_ref), channel_id=1, source_target_pairs={{0,16},{16,0},{1,17},{17,1},{2,18},{18,2},{3,19},{19,3},{4,20},{20... | collective-permute-start | bytes 2359304 | tf_op jit(solution)/shard_map/ppermute | solution.py:805
  89.3 17.0 %collective-permute-start = (f32[80,128]{1,0:T(8,128)S(1)}, f32[80,128]{1,0:T(8,128)S(1)}, u32[]{:S(2)}, u32[]{:S(2)}) collective-permute-start(f32[80,128]{1,0:T(8,128)S(1)} %maximum_maximum_fusion), channel_id=1, source_target_pairs={{0,16},{16,0},{1,17},{17,1},{2,18},{18,2},{3,19},{19,3},{4,20},{20... | collective-permute-start | bytes 122888 | tf_op jit(solution)/shard_map/ppermute | solution.py:805
  89.5 18.2 %collective-permute-start.2 = (bf16[128,768]{1,0:T(8,128)(2,1)S(1)}, bf16[128,768]{1,0:T(8,128)(2,1)S(1)}, u32[]{:S(2)}, u32[]{:S(2)}) collective-permute-start(bf16[128,768]{1,0:T(8,128)(2,1)S(1)} %bitcast.20), channel_id=1, source_target_pairs={{0,16},{16,0},{1,17},{17,1},{2,18},{18,2},{3,19},{19,3},{4,20},{20... | collective-permute-start | bytes 589832 | tf_op jit(solution)/shard_map/ppermute | solution.py:805
  89.9 17.8 %collective-permute-start.4 = (bf16[768,128]{1,0:T(8,128)(2,1)S(1)}, bf16[768,128]{1,0:T(8,128)(2,1)S(1)}, u32[]{:S(2)}, u32[]{:S(2)}) collective-permute-start(bf16[768,128]{1,0:T(8,128)(2,1)S(1)} %copy-done.2), channel_id=1, source_target_pairs={{0,16},{16,0},{1,17},{17,1},{2,18},{18,2},{3,19},{19,3},{4,20},{20... | collective-permute-start | bytes 589832 | tf_op jit(solution)/shard_map/ppermute | solution.py:805
  107.7 0.7 copy-start.4
  107.7 0.8 copy-start.3
  107.8 1.0 copy-start.1
  108.7 0.9 copy-start.5
  139.3 4.2 %collective-permute-start.8 = (bf16[128,2304]{1,0:T(8,128)(2,1)}, bf16[128,2304]{1,0:T(8,128)(2,1)S(1)}, u32[]{:S(2)}, u32[]{:S(2)}) collective-permute-start(bf16[128,2304]{1,0:T(8,128)(2,1)} %get-tuple-element.41.dqkv_ref), channel_id=1, source_target_pairs={{0,16},{16,0},{1,17},{17,1},{2,18},{18,2},{3,19},{19,3},{4,20},{20... | collective-permute-start | bytes 1769480 | tf_op jit(solution)/shard_map/ppermute | solution.py:805
  139.3 4.2 %collective-permute-start.6 = (bf16[768,128]{1,0:T(8,128)(2,1)S(1)}, bf16[768,128]{1,0:T(8,128)(2,1)S(1)}, u32[]{:S(2)}, u32[]{:S(2)}) collective-permute-start(bf16[768,128]{1,0:T(8,128)(2,1)S(1)} %copy-done.7), channel_id=1, source_target_pairs={{0,16},{16,0},{1,17},{17,1},{2,18},{18,2},{3,19},{19,3},{4,20},{20... | collective-permute-start | bytes 589832 | tf_op jit(solution)/shard_map/ppermute | solution.py:805
  139.8 3.7 %collective-permute-start.7 = (bf16[768,128]{1,0:T(8,128)(2,1)}, bf16[768,128]{1,0:T(8,128)(2,1)S(1)}, u32[]{:S(2)}, u32[]{:S(2)}) collective-permute-start(bf16[768,128]{1,0:T(8,128)(2,1)} %get-tuple-element.40.att_ref), channel_id=1, source_target_pairs={{0,16},{16,0},{1,17},{17,1},{2,18},{18,2},{3,19},{19,3},{4,20},{20... | collective-permute-start | bytes 589832 | tf_op jit(solution)/shard_map/ppermute | solution.py:805
  139.9 2.2 %collective-permute-start.5 = (f32[80,128]{1,0:T(8,128)}, f32[80,128]{1,0:T(8,128)S(1)}, u32[]{:S(2)}, u32[]{:S(2)}) collective-permute-start(f32[80,128]{1,0:T(8,128)} %get-tuple-element.38), channel_id=1, source_target_pairs={{0,16},{16,0},{1,17},{17,1},{2,18},{18,2},{3,19},{19,3},{4,20},{20... | collective-permute-start | bytes 122888 | tf_op jit(solution)/shard_map/ppermute | solution.py:805
  143.6 0.7 copy-start.8
  143.6 0.7 copy-start.9
  143.6 1.0 copy-start.6

commit v2 on v1

--- a/solution.py
+++ b/solution.py
@@ -41,79 +41,156 @@
     pl.semaphore_wait(barrier, len(others))
 
 
-def gather_kernel(own_ref, out_ref, send, recv, sib_send, sib_recv, local):
-    pos, core = place()
-    greet(pos, core)
-
-    def region(part, where, c, start, size):
-        idx = [slice(None) if w is None else w for w in where]
-        return out_ref.at[idx[0], c, idx[1], idx[2], pl.ds(start, size), :]
-
-    own = pltpu.make_async_copy(own_ref, out_ref.at[pos[0], core, pos[1], pos[2]], local)
-    own.start()
-    own.wait()
-    sibs = []
-
-    def to_sibling(number, part, where):
+class Gather:
+    scratch = [pltpu.SemaphoreType.DMA((3, 9, 4)), pltpu.SemaphoreType.DMA((3, 9, 4)),
+               pltpu.SemaphoreType.DMA((3, 19)), pltpu.SemaphoreType.DMA((3, 19)), pltpu.SemaphoreType.DMA]
+    rings = ("a", "b0", "b1", "b2", "b3", "c0", "c1", "c2", "c3")
+
+    def __init__(self, own_ref, out_ref, send, recv, sib_send, sib_recv, local):
+        self.own_ref, self.out_ref, self.local = own_ref, out_ref, local
+        self.send_sem, self.recv_sem, self.sib_send, self.sib_recv = send, recv, sib_send, sib_recv
+        self.pos, self.core = place()
+        self.copies, self.sibs = {}, [[], [], []]
+
+    def near(self, axis):
+        q = self.pos[axis]
+        return [q] + [lax.rem(q + k, 4) for k in (3, 1, 2)]
+
+    def region(self, where, start, size):
+        return self.out_ref.at[where[0], self.core, where[1], where[2], pl.ds(start, size), :]
+
+    def base(self, part, ring):
+        a, b, c = PARTS[part][2]
+        where = list(self.pos)
+        if ring == "a":
+            return a, where
+        number = int(ring[1])
+        if ring[0] == "b":
+            where[a] = self.near(a)[number]
+            return b, where
+        where[a] = slice(None)
+        where[b] = self.near(b)[number]
+        return c, where
+
+    def at(self, part, ring, which):
+        axis, where = self.base(part, ring)
+        where[axis] = self.near(axis)[which]
+        return where
+
+    def push(self, part, ring, number, which, by, start, size, src=None):
+        axis, _ = self.base(part, ring)
+        n = self.rings.index(ring)
+        ref = self.region(self.at(part, ring, which), start, size)
+        copy = pltpu.make_async_remote_copy(
+            ref if src is None else src, ref, self.send_sem.at[part, n, number], self.recv_sem.at[part, n, number],
+            device_id=device(moved(self.pos, axis, by), self.core), device_id_type=MESH)
+        copy.start()
+        self.copies[part, ring, number] = copy
+
+    def begin(self, part, ring):
         start, size, _ = PARTS[part]
-        ref = region(part, where, core, start, size)
-        copy = pltpu.make_async_remote_copy(ref, ref, sib_send.at[part, number], sib_recv.at[part, number],
-                                            device_id=device(pos, 1 - core), device_id_type=MESH)
+        src = self.own_ref.at[pl.ds(start, size), :] if ring in ("a", "b0") else None
+        self.push(part, ring, 0, 0, 1, start, size, src)
+        self.push(part, ring, 1, 0, 3, start, size, src)
+
+    def onward(self, part, ring, left=None, right=None):
+        start, size, _ = PARTS[part]
+        half = size // 32 * 16
+        self.copies[part, ring, 0].wait_recv()
+        self.push(part, ring, 2, 1, 1, start, half)
+        if left:
+            left()
+        self.copies[part, ring, 1].wait_recv()
+        self.push(part, ring, 3, 2, 3, start + half, size - half)
+        if right:
+            right()
+
+    def end(self, part, ring):
+        self.copies[part, ring, 2].wait_recv()
+        self.copies[part, ring, 3].wait_recv()
+
+    def sibling(self, part, where, src=None):
+        start, size, _ = PARTS[part]
+        number = len(self.sibs[part])
+        ref = self.region(where, start, size)
+        copy = pltpu.make_async_remote_copy(
+            ref if src is None else src, ref, self.sib_send.at[part, number], self.sib_recv.at[part, number],
+            device_id=device(self.pos, 1 - self.core), device_id_type=MESH)
         copy.start()
-        sibs.append(copy)
-
-    def push(part, phase, number, where, start, size, axis, by):
-        ref = region(part, where, core, start, size)
-        copy = pltpu.make_async_remote_copy(ref, ref, send.at[part, phase, number], recv.at[part, phase, number],
-                                            device_id=device(moved(pos, axis, by), core), device_id_type=MESH)
-        copy.start()
-        return copy
-
-    def before(order, phase):
-        where = [pos[0], pos[1], pos[2]]
-        for a in order[:phase]:
-            where[a] = None
+        self.sibs[part].append(copy)
+
+    def share(self, part, ring, which):
+        return lambda: self.sibling(part, self.at(part, ring, which))
+
+    def row(self, part, number):
+        a, b, _ = PARTS[part][2]
+        where = list(self.pos)
+        where[a] = slice(None)
+        where[b] = self.near(b)[number]
         return where
 
-    for part in range(3):
-        to_sibling(0, part, before(PARTS[part][2], 0))
-    for phase in range(3):
-        firsts, seconds = [], []
-        for part in range(3):
-            start, size, order = PARTS[part]
-            axis = order[phase]
-            where = before(order, phase)
-            firsts.append((push(part, phase, 0, where, start, size, axis, 1), push(part, phase, 1, where, start, size, axis, 3)))
-        for part in range(3):
-            start, size, order = PARTS[part]
-            axis = order[phase]
-            up, down = firsts[part]
-            half = size // 32 * 16
-            left = before(order, phase)
-            left[axis] = lax.rem(pos[axis] + 3, 4)
-            right = before(order, phase)
-            right[axis] = lax.rem(pos[axis] + 1, 4)
-            up.wait_recv()
-            one = push(part, phase, 2, left, start, half, axis, 1)
-            to_sibling(1 + 3 * phase, part, left)
-            down.wait_recv()
-            two = push(part, phase, 3, right, start + half, size - half, axis, 3)
-            to_sibling(2 + 3 * phase, part, right)
-            seconds.append((one, two))
-        for part in range(3):
-            start, size, order = PARTS[part]
-            axis = order[phase]
-            one, two = seconds[part]
-            one.wait_recv()
-            two.wait_recv()
-            far = before(order, phase)
-            far[axis] = lax.rem(pos[axis] + 2, 4)
-            to_sibling(3 + 3 * phase, part, far)
-        for copy in [c for pair in firsts + seconds for c in pair]:
+    def run(self):
+        parts = range(3)
+        own = pltpu.make_async_copy(self.own_ref, self.out_ref.at[self.pos[0], self.core, self.pos[1], self.pos[2]], self.local)
+        own.start()
+        greet(self.pos, self.core)
+        for p in parts:
+            self.begin(p, "a")
+        for p in parts:
+            self.begin(p, "b0")
+        for p in parts:
+            start, size, _ = PARTS[p]
+            self.sibling(p, self.pos, self.own_ref.at[pl.ds(start, size), :])
+        own.wait()
+        for p in parts:
+            def arrived(which, p=p):
+                self.begin(p, "b" + str(which))
+                self.sibling(p, self.at(p, "a", which))
+            self.onward(p, "a", lambda: arrived(1), lambda: arrived(2))
+        for p in parts:
+            self.onward(p, "b0")
+        for p in parts:
+            self.end(p, "a")
+            self.begin(p, "b3")
+            self.begin(p, "c0")
+            self.sibling(p, self.at(p, "a", 3))
+        for p in parts:
+            self.onward(p, "b1")
+            self.onward(p, "b2")
+        for p in parts:
+            self.end(p, "b0")
+            self.onward(p, "b3")
+            self.begin(p, "c1")
+            self.begin(p, "c2")
+            self.sibling(p, self.row(p, 1))
+            self.sibling(p, self.row(p, 2))
+        for p in parts:
+            self.onward(p, "c0", self.share(p, "c0", 1), self.share(p, "c0", 2))
+        for p in parts:
+            for ring in ("b1", "b2", "b3"):
+                self.end(p, ring)
+            self.begin(p, "c3")
+            self.sibling(p, self.row(p, 3))
+        for ring in ("c1", "c2", "c3"):
+            for p in parts:
+                self.onward(p, ring, self.share(p, ring, 1), self.share(p, ring, 2))
+            for p in parts:
+                before = {"c1": "c0", "c2": "c1", "c3": "c2"}[ring]
+                self.end(p, before)
+                self.sibling(p, self.at(p, before, 3))
+        for p in parts:
+            self.end(p, "c3")
+            self.sibling(p, self.at(p, "c3", 3))
+        for copy in self.copies.values():
             copy.wait_send()
-    for copy in sibs:
-        copy.wait_send()
-        copy.wait_recv()
+        for copies in self.sibs:
+            for copy in copies:
+                copy.wait_send()
+                copy.wait_recv()
+
+
+def gather_kernel(*refs):
+    Gather(*refs).run()
 
 
 def gather(own):
@@ -122,8 +199,7 @@
         out_shape=jax.ShapeDtypeStruct((4, 2, 4, 4, ROWS, 128), jnp.bfloat16),
         in_specs=[pl.BlockSpec(memory_space=pl.ANY)],
         out_specs=pl.BlockSpec(memory_space=pl.ANY),
-        scratch_shapes=[pltpu.SemaphoreType.DMA((3, 3, 4)), pltpu.SemaphoreType.DMA((3, 3, 4)),
-                        pltpu.SemaphoreType.DMA((3, 10)), pltpu.SemaphoreType.DMA((3, 10)), pltpu.SemaphoreType.DMA],
+        scratch_shapes=Gather.scratch,
         compiler_params=pltpu.CompilerParams(collective_id=0, has_side_effects=True),
     )(own)
 
@@ -655,148 +731,167 @@
     return half, size - half
 
 
-def pick(ref, axes, axis, index, start, size):
-    idx = tuple(index if a == axis else slice(None) for a in axes)
-    return ref.at[idx + (pl.ds(start, size), slice(None))]
-
-
-def each(count, body):
-    if count == 0:
-        body(())
-        return
-    @pl.loop(0, 4 ** count)
-    def _(n):
-        body(tuple(lax.rem(lax.div(n, 4 ** (count - 1 - d)), 4) for d in range(count)))
-
-
-def scatter_kernel(in_ref, out_ref, *scratch):
-    send, recv = scratch[-2:]
-    bufs = list(scratch[:-2])
-    pos, core = place()
-    greet(pos, core, sibling=False)
-    take = iter(bufs)
-    got = {}
-    for part in range(3):
-        for phase in range(3):
-            got[part, phase] = [next(take) for _ in range(9 if phase < 2 else 8)]
-
-    def push(part, phase, number, src, dst, axis, by):
-        copy = pltpu.make_async_remote_copy(src, dst, send.at[part, phase, number], recv.at[part, phase, number],
-                                            device_id=device(moved(pos, axis, by), core), device_id_type=MESH)
+class Scatter:
+    names = ("c0", "c1", "c2", "c3", "b", "a")
+    count = 3 * (6 * 8 + 2)
+
+    @staticmethod
+    def scratch():
+        out = []
+        for _, size, _ in PARTS:
+            h0, h1 = halves(size)
+            for name in Scatter.names:
+                lead = () if name == "a" else (4,)
+                out += [pltpu.VMEM(lead + (n, 128), jnp.bfloat16) for n in (h0, h1, h1, h0, h0, h1, h0, h1)]
+            out += [pltpu.VMEM((4, 4, size, 128), jnp.bfloat16), pltpu.VMEM((4, size, 128), jnp.bfloat16)]
+        return out + [pltpu.SemaphoreType.DMA((3, 6, 6)), pltpu.SemaphoreType.DMA((3, 6, 6))]
+
+    def __init__(self, in_ref, out_ref, *scratch):
+        self.in_ref, self.out_ref = in_ref, out_ref
+        self.send, self.recv = scratch[-2:]
+        take = iter(scratch[:-2])
+        self.buf, self.rows, self.line = {}, [], []
+        for p in range(3):
+            for name in self.names:
+                self.buf[p, name] = [next(take) for _ in range(8)]
+            self.rows.append(next(take))
+            self.line.append(next(take))
+        self.pos, self.core = place()
+        self.copies = {}
+
+    def near(self, axis):
+        q = self.pos[axis]
+        return [q] + [lax.rem(q + k, 4) for k in (3, 1, 2)]
+
+    def axis(self, p, name):
+        return PARTS[p][2]["abc".index(name[0])]
+
+    def source(self, p, name, which, lo, n):
+        a, b, c = PARTS[p][2]
+        if name == "a":
+            return self.line[p].at[self.near(a)[which], pl.ds(lo, n), :]
+        if name == "b":
+            return self.rows[p].at[which, :, pl.ds(lo, n), :]
+        where = [slice(None)] * 3
+        where[b] = self.near(b)[int(name[1])]
+        where[c] = self.near(c)[which]
+        return self.in_ref.at[where[0], where[1], where[2], pl.ds(PARTS[p][0] + lo, n), :]
+
+    def push(self, p, name, number, src, by):
+        n = self.names.index(name)
+        copy = pltpu.make_async_remote_copy(
+            src, self.buf[p, name][number], self.send.at[p, n, number], self.recv.at[p, n, number],
+            device_id=device(moved(self.pos, self.axis(p, name), by), self.core), device_id_type=MESH)
         copy.start()
-        return copy
-
-    def current(part, phase):
-        start, size, order = PARTS[part]
-        axes = [0, 1, 2]
-        for a in order[::-1][:phase]:
-            axes.remove(a)
-        if phase == 0:
-            return in_ref, axes, start
-        return got[part, phase - 1][8], axes, 0
-
-    copies = {}
-
-    def begin(part, phase):
-        ref, axes, base = current(part, phase)
-        start, size, order = PARTS[part]
-        axis = order[2 - phase]
-        h0, h1 = halves(size)
-        q = pos[axis]
-        far, right, left = (lax.rem(q + k, 4) for k in (2, 1, 3))
-        b = got[part, phase]
-        copies[part, phase] = [
-            push(part, phase, 0, pick(ref, axes, axis, far, base, h0), b[0], axis, 1),
-            push(part, phase, 1, pick(ref, axes, axis, far, base + h0, h1), b[1], axis, 3),
-            push(part, phase, 2, pick(ref, axes, axis, right, base + h0, h1), b[2], axis, 1),
-            push(part, phase, 3, pick(ref, axes, axis, left, base, h0), b[3], axis, 3),
-        ]
-
-    def add(ref, axes, axis, index, base, size, others, put):
-        rest = [a for a in axes if a != axis]
-
-        def body(at):
-            full = dict(zip(rest, at))
-            idx = tuple(index if a == axis else full[a] for a in axes)
-            total = ref[idx + (pl.ds(base, size), slice(None))].astype(jnp.float32)
+        self.copies[p, name, number] = copy
+
+    def far(self, p, name):
+        h0, h1 = halves(PARTS[p][1])
+        self.push(p, name, 0, self.source(p, name, 3, 0, h0), 1)
+        self.push(p, name, 1, self.source(p, name, 3, h0, h1), 3)
+
+    def raw_right(self, p, name):
+        h0, h1 = halves(PARTS[p][1])
+        self.push(p, name, 2, self.source(p, name, 2, h0, h1), 1)
+
+    def raw_left(self, p, name):
+        h0, h1 = halves(PARTS[p][1])
+        self.push(p, name, 3, self.source(p, name, 1, 0, h0), 3)
+
+    def begin(self, p, name):
+        self.far(p, name)
+        self.raw_right(p, name)
+        self.raw_left(p, name)
+
+    def add(self, name, mine, others, put):
+        def one(*at):
+            total = mine[at + (slice(None), slice(None))].astype(jnp.float32)
             for other in others:
                 total = total + other[at + (slice(None), slice(None))].astype(jnp.float32)
             put(at, total)
 
-        each(len(rest), body)
-
-    def middle(part, phase):
-        ref, axes, base = current(part, phase)
-        start, size, order = PARTS[part]
-        axis = order[2 - phase]
-        h0, h1 = halves(size)
-        q = pos[axis]
-        right, left = (lax.rem(q + k, 4) for k in (1, 3))
-        b = got[part, phase]
-        c = copies[part, phase]
+        if name == "a":
+            one()
+        else:
+            pl.loop(0, 4)(lambda i: one(i))
+
+    def onward(self, p, name):
+        h0, h1 = halves(PARTS[p][1])
+        b = self.buf[p, name]
 
         def to(ref):
             def put(at, total):
                 ref[at + (slice(None), slice(None))] = total.astype(jnp.bfloat16)
             return put
 
-        c[0].wait_recv()
-        add(ref, axes, axis, right, base, h0, [b[0]], to(b[6]))
-        c.append(push(part, phase, 4, b[6], b[4], axis, 1))
-        c[1].wait_recv()
-        add(ref, axes, axis, left, base + h0, h1, [b[1]], to(b[7]))
-        c.append(push(part, phase, 5, b[7], b[5], axis, 3))
-
-    def finish(part, phase):
-        ref, axes, base = current(part, phase)
-        start, size, order = PARTS[part]
-        axis = order[2 - phase]
+        self.copies[p, name, 0].wait_recv()
+        self.add(name, self.source(p, name, 2, 0, h0), [b[0]], to(b[6]))
+        self.push(p, name, 4, b[6], 1)
+        self.copies[p, name, 1].wait_recv()
+        self.add(name, self.source(p, name, 1, h0, h1), [b[1]], to(b[7]))
+        self.push(p, name, 5, b[7], 3)
+
+    def end(self, p, name):
+        start, size, _ = PARTS[p]
         h0, h1 = halves(size)
-        q = pos[axis]
-        b = got[part, phase]
-        c = copies[part, phase]
-        for copy in c[2:]:
-            copy.wait_recv()
+        b = self.buf[p, name]
+        for number in (3, 2, 4, 5):
+            self.copies[p, name, number].wait_recv()
         for lo, n, others in ((0, h0, [b[3], b[4]]), (h0, h1, [b[2], b[5]])):
             def put(at, total, lo=lo, n=n):
-                if phase == 2:
-                    out_ref[start + lo:start + lo + n, :] = total
+                if name == "a":
+                    self.out_ref[start + lo:start + lo + n, :] = total
+                elif name == "b":
+                    self.line[p][at + (pl.ds(lo, n), slice(None))] = total.astype(jnp.bfloat16)
                 else:
-                    b[8][at + (pl.ds(lo, n), slice(None))] = total.astype(jnp.bfloat16)
-            add(ref, axes, axis, q, base + lo, n, others, put)
-
-    for phase in range(3):
-        for part in range(3):
-            if phase == 0:
-                begin(part, 0)
-        for part in range(3):
-            middle(part, phase)
-        for part in range(3):
-            finish(part, phase)
-            if phase < 2:
-                begin(part, phase + 1)
-    for c in copies.values():
-        for copy in c:
+                    self.rows[p][(int(name[1]),) + at + (pl.ds(lo, n), slice(None))] = total.astype(jnp.bfloat16)
+            self.add(name, self.source(p, name, 0, lo, n), others, put)
+
+    def run(self):
+        parts = range(3)
+
+        def each(step, name):
+            for p in parts:
+                step(p, name)
+
+        greet(self.pos, self.core, sibling=False)
+        each(self.begin, "c3")
+        each(self.begin, "c1")
+        each(self.onward, "c3")
+        each(self.begin, "c2")
+        each(self.onward, "c1")
+        each(self.end, "c3")
+        each(self.far, "b")
+        each(self.begin, "c0")
+        each(self.onward, "c2")
+        each(self.end, "c1")
+        each(self.raw_left, "b")
+        each(self.onward, "c0")
+        each(self.end, "c2")
+        each(self.raw_right, "b")
+        each(self.onward, "b")
+        for p in parts:
+            self.end(p, "c0")
+            self.end(p, "b")
+            self.begin(p, "a")
+        each(self.onward, "a")
+        each(self.end, "a")
+        for copy in self.copies.values():
             copy.wait_send()
 
 
+def scatter_kernel(*refs):
+    Scatter(*refs).run()
+
+
 def scatter(parts):
-    scratch = []
-    for part in range(3):
-        _, size, _ = PARTS[part]
-        h0, h1 = halves(size)
-        for phase in range(3):
-            lead = (4,) * (2 - phase)
-            sizes = [h0, h1, h1, h0, h0, h1, h0, h1] + ([size] if phase < 2 else [])
-            scratch += [pltpu.VMEM(lead + (n, 128), jnp.bfloat16) for n in sizes]
-    scratch += [pltpu.SemaphoreType.DMA((3, 3, 6)), pltpu.SemaphoreType.DMA((3, 3, 6))]
     return pl.pallas_call(
         scatter_kernel,
+        grid=(1,),
         out_shape=jax.ShapeDtypeStruct((ROWS, 128), jnp.float32),
-        grid=(1,),
         in_specs=[pl.BlockSpec((4, 4, 4, ROWS, 128), lambda e: (0, 0, 0, 0, 0))],
         out_specs=pl.BlockSpec((ROWS, 128), lambda e: (0, 0)),
-        scratch_shapes=scratch,
+        scratch_shapes=Scatter.scratch(),
         compiler_params=pltpu.CompilerParams(collective_id=1, has_side_effects=True, vmem_limit_bytes=VMEM_LIMIT),
     )(parts)
 

time: 202 us -> 192 us (0.950)
  Pallas kernels: 186 us -> 175 us
    pallas_call x1, Pallas kernels: 54.2 us -> 46.5 us  [gather(): pl.pallas_call(gather_kernel, out_shape=jax.ShapeDtypeStruct((4, 2, 4, 4,...]
  transfers between devices with their start and end apart: 9 -> 9, of which waited for: 1 -> 1; matrix products, arithmetic and copies ran while one was open for 2% -> 2% of each run, Pallas kernels for 8% -> 9%
where the time goes in v2:
time: 192 us; the launch traced here: 191 us
  Pallas kernels  175 us (91%)
  local copies, waits for them, and re-layouts  6.22 us (3%)
  other arithmetic  4.67 us (2%)
  starting transfers between devices  2.28 us (1%)
    pallas_call x1, Pallas kernels, gather(): pl.pallas_call(gather_kernel, out_shape=jax.ShapeDtypeStruct((4, 2, 4, 4,...  46.5 us
    pallas_call x1, Pallas kernels, scatter(): pl.pallas_call(scatter_kernel, grid=(1,), out_shape=jax.ShapeDtypeStruct(...  45.7 us
    pallas_call x1, Pallas kernels, late_grads(): pl.pallas_call(late_kernel, grid=(2,), out_shape=[HALVES, jax.ShapeDtypeS...  23.6 us
    pallas_call x1, Pallas kernels, second_part(): pl.pallas_call(second_kernel, grid=(6,), out_shape=outs + [bf(16, 2, 128,...  20.6 us
    pallas_call x1, Pallas kernels, heads(): pl.pallas_call(head_kernel, out_shape=jax.ShapeDtypeStruct((16, 2, 128, 1...  16.3 us
    pallas_call x1, Pallas kernels, early_grads(): pl.pallas_call(early_kernel, grid=(2,), out_shape=HALVES, in_specs=[pl.Bl...  8.72 us
    pallas_call x1, Pallas kernels, first_part(): pl.pallas_call(first_kernel, grid=(3,), out_shape=outs, in_specs=[pl.Bloc...  7.88 us
    pallas_call x1, Pallas kernels, third_part(): pl.pallas_call(third_kernel, grid=(1,), out_shape=outs, in_specs=[const(*...  5.92 us
  transfers between devices with their start and end apart: 9, of which 1 were waited for; matrix products, arithmetic and copies ran while one was open for 2% of the time, Pallas kernels for 9%

profile of v2, /device:TPU:0, one launch (start us, length us, event | category | flops | bytes accessed | tf_op | source)
XLA Modules:
  0.0 191.1 jit_solution(1318447844648740720)
XLA Ops:
  0.8 1.6 pad.4.refs_0_
  2.3 46.5 %shard_map.58 = bf16[4,2,4,4,448,128]{5,4,3,2,1,0:T(8,128)(2,1)} custom-call(bf16[448,128]{1,0:T(8,128)(2,1)} %pad.4.refs_0_), custom_call_target="tpu_custom_call" | custom-call | tf_op jit(solution)/shard_map/pallas_call | solution.py:197
  48.9 0.3 fusion.3
  49.2 0.7 pad_maximum_fusion.tables_ref
  49.9 7.9 %shard_map.59 = (bf16[768,2304]{1,0:T(8,128)(2,1)}, bf16[768,768]{1,0:T(8,128)(2,1)}, bf16[12,2,128,128]{3,2,1,0:T(8,128)(2,1)}, bf16[768,128]{1,0:T(8,128)(2,1)...) custom-call(bf16[128,448,128]{2,1,0:T(8,128)(2,1)} %bitcast.12, ...), custom_call_target="tpu_custom_call" | custom-call | tf_op jit(solution)/shard_map/pallas_call | solution.py:464
  57.8 20.6 %shard_map.60 = (f32[128,768]{1,0:T(8,128)}, f32[128,768]{1,0:T(8,128)}, bf16[3072,128]{1,0:T(8,128)(2,1)}, bf16[128,3072]{1,0:T(8,128)(2,1)}, f32[24,128]{1,0:T(8,128)}, /*index=5*/bf16[16,2,128,128]{3,2,1,0:T(8,128)(2,1)}) custom-call(bf16[128,448,128]{2,1,0:T(8,128)(2,1)} %bitcast.13, bf16[128,768]{1,0:T(8,128)(2,1)} %get-tuple-element.23.h2_ref, ...), custom_call_target="tpu_custom_call" | custom-call | tf_op jit(solution)/shard_map/pallas_call | solution.py:522
  78.5 0.5 collective-permute-start.1
  79.1 0.8 maximum_maximum_fusion
  80.1 0.4 collective-permute-start.2
  80.6 16.3 %shard_map.61.heads_ref = bf16[16,2,128,128]{3,2,1,0:T(8,128)(2,1)} custom-call(bf16[16,2,128,128]{3,2,1,0:T(8,128)(2,1)} %get-tuple-element.29.in_ref), custom_call_target="tpu_custom_call" | custom-call | tf_op jit(solution)/shard_map/pallas_call | solution.py:364
  96.9 1.4 fusion.4.vec_ref
  98.4 0.6 copy-done.4
  99.4 0.9 copy-done.5
  100.2 23.6 %shard_map.62 = (bf16[4,16,448,128]{3,2,1,0:T(8,128)(2,1)}, bf16[12,2,128,128]{3,2,1,0:T(8,128)(2,1)}) custom-call(f32[80,128]{1,0:T(8,128)} %fusion.4.vec_ref, bf16[3072,128]{1,0:T(8,128)(2,1)} %get-tuple-element.26.act_ref, bf16[3072,128]{1,0:T(8,128)(2,1)} %copy-done.5, bf16[128,768]{1,0:T(8,128)(2,1)} %bitcast.17, bf16[128,768]{1,0:T(8,128)(2,1)} %copy-done.3, ...), custom_call_target="tpu_custom_call" | custom-call | tf_op jit(solution)/shard_map/pallas_call | solution.py:685
  123.8 5.9 %shard_map.63 = (bf16[128,768]{1,0:T(8,128)(2,1)}, f32[128,768]{1,0:T(8,128)}, bf16[768,128]{1,0:T(8,128)(2,1)}, bf16[128,2304]{1,0:T(8,128)(2,1)}, f32[80,128]{1,0:T(8,128)}) custom-call(bf16[12,2,128,128]{3,2,1,0:T(8,128)(2,1)} %get-tuple-element.30.back_ref, bf16[128,768]{1,0:T(8,128)(2,1)} %bitcast.22, bf16[128,768]{1,0:T(8,128)(2,1)} %bitcast.18, ...), custom_call_target="tpu_custom_call" | custom-call | tf_op jit(solution)/shard_map/pallas_call | solution.py:578
  129.8 0.5 collective-permute-start.6
  130.4 0.4 collective-permute-start.5
  130.8 1.8 collective-permute-done.5
  132.6 1.4 add.36.vec_ref
  134.0 0.6 copy-done.8
  134.7 0.3 copy-done.6
  135.0 8.7 %shard_map.64 = bf16[4,16,448,128]{3,2,1,0:T(8,128)(2,1)} custom-call(s32[1]{0:T(128)} %bitcast.7.core_ref, f32[80,128]{1,0:T(8,128)} %add.36.vec_ref, bf16[768,128]{1,0:T(8,128)(2,1)} %get-tuple-element.39.h1_ref, bf16[768,128]{1,0:T(8,128)(2,1)} %copy-done.8, bf16[768,128]{1,0:T(8,128)(2,1)} %get-tuple-element.40.att_ref, ...), custom_call_target="tpu_custom_call", output_to_operand_aliasing={{}: (14, {})} | custom-call | tf_op jit(solution)/shard_map/pallas_call | solution.py:717
  143.7 45.7 %shard_map.65 = f32[448,128]{1,0:T(8,128)} custom-call(bf16[4,4,4,448,128]{4,3,2,1,0:T(8,128)(2,1)} %bitcast.14), custom_call_target="tpu_custom_call" | custom-call | tf_op jit(solution)/shard_map/pallas_call | solution.py:888
  189.4 1.6 slice_bitcast_fusion
  (40 shorter events, 1.1 us)
Async XLA Ops:
  57.8 21.3 %copy-start = (bf16[1,128,768]{2,1,0:T(8,128)(2,1)S(1)}, bf16[1,128,768]{2,1,0:T(8,128)(2,1)}, u32[]{:S(2)}) copy-start(bf16[1,128,768]{2,1,0:T(8,128)(2,1)} %param.5) | copy-start | bytes 589828
  57.8 22.8 %copy-start.2 = (bf16[768,128]{1,0:T(8,128)(2,1)S(1)}, bf16[768,128]{1,0:T(8,128)(2,1)}, u32[]{:S(2)}) copy-start(bf16[768,128]{1,0:T(8,128)(2,1)} %get-tuple-element.28.h2_ref) | copy-start | bytes 589828
  78.4 51.4 %copy-start.7 = (bf16[768,128]{1,0:T(8,128)(2,1)S(1)}, bf16[768,128]{1,0:T(8,128)(2,1)}, u32[]{:S(2)}) copy-start(bf16[768,128]{1,0:T(8,128)(2,1)} %get-tuple-element.39.h1_ref) | copy-start | bytes 589828
  78.4 19.9 %collective-permute-start.3 = (bf16[128,3072]{1,0:T(8,128)(2,1)}, bf16[128,3072]{1,0:T(8,128)(2,1)S(1)}, u32[]{:S(2)}, u32[]{:S(2)}) collective-permute-start(bf16[128,3072]{1,0:T(8,128)(2,1)} %get-tuple-element.27.dup_ref), channel_id=1, source_target_pairs={{0,16},{16,0},{1,17},{17,1},{2,18},{18,2},{3,19},{19,3},{4,20},{20... | collective-permute-start | bytes 2359304 | tf_op jit(solution)/shard_map/ppermute | solution.py:900
  78.5 19.9 %collective-permute-start.1 = (bf16[3072,128]{1,0:T(8,128)(2,1)}, bf16[3072,128]{1,0:T(8,128)(2,1)S(1)}, u32[]{:S(2)}, u32[]{:S(2)}) collective-permute-start(bf16[3072,128]{1,0:T(8,128)(2,1)} %get-tuple-element.26.act_ref), channel_id=1, source_target_pairs={{0,16},{16,0},{1,17},{17,1},{2,18},{18,2},{3,19},{19,3},{4,20},{20... | collective-permute-start | bytes 2359304 | tf_op jit(solution)/shard_map/ppermute | solution.py:900
  79.9 17.0 %collective-permute-start = (f32[80,128]{1,0:T(8,128)S(1)}, f32[80,128]{1,0:T(8,128)S(1)}, u32[]{:S(2)}, u32[]{:S(2)}) collective-permute-start(f32[80,128]{1,0:T(8,128)S(1)} %maximum_maximum_fusion), channel_id=1, source_target_pairs={{0,16},{16,0},{1,17},{17,1},{2,18},{18,2},{3,19},{19,3},{4,20},{20... | collective-permute-start | bytes 122888 | tf_op jit(solution)/shard_map/ppermute | solution.py:900
  80.1 18.2 %collective-permute-start.2 = (bf16[128,768]{1,0:T(8,128)(2,1)S(1)}, bf16[128,768]{1,0:T(8,128)(2,1)S(1)}, u32[]{:S(2)}, u32[]{:S(2)}) collective-permute-start(bf16[128,768]{1,0:T(8,128)(2,1)S(1)} %bitcast.20), channel_id=1, source_target_pairs={{0,16},{16,0},{1,17},{17,1},{2,18},{18,2},{3,19},{19,3},{4,20},{20... | collective-permute-start | bytes 589832 | tf_op jit(solution)/shard_map/ppermute | solution.py:900
  80.5 17.8 %collective-permute-start.4 = (bf16[768,128]{1,0:T(8,128)(2,1)S(1)}, bf16[768,128]{1,0:T(8,128)(2,1)S(1)}, u32[]{:S(2)}, u32[]{:S(2)}) collective-permute-start(bf16[768,128]{1,0:T(8,128)(2,1)S(1)} %copy-done.2), channel_id=1, source_target_pairs={{0,16},{16,0},{1,17},{17,1},{2,18},{18,2},{3,19},{19,3},{4,20},{20... | collective-permute-start | bytes 589832 | tf_op jit(solution)/shard_map/ppermute | solution.py:900
  98.3 0.7 copy-start.4
  98.3 0.8 copy-start.3
  98.4 1.0 copy-start.1
  99.3 0.9 copy-start.5
  129.8 4.2 %collective-permute-start.8 = (bf16[128,2304]{1,0:T(8,128)(2,1)}, bf16[128,2304]{1,0:T(8,128)(2,1)S(1)}, u32[]{:S(2)}, u32[]{:S(2)}) collective-permute-start(bf16[128,2304]{1,0:T(8,128)(2,1)} %get-tuple-element.41.dqkv_ref), channel_id=1, source_target_pairs={{0,16},{16,0},{1,17},{17,1},{2,18},{18,2},{3,19},{19,3},{4,20},{20... | collective-permute-start | bytes 1769480 | tf_op jit(solution)/shard_map/ppermute | solution.py:900
  129.8 4.2 %collective-permute-start.6 = (bf16[768,128]{1,0:T(8,128)(2,1)S(1)}, bf16[768,128]{1,0:T(8,128)(2,1)S(1)}, u32[]{:S(2)}, u32[]{:S(2)}) collective-permute-start(bf16[768,128]{1,0:T(8,128)(2,1)S(1)} %copy-done.7), channel_id=1, source_target_pairs={{0,16},{16,0},{1,17},{17,1},{2,18},{18,2},{3,19},{19,3},{4,20},{20... | collective-permute-start | bytes 589832 | tf_op jit(solution)/shard_map/ppermute | solution.py:900
  130.3 3.7 %collective-permute-start.7 = (bf16[768,128]{1,0:T(8,128)(2,1)}, bf16[768,128]{1,0:T(8,128)(2,1)S(1)}, u32[]{:S(2)}, u32[]{:S(2)}) collective-permute-start(bf16[768,128]{1,0:T(8,128)(2,1)} %get-tuple-element.40.att_ref), channel_id=1, source_target_pairs={{0,16},{16,0},{1,17},{17,1},{2,18},{18,2},{3,19},{19,3},{4,20},{20... | collective-permute-start | bytes 589832 | tf_op jit(solution)/shard_map/ppermute | solution.py:900
  130.4 2.2 %collective-permute-start.5 = (f32[80,128]{1,0:T(8,128)}, f32[80,128]{1,0:T(8,128)S(1)}, u32[]{:S(2)}, u32[]{:S(2)}) collective-permute-start(f32[80,128]{1,0:T(8,128)} %get-tuple-element.38), channel_id=1, source_target_pairs={{0,16},{16,0},{1,17},{17,1},{2,18},{18,2},{3,19},{19,3},{4,20},{20... | collective-permute-start | bytes 122888 | tf_op jit(solution)/shard_map/ppermute | solution.py:900
  134.0 0.7 copy-start.8
  134.0 0.7 copy-start.9
  134.0 1.0 copy-start.6

commit v3 on v2

v3 whole, which is shorter than its diff:
```python
import functools

import jax
import jax.numpy as jnp
from jax import lax
from jax.experimental import pallas as pl
from jax.experimental.pallas import tpu as pltpu
from jax.sharding import Mesh
from jax.sharding import PartitionSpec as P

DP_SEQ = ("dp_0", "dp_1", "seq_0", "seq_1")
SEQ = ("seq_0", "seq_1")
DP = ("dp_0", "dp_1")
VMEM_LIMIT = 60 * 2**20
MESH = pl.DeviceIdType.MESH
ROWS = 448
PARTS = ((0, 144, (0, 2, 1)), (144, 144, (2, 1, 0)), (288, 160, (1, 0, 2)))


def place():
    return [lax.axis_index("dp_0"), lax.axis_index("seq_0"), lax.axis_index("seq_1")], lax.axis_index("dp_1")


def device(pos, core):
    return (pos[0], core, pos[1], pos[2])


def moved(pos, axis, by):
    out = list(pos)
    out[axis] = lax.rem(pos[axis] + by, 4)
    return out


def greet(pos, core, sibling=True):
    barrier = pltpu.get_barrier_semaphore()
    others = [device(moved(pos, a, by), core) for a in range(3) for by in (1, 3)]
    if sibling:
        others.append(device(pos, 1 - core))
    for other in others:
        pl.semaphore_signal(barrier, inc=1, device_id=other, device_id_type=MESH)
    pl.semaphore_wait(barrier, len(others))


class Gather:
    scratch = [pltpu.SemaphoreType.DMA((3, 9, 4)), pltpu.SemaphoreType.DMA((3, 9, 4)),
               pltpu.SemaphoreType.DMA((3, 19)), pltpu.SemaphoreType.DMA((3, 19)), pltpu.SemaphoreType.DMA]
    rings = ("a", "b0", "b1", "b2", "b3", "c0", "c1", "c2", "c3")

    def __init__(self, own_ref, out_ref, send, recv, sib_send, sib_recv, local):
        self.own_ref, self.out_ref, self.local = own_ref, out_ref, local
        self.send_sem, self.recv_sem, self.sib_send, self.sib_recv = send, recv, sib_send, sib_recv
        self.pos, self.core = place()
        self.copies, self.sibs = {}, [[], [], []]

    def near(self, axis):
        q = self.pos[axis]
        return [q] + [lax.rem(q + k, 4) for k in (3, 1, 2)]

    def region(self, where, start, size):
        return self.out_ref.at[where[0], self.core, where[1], where[2], pl.ds(start, size), :]

    def base(self, part, ring):
        a, b, c = PARTS[part][2]
        where = list(self.pos)
        if ring == "a":
            return a, where
        number = int(ring[1])
        if ring[0] == "b":
            where[a] = self.near(a)[number]
            return b, where
        where[a] = slice(None)
        where[b] = self.near(b)[number]
        return c, where

    def at(self, part, ring, which):
        axis, where = self.base(part, ring)
        where[axis] = self.near(axis)[which]
        return where

    def push(self, part, ring, number, which, by, start, size, src=None):
        axis, _ = self.base(part, ring)
        n = self.rings.index(ring)
        ref = self.region(self.at(part, ring, which), start, size)
        copy = pltpu.make_async_remote_copy(
            ref if src is None else src, ref, self.send_sem.at[part, n, number], self.recv_sem.at[part, n, number],
            device_id=device(moved(self.pos, axis, by), self.core), device_id_type=MESH)
        copy.start()
        self.copies[part, ring, number] = copy

    def begin(self, part, ring):
        start, size, _ = PARTS[part]
        src = self.own_ref.at[pl.ds(start, size), :] if ring in ("a", "b0") else None
        self.push(part, ring, 0, 0, 1, start, size, src)
        self.push(part, ring, 1, 0, 3, start, size, src)

    def onward(self, part, ring, left=None, right=None):
        start, size, _ = PARTS[part]
        half = size // 32 * 16
        self.copies[part, ring, 0].wait_recv()
        self.push(part, ring, 2, 1, 1, start, half)
        if left:
            left()
        self.copies[part, ring, 1].wait_recv()
        self.push(part, ring, 3, 2, 3, start + half, size - half)
        if right:
            right()

    def end(self, part, ring):
        self.copies[part, ring, 2].wait_recv()
        self.copies[part, ring, 3].wait_recv()

    def sibling(self, part, where, src=None):
        start, size, _ = PARTS[part]
        number = len(self.sibs[part])
        ref = self.region(where, start, size)
        copy = pltpu.make_async_remote_copy(
            ref if src is None else src, ref, self.sib_send.at[part, number], self.sib_recv.at[part, number],
            device_id=device(self.pos, 1 - self.core), device_id_type=MESH)
        copy.start()
        self.sibs[part].append(copy)

    def share(self, part, ring, which):
        return lambda: self.sibling(part, self.at(part, ring, which))

    def row(self, part, number):
        a, b, _ = PARTS[part][2]
        where = list(self.pos)
        where[a] = slice(None)
        where[b] = self.near(b)[number]
        return where

    def run(self):
        parts = range(3)
        own = pltpu.make_async_copy(self.own_ref, self.out_ref.at[self.pos[0], self.core, self.pos[1], self.pos[2]], self.local)
        own.start()
        greet(self.pos, self.core)
        for p in parts:
            self.begin(p, "a")
        for p in parts:
            self.begin(p, "b0")
        for p in parts:
            start, size, _ = PARTS[p]
            self.sibling(p, self.pos, self.own_ref.at[pl.ds(start, size), :])
        own.wait()
        for p in parts:
            def arrived(which, p=p):
                self.begin(p, "b" + str(which))
                self.sibling(p, self.at(p, "a", which))
            self.onward(p, "a", lambda: arrived(1), lambda: arrived(2))
        for p in parts:
            self.onward(p, "b0")
        for p in parts:
            self.end(p, "a")
            self.begin(p, "b3")
            self.begin(p, "c0")
            self.sibling(p, self.at(p, "a", 3))
        for p in parts:
            self.onward(p, "b1")
            self.onward(p, "b2")
        for p in parts:
            self.end(p, "b0")
            self.onward(p, "b3")
            self.begin(p, "c1")
            self.begin(p, "c2")
            self.sibling(p, self.row(p, 1))
            self.sibling(p, self.row(p, 2))
        for p in parts:
            self.onward(p, "c0", self.share(p, "c0", 1), self.share(p, "c0", 2))
        for p in parts:
            for ring in ("b1", "b2", "b3"):
                self.end(p, ring)
            self.begin(p, "c3")
            self.sibling(p, self.row(p, 3))
        for ring in ("c1", "c2", "c3"):
            for p in parts:
                self.onward(p, ring, self.share(p, ring, 1), self.share(p, ring, 2))
            for p in parts:
                before = {"c1": "c0", "c2": "c1", "c3": "c2"}[ring]
                self.end(p, before)
                self.sibling(p, self.at(p, before, 3))
        for p in parts:
            self.end(p, "c3")
            self.sibling(p, self.at(p, "c3", 3))
        for copy in self.copies.values():
            copy.wait_send()
        for copies in self.sibs:
            for copy in copies:
                copy.wait_send()
                copy.wait_recv()


def gather_kernel(*refs):
    Gather(*refs).run()


def gather(own):
    return pl.pallas_call(
        gather_kernel,
        out_shape=jax.ShapeDtypeStruct((4, 2, 4, 4, ROWS, 128), jnp.bfloat16),
        in_specs=[pl.BlockSpec(memory_space=pl.ANY)],
        out_specs=pl.BlockSpec(memory_space=pl.ANY),
        scratch_shapes=Gather.scratch,
        compiler_params=pltpu.CompilerParams(collective_id=0, has_side_effects=True),
    )(own)


EIGHTH = 16 * 433
W_QKV = (24, 768, 18)
W_OUT = (13866, 768, 6)
W_UP = (18480, 768, 24)
W_DOWN = (36936, 3072, 6)
VECTORS = {"ln1_gain": (0, 6), "ln1_shift": (6, 6), "ln2_gain": (12, 6), "ln2_shift": (18, 6),
           "b_qkv": (13848, 18), "b_out": (18474, 6), "b_up": (36912, 24), "b_down": (55368, 6)}


HEADS = 12
TILE = 1024
KEYS = 1024


class Exchange:
    scratch = [pltpu.SemaphoreType.DMA((16,)), pltpu.SemaphoreType.DMA((16,)), pltpu.SemaphoreType.DMA]

    def __init__(self, to_heads, in_ref, out_ref, send, recv, local):
        self.to_heads, self.in_ref, self.out_ref = to_heads, in_ref, out_ref
        self.send, self.recv, self.local = send, recv, local
        self.x, self.core = lax.axis_index("dp_0"), lax.axis_index("dp_1")
        self.me = lax.axis_index("seq_0") * 4 + lax.axis_index("seq_1")
        self.others = [lax.rem(self.me + k, 16) for k in range(1, 16)]

    def where(self, t):
        return (self.x, self.core, lax.div(t, 4), lax.rem(t, 4))

    def copy(self, t):
        return pltpu.make_async_remote_copy(
            self.in_ref.at[t], self.out_ref.at[self.me], self.send.at[t], self.recv.at[self.me],
            device_id=self.where(t), device_id_type=MESH)

    def arrival(self, t):
        return pltpu.make_async_remote_copy(
            self.out_ref.at[t], self.out_ref.at[t], self.send.at[t], self.recv.at[t],
            device_id=self.where(t), device_id_type=MESH)

    def own(self):
        return pltpu.make_async_copy(self.in_ref.at[self.me], self.out_ref.at[self.me], self.local)

    def greet(self):
        barrier = pltpu.get_barrier_semaphore()
        for t in self.others:
            pl.semaphore_signal(barrier, inc=1, device_id=self.where(t), device_id_type=MESH)
        twin = (self.x, 1 - self.core, lax.div(self.me, 4), lax.rem(self.me, 4))
        pl.semaphore_signal(barrier, inc=1, device_id=twin, device_id_type=MESH)
        pl.semaphore_wait(barrier, 16)

    def start(self):
        if self.to_heads:
            for t in self.others:
                pl.when(t < HEADS)(lambda t=t: self.copy(t).start())
            pl.when(self.me < HEADS)(lambda: self.own().start())
        else:
            @pl.when(self.me < HEADS)
            def _():
                for t in self.others:
                    self.copy(t).start()
                self.own().start()

    def wait(self):
        if self.to_heads:
            @pl.when(self.me < HEADS)
            def _():
                for t in self.others:
                    self.arrival(t).wait_recv()
                self.own().wait()
        else:
            for t in self.others:
                pl.when(t < HEADS)(lambda t=t: self.arrival(t).wait_recv())

            @pl.when(self.me < HEADS)
            def _():
                for t in self.others:
                    self.copy(t).wait_send()
                self.own().wait()

    def wait_send(self):
        for t in self.others:
            pl.when(t < HEADS)(lambda t=t: self.copy(t).wait_send())


NT = (((1,), (1,)), ((), ()))


def product(a, b, dims=(((1,), (0,)), ((), ()))):
    return lax.dot_general(a, b, dims, preferred_element_type=jnp.float32)


def head_kernel(in_ref, out_ref, k, v, kt, vt, scores, dk, dv):
    blocks = 2048 // TILE
    per = TILE // 128

    def rows(which, i):
        return jnp.concatenate([in_ref[i * per + p, which] for p in range(per)], 0)

    @pl.loop(0, blocks)
    def _(i):
        at = pl.ds(pl.multiple_of(i * TILE, TILE), TILE)
        key = rows(0, i)[:, 64:]
        value = rows(1, i)[:, :64]
        k[at, :] = key
        v[at, :] = value
        kt[:, at] = key.T
        vt[:, at] = value.T
        dk[at, :] = jnp.zeros((TILE, 64), jnp.float32)
        dv[at, :] = jnp.zeros((TILE, 64), jnp.float32)

    @pl.loop(0, blocks)
    def _(i):
        query = rows(0, i)[:, :64] * jnp.bfloat16(0.125)
        grad = rows(1, i)[:, 64:]

        def tile(j):
            return pl.ds(pl.multiple_of(j * KEYS, KEYS), KEYS)

        def put(j, s):
            for n in range(TILE // 128):
                scores[pl.ds(pl.multiple_of(j * KEYS, KEYS) + n * 2048, KEYS), :] = s[:, 128 * n:128 * (n + 1)]

        def get(j):
            return jnp.concatenate(
                [scores[pl.ds(pl.multiple_of(j * KEYS, KEYS) + n * 2048, KEYS), :] for n in range(TILE // 128)], 1)

        last = lax.div(i * TILE, KEYS)

        def first(j, top):
            s = product(k[tile(j), :], query, NT)
            put(j, s)
            return jnp.maximum(top, jnp.max(s, 0, keepdims=True))

        top = lax.fori_loop(0, last, first, jnp.full((1, TILE), -1e30, jnp.float32))
        s = product(k[tile(last), :], query, NT)
        keep = lax.broadcasted_iota(jnp.int32, (KEYS, TILE), 0) - lax.broadcasted_iota(jnp.int32, (KEYS, TILE), 1) <= i * TILE - last * KEYS
        s = jnp.where(keep, s, -1e30)
        put(last, s)
        top = jnp.maximum(top, jnp.max(s, 0, keepdims=True))

        def second(j, carry):
            total, out = carry
            e = jnp.exp(get(j) - top)
            put(j, e)
            return total + jnp.sum(e, 0, keepdims=True), out + product(vt[:, tile(j)], e.astype(jnp.bfloat16))

        total, out = lax.fori_loop(0, last + 1, second, (jnp.zeros((1, TILE), jnp.float32), jnp.zeros((64, TILE), jnp.float32)))
        scale = 1.0 / total
        out = out * scale
        inner = jnp.sum(out * grad.astype(jnp.float32).T, 0, keepdims=True)

        def third(j, dq):
            p = get(j) * scale
            dp = product(v[tile(j), :], grad, NT)
            ds = (p * (dp - inner)).astype(jnp.bfloat16)
            dv[tile(j), :] += product(p.astype(jnp.bfloat16), grad)
            dk[tile(j), :] += product(ds, query)
            return dq + product(kt[:, tile(j)], ds)

        dq = lax.fori_loop(0, last + 1, third, jnp.zeros((64, TILE), jnp.float32)) * 0.125
        both = jnp.concatenate([out, dq], 0).T.astype(jnp.bfloat16)
        for p in range(per):
            out_ref[i * per + p, 0] = both[128 * p:128 * (p + 1)]

    @pl.loop(0, blocks)
    def _(i):
        at = pl.ds(pl.multiple_of(i * TILE, TILE), TILE)
        both = jnp.concatenate([dk[at, :], dv[at, :]], 1).astype(jnp.bfloat16)
        for p in range(per):
            out_ref[i * per + p, 1] = both[128 * p:128 * (p + 1)]


HEAD_SCRATCH = [pltpu.VMEM((2048, 64), jnp.bfloat16), pltpu.VMEM((2048, 64), jnp.bfloat16),
                pltpu.VMEM((64, 2048), jnp.bfloat16), pltpu.VMEM((64, 2048), jnp.bfloat16),
                pltpu.VMEM((2048, 64), jnp.float32), pltpu.VMEM((2048, 64), jnp.float32)]


MARGIN = 384
CHUNK = 128


def weight_eighth(number, pairs, vec_ref, flat):
    low, high = number * EIGHTH, (number + 1) * EIGHTH
    at = MARGIN - low
    for (offset, rows, blocks), left, right in pairs:
        first = max(0, (low - offset) // blocks) // 16 * 16
        last = min(rows, -(-(high - offset) // blocks))
        last = -(-last // 16) * 16
        if last <= first:
            continue
        size = min(CHUNK, last - first)
        count = -(-(last - first) // size)
        base = offset + at

        @pl.loop(0, count)
        def _(i, first=first, last=last, size=size, blocks=blocks, base=base, left=left, right=right):
            row = pl.multiple_of(jnp.minimum(first + i * size, last - size), 16)
            lhs = left[pl.ds(row, size), :]

            @pl.loop(0, blocks // 2, unroll=3)
            def _(j):
                rhs = right[:, pl.ds(pl.multiple_of(j * 256, 256), 256)]
                result = product(lhs, rhs)
                start = base + row * blocks + 2 * j
                flat[pl.ds(start, size, stride=blocks), :] = result[:, :128]
                flat[pl.ds(start + 1, size, stride=blocks), :] = result[:, 128:]

    row = 0
    for name in ORDER:
        start, count = VECTORS[name]
        lo, hi = max(start, low), min(start + count, high)
        if lo < hi:
            flat[lo + at:hi + at, :] = vec_ref[row + lo - start:row + hi - start, :]
        row += count
    end = 55374
    if high > end:
        flat[end + at:high + at, :] = jnp.zeros((high - end, 128), jnp.float32)


def halves(size):
    half = size // 32 * 16
    return half, size - half


class Scatter:
    names = ("c0", "c1", "c2", "c3", "b", "a")
    count = 3 * (6 * 8 + 2)

    @staticmethod
    def scratch():
        out = []
        for _, size, _ in PARTS:
            h0, h1 = halves(size)
            for name in Scatter.names:
                lead = () if name == "a" else (4,)
                out += [pltpu.VMEM(lead + (n, 128), jnp.bfloat16) for n in (h0, h1, h1, h0, h0, h1, h0, h1)]
            out += [pltpu.VMEM((4, 4, size, 128), jnp.bfloat16), pltpu.VMEM((4, size, 128), jnp.bfloat16)]
        return out + [pltpu.SemaphoreType.DMA((3, 6, 6)), pltpu.SemaphoreType.DMA((3, 6, 6))]

    def __init__(self, in_ref, out_ref, *scratch):
        self.in_ref, self.out_ref = in_ref, out_ref
        self.send, self.recv = scratch[-2:]
        take = iter(scratch[:-2])
        self.buf, self.rows, self.line = {}, [], []
        for p in range(3):
            for name in self.names:
                self.buf[p, name] = [next(take) for _ in range(8)]
            self.rows.append(next(take))
            self.line.append(next(take))
        self.pos, self.core = place()
        self.copies = {}

    def near(self, axis):
        q = self.pos[axis]
        return [q] + [lax.rem(q + k, 4) for k in (3, 1, 2)]

    def axis(self, p, name):
        return PARTS[p][2]["abc".index(name[0])]

    def source(self, p, name, which, lo, n):
        a, b, c = PARTS[p][2]
        if name == "a":
            return self.line[p].at[self.near(a)[which], pl.ds(lo, n), :]
        if name == "b":
            return self.rows[p].at[which, :, pl.ds(lo, n), :]
        where = [slice(None)] * 3
        where[b] = self.near(b)[int(name[1])]
        where[c] = self.near(c)[which]
        return self.in_ref.at[where[0], where[1], where[2], pl.ds(PARTS[p][0] + lo, n), :]

    def push(self, p, name, number, src, by):
        n = self.names.index(name)
        copy = pltpu.make_async_remote_copy(
            src, self.buf[p, name][number], self.send.at[p, n, number], self.recv.at[p, n, number],
            device_id=device(moved(self.pos, self.axis(p, name), by), self.core), device_id_type=MESH)
        copy.start()
        self.copies[p, name, number] = copy

    def far(self, p, name):
        h0, h1 = halves(PARTS[p][1])
        self.push(p, name, 0, self.source(p, name, 3, 0, h0), 1)
        self.push(p, name, 1, self.source(p, name, 3, h0, h1), 3)

    def raw_right(self, p, name):
        h0, h1 = halves(PARTS[p][1])
        self.push(p, name, 2, self.source(p, name, 2, h0, h1), 1)

    def raw_left(self, p, name):
        h0, h1 = halves(PARTS[p][1])
        self.push(p, name, 3, self.source(p, name, 1, 0, h0), 3)

    def begin(self, p, name):
        self.far(p, name)
        self.raw_right(p, name)
        self.raw_left(p, name)

    def add(self, name, mine, others, put):
        def one(*at):
            total = mine[at + (slice(None), slice(None))].astype(jnp.float32)
            for other in others:
                total = total + other[at + (slice(None), slice(None))].astype(jnp.float32)
            put(at, total)

        if name == "a":
            one()
        else:
            pl.loop(0, 4)(lambda i: one(i))

    def onward(self, p, name):
        h0, h1 = halves(PARTS[p][1])
        b = self.buf[p, name]

        def to(ref):
            def put(at, total):
                ref[at + (slice(None), slice(None))] = total.astype(jnp.bfloat16)
            return put

        self.copies[p, name, 0].wait_recv()
        self.add(name, self.source(p, name, 2, 0, h0), [b[0]], to(b[6]))
        self.push(p, name, 4, b[6], 1)
        self.copies[p, name, 1].wait_recv()
        self.add(name, self.source(p, name, 1, h0, h1), [b[1]], to(b[7]))
        self.push(p, name, 5, b[7], 3)

    def end(self, p, name):
        start, size, _ = PARTS[p]
        h0, h1 = halves(size)
        b = self.buf[p, name]
        for number in (3, 2, 4, 5):
            self.copies[p, name, number].wait_recv()
        for lo, n, others in ((0, h0, [b[3], b[4]]), (h0, h1, [b[2], b[5]])):
            def put(at, total, lo=lo, n=n):
                if name == "a":
                    self.out_ref[start + lo:start + lo + n, :] = total
                elif name == "b":
                    self.line[p][at + (pl.ds(lo, n), slice(None))] = total.astype(jnp.bfloat16)
                else:
                    self.rows[p][(int(name[1]),) + at + (pl.ds(lo, n), slice(None))] = total.astype(jnp.bfloat16)
            self.add(name, self.source(p, name, 0, lo, n), others, put)

    def run(self):
        parts = range(3)

        def each(step, name):
            for p in parts:
                step(p, name)

        each(self.begin, "c3")
        each(self.begin, "c1")
        each(self.onward, "c3")
        each(self.begin, "c2")
        each(self.onward, "c1")
        each(self.end, "c3")
        each(self.far, "b")
        each(self.begin, "c0")
        each(self.onward, "c2")
        each(self.end, "c1")
        each(self.raw_left, "b")
        each(self.onward, "c0")
        each(self.end, "c2")
        each(self.raw_right, "b")
        each(self.onward, "b")
        for p in parts:
            self.end(p, "c0")
            self.end(p, "b")
            self.begin(p, "a")
        each(self.onward, "a")
        each(self.end, "a")
        for copy in self.copies.values():
            copy.wait_send()


EPS = 1e-05
ORDER = ("ln1_gain", "ln1_shift", "ln2_gain", "ln2_shift", "b_qkv", "b_out", "b_up", "b_down")


def widen(g_ref, flat, step):
    @pl.loop(0, 16)
    def _(k):
        base = (step * 16 + k) * 433
        flat[pl.ds(base, 440), :] = g_ref[k, 0:440, :].astype(jnp.float32)


def unpack_matrix(flat, first, where, out, size=64):
    offset, rows, blocks = where
    start = offset - first * EIGHTH

    @pl.loop(0, rows // size)
    def _(i):
        for j in range(blocks):
            piece = flat[pl.ds(start + j + i * (size * blocks), size, stride=blocks), :]
            out[pl.ds(pl.multiple_of(i * size, size), size), 128 * j:128 * (j + 1)] = piece.astype(jnp.bfloat16)


def as_row(ref, start, count):
    return jnp.concatenate([ref[start + n:start + n + 1, :] for n in range(count)], 1)


def to_rows(ref, start, row):
    for n in range(row.shape[1] // 128):
        ref[start + n:start + n + 1, :] = row[:, 128 * n:128 * (n + 1)]


def normalized(values):
    center = jnp.mean(values, -1, keepdims=True)
    centered = values - center
    factor = lax.rsqrt(jnp.mean(centered * centered, -1, keepdims=True) + EPS)
    return centered * factor, factor


def turn(x, tables, sign):
    return x * tables[0] + (pltpu.roll(x, 120, 1) * tables[1] + pltpu.roll(x, 8, 1) * tables[2]) * sign


def first_kernel(g_ref, tokens_ref, grad_ref, tables_ref, w_qkv, w_out, blocks_ref, h1t_ref, h2_ref, h2t_ref, vec_ref, flat, wide):
    step = pl.program_id(0)
    widen(g_ref, flat, step)

    @pl.when(step == 1)
    def _():
        unpack_matrix(flat, 0, W_QKV, w_qkv)

    @pl.when(step == 2)
    def _():
        unpack_matrix(flat, 0, W_OUT, w_out)
        vec_ref[0:24, :] = flat[0:24, :]
        start = VECTORS["b_out"][0]
        vec_ref[24:30, :] = flat[start:start + 6, :]
        normal, _ = normalized(tokens_ref[...].astype(jnp.float32))
        h1 = (normal * as_row(flat, 0, 6) + as_row(flat, 6, 6)).astype(jnp.bfloat16)
        h2 = (normal * as_row(flat, 12, 6) + as_row(flat, 18, 6)).astype(jnp.bfloat16)
        h1t_ref[...] = h1.T
        h2_ref[...] = h2
        h2t_ref[...] = h2.T
        for n in range(9):
            start = VECTORS["b_qkv"][0] + 2 * n
            wide[:, 256 * n:256 * (n + 1)] = product(h1, w_qkv[:, 256 * n:256 * (n + 1)]) + as_row(flat, start, 2)
        low = lax.broadcasted_iota(jnp.int32, (128, 128), 1) < 64
        for m in range(6):
            q, k, v = (wide[:, 768 * p + 128 * m:768 * p + 128 * (m + 1)] for p in range(3))
            q = turn(q, tables_ref, 1.0)
            k = turn(k, tables_ref, 1.0)
            a = product(grad_ref[...], w_out[128 * m:128 * (m + 1), :], NT)
            swap = lambda t: pltpu.roll(t, 64, 1)
            blocks_ref[2 * m, 0] = jnp.where(low, q, swap(k)).astype(jnp.bfloat16)
            blocks_ref[2 * m + 1, 0] = jnp.where(low, swap(q), k).astype(jnp.bfloat16)
            blocks_ref[2 * m, 1] = jnp.where(low, v, swap(a)).astype(jnp.bfloat16)
            blocks_ref[2 * m + 1, 1] = jnp.where(low, swap(v), a).astype(jnp.bfloat16)


def const(*shape):
    return pl.BlockSpec(shape, lambda e: (0,) * len(shape))


def first_part(gathered, tokens, grad, tables):
    bf = lambda *s: jax.ShapeDtypeStruct(s, jnp.bfloat16)
    outs = [bf(768, 2304), bf(768, 768), bf(HEADS, 2, 128, 128), bf(768, 128), bf(128, 768), bf(768, 128),
            jax.ShapeDtypeStruct((32, 128), jnp.float32)]
    return pl.pallas_call(
        first_kernel,
        grid=(3,),
        out_shape=outs,
        in_specs=[pl.BlockSpec((16, 448, 128), lambda e: (e, 0, 0)), const(128, 768), const(128, 768), const(3, 128, 128)],
        out_specs=[const(*o.shape) for o in outs],
        scratch_shapes=[pltpu.VMEM((3 * EIGHTH + 16, 128), jnp.float32), pltpu.VMEM((128, 2304), jnp.float32)],
        compiler_params=pltpu.CompilerParams(vmem_limit_bytes=VMEM_LIMIT),
    )(gathered, tokens, grad, tables)


def gelu_pair(u):
    inside = 0.5 * (1.0 + lax.erf(u * 0.7071067811865476))
    return u * inside, inside + u * jnp.exp(-0.5 * u * u) * 0.3989422804014327


class Twin:
    def __init__(self, send, recv):
        self.send, self.recv, self.copies = send, recv, []
        self.pos, self.core = place()

    def push(self, src, dst):
        number = len(self.copies)
        copy = pltpu.make_async_remote_copy(src, dst, self.send.at[number], self.recv.at[number],
                                            device_id=device(self.pos, 1 - self.core), device_id_type=MESH)
        copy.start()
        self.copies.append(copy)
        return copy

    def wait_send(self):
        for copy in self.copies:
            copy.wait_send()


def middle_kernel(g_ref, h2_ref, grad_ref, h2t_ref, blocks_ref,
                  mlp_ref, dh2_ref, bias_ref, up_ref, halves_ref, back_ref,
                  gbuf, flat, w_up, w_down, act, slope, act_pair, h2_pair, g_pair, dup_pair, vec, vec2,
                  heads_in, heads_out, *rest):
    head_scratch, rest = rest[:6], rest[6:]
    there = Exchange(True, blocks_ref, heads_in, *rest[0:3])
    home = Exchange(False, heads_out, back_ref, *rest[3:6])
    twin = Twin(*rest[6:8])
    load, store = rest[8:10]
    core = lax.axis_index("dp_1")
    loads = [pltpu.make_async_copy(g_ref.at[pl.ds(32 + 16 * e, 16)], gbuf.at[pl.ds(16 * (e % 3), 16)], load.at[e]) for e in range(6)]
    for copy in loads[:3]:
        copy.start()
    there.greet()
    there.start()
    h2_pair[:, :128] = h2t_ref[...]
    g_pair[:128, :] = grad_ref[...]
    h2_copy = twin.push(h2_pair.at[:, pl.ds(0, 128)], h2_pair.at[:, pl.ds(128, 128)])
    g_copy = twin.push(g_pair.at[pl.ds(0, 128), :], g_pair.at[pl.ds(128, 128), :])

    def widen(eighth, at):
        @pl.loop(0, 16)
        def _(k):
            flat[pl.ds((at * 16 + k) * 433, 440), :] = gbuf[(eighth - 2) % 3 * 16 + k, 0:440, :].astype(jnp.float32)

    for e in range(4):
        loads[e].wait()
        widen(2 + e, e)
        if e < 3:
            loads[3 + e].start()
    unpack_matrix(flat, 2, W_UP, w_up)
    start = VECTORS["b_up"][0] - 2 * EIGHTH
    for n in range(12):
        at = slice(256 * n, 256 * (n + 1))
        up = product(h2_ref[...], w_up[:, at]) + as_row(flat, start + 2 * n, 2)
        value, slope[:, at] = gelu_pair(up)
        value = value.astype(jnp.bfloat16)
        act[:, at] = value
        act_pair[at, :128] = value.T
    act_copy = twin.push(act_pair.at[:, pl.ds(0, 128)], act_pair.at[:, pl.ds(128, 128)])
    for e in range(3):
        if e:
            loads[3 + e].wait()
        widen(5 + e, e)
    unpack_matrix(flat, 5, W_DOWN, w_down, 128)
    start = VECTORS["b_down"][0] - 5 * EIGHTH
    for n in range(12):
        at = slice(256 * n, 256 * (n + 1))
        dup = (product(grad_ref[...], w_down[at, :], NT) * slope[:, at]).astype(jnp.bfloat16)
        dup_pair[:128, at] = dup
        to_rows(vec, 48 + 2 * n, jnp.sum(dup.astype(jnp.float32), 0, keepdims=True))
    dup_copy = twin.push(dup_pair.at[pl.ds(0, 128), :], dup_pair.at[pl.ds(128, 128), :])
    bias_ref[...] = vec[48:72, :]
    shift = jnp.sum(grad_ref[...].astype(jnp.float32), 0, keepdims=True)
    to_rows(vec, 72, shift)
    vec[78:80, :] = jnp.zeros((2, 128), jnp.float32)
    vec_copy = twin.push(vec.at[pl.ds(48, 32), :], vec2)
    for n in range(3):
        at = slice(256 * n, 256 * (n + 1))
        mlp_ref[:, at] = product(act[...], w_down[:, at]) + as_row(flat, start + 2 * n, 2)
        dh2_ref[:, at] = product(dup_pair[:128, :], w_up[at, :], NT)
    there.wait()
    head_kernel(heads_in, heads_out, *head_scratch[:4], flat, *head_scratch[4:])
    home.start()
    for copy in (h2_copy, g_copy, act_copy, dup_copy, vec_copy):
        copy.wait_recv()
    vec_copy.wait_send()
    vec[48:80, :] = vec[48:80, :] + vec2[...]
    stores = []
    for t in (1, 2, 3):
        for c in range(2):
            if t > 1 or c == 1:
                pl.when(core == c)(
                    lambda number=2 * t + c: weight_eighth(number, ((W_UP, h2_pair, dup_pair), (W_DOWN, act_pair, g_pair)), vec, flat))

        @pl.loop(0, 16)
        def _(k):
            gbuf[16 * (t - 1) + k] = flat[pl.ds(MARGIN + 433 * k, 448), :].astype(jnp.bfloat16)

        copy = pltpu.make_async_copy(gbuf.at[pl.ds(16 * (t - 1), 16)], halves_ref.at[t - 1], store.at[t - 1])
        copy.start()
        stores.append(copy)

    @pl.when(core == 0)
    def _():
        @pl.loop(0, 12)
        def _(j):
            result = product(h2_pair[:96, :], dup_pair[:, pl.ds(pl.multiple_of(j * 256, 256), 256)])
            up_ref[pl.ds(2 * j, 96, stride=24), :] = result[:, :128]
            up_ref[pl.ds(2 * j + 1, 96, stride=24), :] = result[:, 128:]

    home.wait()
    there.wait_send()
    for copy in (h2_copy, g_copy, act_copy, dup_copy):
        copy.wait_send()
    for copy in stores:
        copy.wait()


def middle_part(gathered, h2, grad, h2t, blocks):
    f32 = lambda *s: jax.ShapeDtypeStruct(s, jnp.float32)
    bf = lambda *s: jax.ShapeDtypeStruct(s, jnp.bfloat16)
    vm = lambda *s: pltpu.VMEM(s, jnp.bfloat16)
    vf = lambda *s: pltpu.VMEM(s, jnp.float32)
    anywhere = pl.BlockSpec(memory_space=pl.ANY)
    outs = [f32(128, 768), f32(128, 768), f32(24, 128), f32(2304, 128)]
    dma = pltpu.SemaphoreType.DMA
    return pl.pallas_call(
        middle_kernel,
        grid=(1,),
        out_shape=outs + [bf(3, 16, 448, 128), bf(HEADS, 2, 128, 128)],
        in_specs=[anywhere, const(128, 768), const(128, 768), const(768, 128), anywhere],
        out_specs=[const(*o.shape) for o in outs] + [anywhere, anywhere],
        scratch_shapes=[vm(48, 448, 128), vf(4 * EIGHTH + 16, 128), vm(768, 3072), vm(3072, 768), vm(128, 3072),
                        vf(128, 3072), vm(3072, 256), vm(768, 256), vm(256, 768), vm(256, 3072), vf(80, 128), vf(32, 128),
                        vm(16, 2, 128, 128), vm(16, 2, 128, 128)]
        + HEAD_SCRATCH + Exchange.scratch + Exchange.scratch + [dma((5,)), dma((5,)), dma((6,)), dma((3,))],
        compiler_params=pltpu.CompilerParams(collective_id=2, has_side_effects=True, vmem_limit_bytes=VMEM_LIMIT),
    )(gathered, h2, grad, h2t, blocks)


def last_kernel(back_ref, tokens_ref, grad_ref, tables_ref, w_qkv, w_out, mlp_ref, dh2_ref, bias_ref, in_vec, h1t_ref,
                up_ref, halves_ref, layer_ref, input_ref, own_ref,
                sums, flat, h1_pair, att_pair, dqkv_pair, g_pair, vec, vec2, twin_send, twin_recv, load, *scratch):
    later = pltpu.make_async_copy(halves_ref, sums.at[pl.ds(1, 3)], load)
    later.start()
    scatter = Scatter(sums, own_ref, *scratch)
    greet(scatter.pos, scatter.core)
    twin = Twin(twin_send, twin_recv)
    h1_pair[:, :128] = h1t_ref[...]
    g_pair[:128, :] = grad_ref[...]
    lanes = lambda pair: twin.push(pair.at[:, pl.ds(0, 128)], pair.at[:, pl.ds(128, 128)])
    rows = lambda pair: twin.push(pair.at[pl.ds(0, 128), :], pair.at[pl.ds(128, 128), :])
    lanes(h1_pair)
    rows(g_pair)
    low = lax.broadcasted_iota(jnp.int32, (128, 128), 1) < 64
    swap = lambda t: pltpu.roll(t, 64, 1)
    f32 = lambda t: t.astype(jnp.float32)
    attended = []
    for m in range(6):
        a, b = f32(back_ref[2 * m, 0]), f32(back_ref[2 * m + 1, 0])
        c, d = f32(back_ref[2 * m, 1]), f32(back_ref[2 * m + 1, 1])
        attended.append(jnp.where(low, a, swap(b)).astype(jnp.bfloat16))
        dq = turn(jnp.where(low, swap(a), b), tables_ref, -1.0)
        dk = turn(jnp.where(low, c, swap(d)), tables_ref, -1.0)
        dv = jnp.where(low, swap(c), d)
        for p, part in enumerate((dq, dk, dv)):
            dqkv_pair[:128, 768 * p + 128 * m:768 * p + 128 * (m + 1)] = part.astype(jnp.bfloat16)
    rows(dqkv_pair)
    attended = jnp.concatenate(attended, 1)
    att_pair[:, :128] = attended.T
    lanes(att_pair)
    tokens = f32(tokens_ref[...])
    grad = f32(grad_ref[...])
    normal, factor = normalized(tokens)
    total = grad
    row = 0
    for gain_at, dh in ((0, product(dqkv_pair[:128, :], w_qkv[...], NT)), (12, dh2_ref[...])):
        to_rows(vec, row, jnp.sum(dh * normal, 0, keepdims=True))
        to_rows(vec, row + 6, jnp.sum(dh, 0, keepdims=True))
        row += 12
        scaled = dh * as_row(in_vec, gain_at, 6)
        inner = scaled - jnp.mean(scaled, -1, keepdims=True) - normal * jnp.mean(scaled * normal, -1, keepdims=True)
        total = total + factor * inner
    input_ref[...] = total
    to_rows(vec, 24, jnp.sum(f32(dqkv_pair[:128, :]), 0, keepdims=True))
    shift = jnp.sum(grad, 0, keepdims=True)
    to_rows(vec, 42, shift)
    vec[48:72, :] = bias_ref[...]
    to_rows(vec, 72, shift)
    vec[78:80, :] = jnp.zeros((2, 128), jnp.float32)
    twin.push(vec, vec2)
    layer_ref[...] = (tokens + (product(attended, w_out[...]) + as_row(in_vec, 24, 6)) + mlp_ref[...]).astype(jnp.bfloat16)
    for copy in twin.copies:
        copy.wait_recv()
    twin.copies[-1].wait_send()
    vec[...] = vec[...] + vec2[...]
    pairs = ((W_QKV, h1_pair, dqkv_pair), (W_OUT, att_pair, g_pair))

    def keep(t):
        for z in range(4):
            @pl.loop(0, 4)
            def _(y):
                sums[t, z, y] = flat[pl.ds(MARGIN + 433 * (4 * z + y), 448), :].astype(jnp.bfloat16)

    for c in range(2):
        pl.when(scatter.core == c)(lambda c=c: weight_eighth(c, pairs, vec, flat))
    keep(0)
    later.wait()

    @pl.when(scatter.core == 0)
    def _():
        weight_eighth(2, pairs, vec, flat)
        at = W_UP[0] - 2 * EIGHTH + MARGIN
        flat[at:at + 2304, :] = up_ref[...]
        keep(1)

    scatter.run()
    for copy in twin.copies[:-1]:
        copy.wait_send()


def last_part(*args):
    halves = args[-1].reshape(3, 4, 4, 448, 128)
    bf = lambda *s: jax.ShapeDtypeStruct(s, jnp.bfloat16)
    f32 = lambda *s: jax.ShapeDtypeStruct(s, jnp.float32)
    vm = lambda *s: pltpu.VMEM(s, jnp.bfloat16)
    vf = lambda *s: pltpu.VMEM(s, jnp.float32)
    dma = pltpu.SemaphoreType.DMA
    outs = [bf(128, 768), f32(128, 768), f32(448, 128)]
    return pl.pallas_call(
        last_kernel,
        grid=(1,),
        out_shape=outs,
        in_specs=[const(*a.shape) for a in args[:-1]] + [pl.BlockSpec(memory_space=pl.ANY)],
        out_specs=[const(*o.shape) for o in outs],
        scratch_shapes=[vm(4, 4, 4, 448, 128), vf(EIGHTH + 2 * MARGIN, 128), vm(768, 256), vm(768, 256), vm(256, 2304),
                        vm(256, 768), vf(80, 128), vf(80, 128), dma((5,)), dma((5,)), dma] + Scatter.scratch(),
        compiler_params=pltpu.CompilerParams(collective_id=1, has_side_effects=True, vmem_limit_bytes=VMEM_LIMIT),
    )(*args[:-1], halves)


def rotary_tables(positions):
    lane = jnp.arange(128) % 64
    freq = jnp.tile(10000.0 ** (-jnp.arange(8).astype(jnp.float32) * 2.0 / 16), 16)
    angles = positions.astype(jnp.float32)[:, None] * freq[None, :]
    cosine, sine = jnp.cos(angles), jnp.sin(angles)
    return jnp.stack([jnp.where(lane < 16, cosine, 1.0), jnp.where(lane < 8, -sine, 0.0),
                      jnp.where((lane >= 8) & (lane < 16), sine, 0.0)])


def body(tokens, params, out_grad):
    piece = tokens.shape[1]
    x, grad = tokens[0], out_grad[0]
    own = jnp.pad(params.reshape(433, 128), ((0, ROWS - 433), (0, 0)))
    gathered = gather(own).reshape(128, ROWS, 128)
    tables = rotary_tables(lax.axis_index(SEQ) * piece + jnp.arange(piece))
    w_qkv, w_out, blocks, h1t, h2, h2t, in_vec = first_part(gathered, x, grad, tables)
    mlp, dh2, bias, up_rows, halves_sum, back = middle_part(gathered, h2, grad, h2t, blocks)
    layer_out, input_grad, own_sum = last_part(
        back, x, grad, tables, w_qkv, w_out, mlp, dh2, bias, in_vec, h1t, up_rows, halves_sum
    )
    param_grad = own_sum[:433].reshape(-1)
    return layer_out[None], input_grad[None], param_grad


def solution(mesh):
    finer = Mesh(mesh.devices.reshape(4, 2, 4, 4), DP_SEQ)
    in_specs = (P(DP, SEQ, None), P(DP_SEQ), P(DP, SEQ, None))
    out_specs = (P(DP, SEQ, None), P(DP, SEQ, None), P(DP_SEQ))
    return jax.shard_map(body, mesh=finer, in_specs=in_specs, out_specs=out_specs, check_vma=False)
```

time: 192 us -> 165 us (0.86)
  Pallas kernels: 175 us -> 157 us
  other arithmetic: 4.67 us -> 1.03 us
  starting transfers between devices: 2.28 us -> 0 us
    pallas_call x6 -> x2, Pallas kernels: 121 us -> 102 us  [the longest x1 53.3 us: last_part(): pl.pallas_call(last_kernel, grid=(1,), out_shape=outs, in_specs=[const(*a...]
    add x2 -> x0, other arithmetic: 2.8 us -> none  [the longest x1 1.41 us: body(): late_vec = late_vec + twin(late_vec)]
    ppermute x9 -> x0, starting transfers between devices: 2.28 us -> none  [twin(): return lax.ppermute(array, 'dp_1', [(0, 1), (1, 0)])]
  transfers between devices with their start and end apart: 9 -> 0, of which waited for: 1 -> 0; matrix products, arithmetic and copies ran while one was open for 2% -> 0% of each run, Pallas kernels for 9% -> 0%
where the time goes in v3:
time: 165 us
  Pallas kernels  157 us (95%)
  local copies, waits for them, and re-layouts  6.67 us (4%)
    pallas_call x1, Pallas kernels, last_part(): pl.pallas_call(last_kernel, grid=(1,), out_shape=outs, in_specs=[const(*a...  53.3 us
    pallas_call x1, Pallas kernels, middle_part(): pl.pallas_call(middle_kernel, grid=(1,), out_shape=outs + [bf(3, 16, 448,...  48.7 us
    pallas_call x1, Pallas kernels, gather(): pl.pallas_call(gather_kernel, out_shape=jax.ShapeDtypeStruct((4, 2, 4, 4,...  46.5 us
    pallas_call x1, Pallas kernels, first_part(): pl.pallas_call(first_kernel, grid=(3,), out_shape=outs, in_specs=[pl.Bloc...  8.08 us
    unnamed x2, local copies, waits for them, and re-layouts  3.38 us

profile of v3, /device:TPU:0, one launch (start us, length us, event | category | flops | bytes accessed | tf_op | source)
XLA Modules:
  0.0 165.0 jit_solution(358901468058878226)
XLA Ops:
  0.7 0.1 mul.41
  0.8 1.6 pad.4.refs_0_
  2.3 0.3 fusion.3
  2.7 0.7 pad_maximum_fusion.tables_ref
  3.4 46.5 %shard_map.58 = bf16[4,2,4,4,448,128]{5,4,3,2,1,0:T(8,128)(2,1)} custom-call(bf16[448,128]{1,0:T(8,128)(2,1)} %pad.4.refs_0_), custom_call_target="tpu_custom_call" | custom-call | tf_op jit(solution)/shard_map/pallas_call | solution.py:197
  49.9 8.1 %shard_map.59 = (bf16[768,2304]{1,0:T(8,128)(2,1)}, bf16[768,768]{1,0:T(8,128)(2,1)}, bf16[12,2,128,128]{3,2,1,0:T(8,128)(2,1)}, bf16[768,128]{1,0:T(8,128)(2,1)...) custom-call(bf16[128,448,128]{2,1,0:T(8,128)(2,1)} %bitcast.9, ...), custom_call_target="tpu_custom_call" | custom-call | tf_op jit(solution)/shard_map/pallas_call | solution.py:663
  58.0 48.7 %shard_map.60 = (f32[128,768]{1,0:T(8,128)}, f32[128,768]{1,0:T(8,128)}, f32[24,128]{1,0:T(8,128)}, f32[2304,128]{1,0:T(8,128)}, bf16[3,16,448,128]{3,2,1,0:T(8,128)(2,1)}, /*index=5*/bf16[12,2,128,128]{3,2,1,0:T(8,128)(2,1)}) custom-call(bf16[128,448,128]{2,1,0:T(8,128)(2,1)} %bitcast.10, bf16[128,768]{1,0:T(8,128)(2,1)} %get-tuple-element.19.h2_ref, ...), custom_call_target="tpu_custom_call" | custom-call | tf_op jit(solution)/shard_map/pallas_call | solution.py:804
  106.7 53.3 %shard_map.61 = (bf16[128,768]{1,0:T(8,128)(2,1)}, f32[128,768]{1,0:T(8,128)}, f32[448,128]{1,0:T(8,128)}) custom-call(bf16[12,2,128,128]{3,2,1,0:T(8,128)(2,1)} %get-tuple-element.22.back_ref, bf16[128,768]{1,0:T(8,128)(2,1)} %bitcast.16, bf16[128,768]{1,0:T(8,128)(2,1)} %bitcast.14, f32[3,128,128]{2,1,0:T(8,128)} %pad_maximum_fusion.tables_ref, ...), custom_call_target="tpu_custom_call" | custom-call | tf_op jit(solution)/shard_map/pallas_call | solution.py:907
  160.0 1.6 slice_bitcast_fusion
  161.6 1.6 copy.8
  163.2 1.8 %copy.9 = f32[1,128,768]{2,1,0:T(8,128)} copy(f32[1,128,768]{2,1,0:T(8,128)} %bitcast.17) | data formatting | bytes 786432
  (5 shorter events, 0.0 us)

commit v4 on v3

--- a/solution.py
+++ b/solution.py
@@ -33,7 +33,7 @@
 
 def greet(pos, core, sibling=True):
     barrier = pltpu.get_barrier_semaphore()
-    others = [device(moved(pos, a, by), core) for a in range(3) for by in (1, 3)]
+    others = [device(moved(pos, a, by), core) for a in range(3) for by in (1, 2, 3)]
     if sibling:
         others.append(device(pos, 1 - core))
     for other in others:
@@ -92,22 +92,27 @@
         src = self.own_ref.at[pl.ds(start, size), :] if ring in ("a", "b0") else None
         self.push(part, ring, 0, 0, 1, start, size, src)
         self.push(part, ring, 1, 0, 3, start, size, src)
+        if ring == "a":
+            self.push(part, ring, 2, 0, 2, start, size, src)
 
     def onward(self, part, ring, left=None, right=None):
         start, size, _ = PARTS[part]
         half = size // 32 * 16
         self.copies[part, ring, 0].wait_recv()
-        self.push(part, ring, 2, 1, 1, start, half)
+        if ring != "a":
+            self.push(part, ring, 2, 1, 1, start, half)
         if left:
             left()
         self.copies[part, ring, 1].wait_recv()
-        self.push(part, ring, 3, 2, 3, start + half, size - half)
+        if ring != "a":
+            self.push(part, ring, 3, 2, 3, start + half, size - half)
         if right:
             right()
 
     def end(self, part, ring):
         self.copies[part, ring, 2].wait_recv()
-        self.copies[part, ring, 3].wait_recv()
+        if ring != "a":
+            self.copies[part, ring, 3].wait_recv()
 
     def sibling(self, part, where, src=None):
         start, size, _ = PARTS[part]
@@ -189,19 +194,23 @@
                 copy.wait_recv()
 
 
-def gather_kernel(*refs):
-    Gather(*refs).run()
-
-
-def gather(own):
+def gather_kernel(params_ref, out_ref, own_ref, *sems):
+    own_ref[0:432, :] = params_ref[0:432, :]
+    own_ref[432:448, :] = jnp.zeros((16, 128), jnp.bfloat16)
+    own_ref[432:433, :] = params_ref[432:433, :]
+    Gather(own_ref, out_ref, *sems).run()
+
+
+def gather(params):
     return pl.pallas_call(
         gather_kernel,
+        grid=(1,),
         out_shape=jax.ShapeDtypeStruct((4, 2, 4, 4, ROWS, 128), jnp.bfloat16),
-        in_specs=[pl.BlockSpec(memory_space=pl.ANY)],
+        in_specs=[pl.BlockSpec((433, 128), lambda e: (0, 0))],
         out_specs=pl.BlockSpec(memory_space=pl.ANY),
-        scratch_shapes=Gather.scratch,
+        scratch_shapes=[pltpu.VMEM((ROWS, 128), jnp.bfloat16)] + Gather.scratch,
         compiler_params=pltpu.CompilerParams(collective_id=0, has_side_effects=True),
-    )(own)
+    )(params)
 
 
 EIGHTH = 16 * 433
@@ -214,8 +223,8 @@
 
 
 HEADS = 12
-TILE = 1024
-KEYS = 1024
+TILE = 512
+KEYS = 512
 
 
 class Exchange:
@@ -293,6 +302,12 @@
     return lax.dot_general(a, b, dims, preferred_element_type=jnp.float32)
 
 
+def unrolled(low, high, body, carry):
+    for j in range(low, high):
+        carry = body(j, carry)
+    return carry
+
+
 def head_kernel(in_ref, out_ref, k, v, kt, vt, scores, dk, dv):
     blocks = 2048 // TILE
     per = TILE // 128
@@ -312,30 +327,29 @@
         dk[at, :] = jnp.zeros((TILE, 64), jnp.float32)
         dv[at, :] = jnp.zeros((TILE, 64), jnp.float32)
 
-    @pl.loop(0, blocks)
-    def _(i):
+    def block(i):
         query = rows(0, i)[:, :64] * jnp.bfloat16(0.125)
         grad = rows(1, i)[:, 64:]
 
         def tile(j):
-            return pl.ds(pl.multiple_of(j * KEYS, KEYS), KEYS)
+            return pl.ds(j * KEYS, KEYS)
 
         def put(j, s):
             for n in range(TILE // 128):
-                scores[pl.ds(pl.multiple_of(j * KEYS, KEYS) + n * 2048, KEYS), :] = s[:, 128 * n:128 * (n + 1)]
+                scores[pl.ds(j * KEYS + n * 2048, KEYS), :] = s[:, 128 * n:128 * (n + 1)]
 
         def get(j):
             return jnp.concatenate(
-                [scores[pl.ds(pl.multiple_of(j * KEYS, KEYS) + n * 2048, KEYS), :] for n in range(TILE // 128)], 1)
-
-        last = lax.div(i * TILE, KEYS)
+                [scores[pl.ds(j * KEYS + n * 2048, KEYS), :] for n in range(TILE // 128)], 1)
+
+        last = i * TILE // KEYS
 
         def first(j, top):
             s = product(k[tile(j), :], query, NT)
             put(j, s)
             return jnp.maximum(top, jnp.max(s, 0, keepdims=True))
 
-        top = lax.fori_loop(0, last, first, jnp.full((1, TILE), -1e30, jnp.float32))
+        top = unrolled(0, last, first, jnp.full((1, TILE), -1e30, jnp.float32))
         s = product(k[tile(last), :], query, NT)
         keep = lax.broadcasted_iota(jnp.int32, (KEYS, TILE), 0) - lax.broadcasted_iota(jnp.int32, (KEYS, TILE), 1) <= i * TILE - last * KEYS
         s = jnp.where(keep, s, -1e30)
@@ -348,7 +362,7 @@
             put(j, e)
             return total + jnp.sum(e, 0, keepdims=True), out + product(vt[:, tile(j)], e.astype(jnp.bfloat16))
 
-        total, out = lax.fori_loop(0, last + 1, second, (jnp.zeros((1, TILE), jnp.float32), jnp.zeros((64, TILE), jnp.float32)))
+        total, out = unrolled(0, last + 1, second, (jnp.zeros((1, TILE), jnp.float32), jnp.zeros((64, TILE), jnp.float32)))
         scale = 1.0 / total
         out = out * scale
         inner = jnp.sum(out * grad.astype(jnp.float32).T, 0, keepdims=True)
@@ -361,10 +375,13 @@
             dk[tile(j), :] += product(ds, query)
             return dq + product(kt[:, tile(j)], ds)
 
-        dq = lax.fori_loop(0, last + 1, third, jnp.zeros((64, TILE), jnp.float32)) * 0.125
+        dq = unrolled(0, last + 1, third, jnp.zeros((64, TILE), jnp.float32)) * 0.125
         both = jnp.concatenate([out, dq], 0).T.astype(jnp.bfloat16)
         for p in range(per):
             out_ref[i * per + p, 0] = both[128 * p:128 * (p + 1)]
+
+    for i in range(blocks):
+        block(i)
 
     @pl.loop(0, blocks)
     def _(i):
@@ -428,18 +445,18 @@
 
 class Scatter:
     names = ("c0", "c1", "c2", "c3", "b", "a")
-    count = 3 * (6 * 8 + 2)
-
     @staticmethod
     def scratch():
         out = []
         for _, size, _ in PARTS:
             h0, h1 = halves(size)
             for name in Scatter.names:
-                lead = () if name == "a" else (4,)
-                out += [pltpu.VMEM(lead + (n, 128), jnp.bfloat16) for n in (h0, h1, h1, h0, h0, h1, h0, h1)]
+                if name == "a":
+                    out += [pltpu.VMEM((size, 128), jnp.bfloat16)] * 3
+                else:
+                    out += [pltpu.VMEM((4, n, 128), jnp.bfloat16) for n in (h0, h1, h1, h0, h0, h1, h0, h1)]
             out += [pltpu.VMEM((4, 4, size, 128), jnp.bfloat16), pltpu.VMEM((4, size, 128), jnp.bfloat16)]
-        return out + [pltpu.SemaphoreType.DMA((3, 6, 6)), pltpu.SemaphoreType.DMA((3, 6, 6))]
+        return out + [pltpu.SemaphoreType.DMA((3, 6, 10)), pltpu.SemaphoreType.DMA((3, 6, 10))]
 
     def __init__(self, in_ref, out_ref, *scratch):
         self.in_ref, self.out_ref = in_ref, out_ref
@@ -448,7 +465,7 @@
         self.buf, self.rows, self.line = {}, [], []
         for p in range(3):
             for name in self.names:
-                self.buf[p, name] = [next(take) for _ in range(8)]
+                self.buf[p, name] = [next(take) for _ in range(3 if name == "a" else 8)]
             self.rows.append(next(take))
             self.line.append(next(take))
         self.pos, self.core = place()
@@ -472,31 +489,59 @@
         where[c] = self.near(c)[which]
         return self.in_ref.at[where[0], where[1], where[2], pl.ds(PARTS[p][0] + lo, n), :]
 
-    def push(self, p, name, number, src, by):
+    def push(self, p, name, number, src, by, when=None, dst=None, sem=None):
         n = self.names.index(name)
+        sem = number if sem is None else sem
         copy = pltpu.make_async_remote_copy(
-            src, self.buf[p, name][number], self.send.at[p, n, number], self.recv.at[p, n, number],
+            src, self.buf[p, name][number] if dst is None else dst, self.send.at[p, n, sem], self.recv.at[p, n, sem],
             device_id=device(moved(self.pos, self.axis(p, name), by), self.core), device_id_type=MESH)
-        copy.start()
-        self.copies[p, name, number] = copy
-
-    def far(self, p, name):
+        if when is None:
+            copy.start()
+        else:
+            pl.when(when)(copy.start)
+        self.copies.setdefault((p, name, number), []).append(copy)
+
+    def arrived(self, p, name, number):
+        for copy in self.copies[p, name, number]:
+            copy.wait_recv()
+
+    def sends(self, p):
         h0, h1 = halves(PARTS[p][1])
-        self.push(p, name, 0, self.source(p, name, 3, 0, h0), 1)
-        self.push(p, name, 1, self.source(p, name, 3, h0, h1), 3)
-
-    def raw_right(self, p, name):
-        h0, h1 = halves(PARTS[p][1])
-        self.push(p, name, 2, self.source(p, name, 2, h0, h1), 1)
-
-    def raw_left(self, p, name):
-        h0, h1 = halves(PARTS[p][1])
-        self.push(p, name, 3, self.source(p, name, 1, 0, h0), 3)
-
-    def begin(self, p, name):
-        self.far(p, name)
-        self.raw_right(p, name)
-        self.raw_left(p, name)
+        return ((0, 3, 0, h0, 1), (1, 3, h0, h1, 3), (2, 2, h0, h1, 1), (3, 1, 0, h0, 3))
+
+    def begin(self, p, name, numbers=(0, 1, 2, 3)):
+        for number, which, lo, n, by in self.sends(p):
+            if number in numbers:
+                self.push(p, name, number, self.source(p, name, which, lo, n), by)
+
+    def ahead(self, name, later):
+        for p in range(3):
+            a, b, c = PARTS[p][2]
+            for number, which, lo, n, by in self.sends(p):
+                src = self.source(p, name, which, lo, n)
+                if a == 0:
+                    part = pl.ds(2 if later else 0, 2)
+                    self.push(p, name, number, src.at[part], by, None, self.buf[p, name][number].at[part],
+                              number if later else 6 + number)
+                    continue
+                x = self.near(0)[int(name[1])] if b == 0 else self.near(0)[which]
+                if later:
+                    self.push(p, name, number, src, by, x >= 2)
+                else:
+                    pl.when(x < 2)(self.copies[p, name, number][0].start)
+
+    def direct(self, p):
+        for number, (which, by) in enumerate(((1, 3), (2, 1), (3, 2))):
+            self.push(p, "a", number, self.source(p, "a", which, 0, PARTS[p][1]), by)
+
+    def total(self, p):
+        start, size, _ = PARTS[p]
+        for number in range(3):
+            self.arrived(p, "a", number)
+        value = self.source(p, "a", 0, 0, size)[...].astype(jnp.float32)
+        for other in self.buf[p, "a"]:
+            value = value + other[...].astype(jnp.float32)
+        self.out_ref[start:start + size, :] = value
 
     def add(self, name, mine, others, put):
         def one(*at):
@@ -505,10 +550,7 @@
                 total = total + other[at + (slice(None), slice(None))].astype(jnp.float32)
             put(at, total)
 
-        if name == "a":
-            one()
-        else:
-            pl.loop(0, 4)(lambda i: one(i))
+        pl.loop(0, 4)(lambda i: one(i))
 
     def onward(self, p, name):
         h0, h1 = halves(PARTS[p][1])
@@ -519,59 +561,61 @@
                 ref[at + (slice(None), slice(None))] = total.astype(jnp.bfloat16)
             return put
 
-        self.copies[p, name, 0].wait_recv()
+        self.arrived(p, name, 0)
         self.add(name, self.source(p, name, 2, 0, h0), [b[0]], to(b[6]))
         self.push(p, name, 4, b[6], 1)
-        self.copies[p, name, 1].wait_recv()
+        self.arrived(p, name, 1)
         self.add(name, self.source(p, name, 1, h0, h1), [b[1]], to(b[7]))
         self.push(p, name, 5, b[7], 3)
 
     def end(self, p, name):
-        start, size, _ = PARTS[p]
-        h0, h1 = halves(size)
+        h0, h1 = halves(PARTS[p][1])
         b = self.buf[p, name]
         for number in (3, 2, 4, 5):
-            self.copies[p, name, number].wait_recv()
+            self.arrived(p, name, number)
         for lo, n, others in ((0, h0, [b[3], b[4]]), (h0, h1, [b[2], b[5]])):
             def put(at, total, lo=lo, n=n):
-                if name == "a":
-                    self.out_ref[start + lo:start + lo + n, :] = total
-                elif name == "b":
+                if name == "b":
                     self.line[p][at + (pl.ds(lo, n), slice(None))] = total.astype(jnp.bfloat16)
                 else:
                     self.rows[p][(int(name[1]),) + at + (pl.ds(lo, n), slice(None))] = total.astype(jnp.bfloat16)
             self.add(name, self.source(p, name, 0, lo, n), others, put)
 
+    def before(self):
+        for name in ("c3", "c1", "c2", "c0"):
+            self.ahead(name, True)
+
     def run(self):
         parts = range(3)
 
-        def each(step, name):
+        def each(step, name, *more):
             for p in parts:
-                step(p, name)
-
-        each(self.begin, "c3")
-        each(self.begin, "c1")
+                step(p, name, *more)
+
+        self.ahead("c3", False)
+        self.ahead("c1", False)
         each(self.onward, "c3")
-        each(self.begin, "c2")
+        self.ahead("c2", False)
         each(self.onward, "c1")
         each(self.end, "c3")
-        each(self.far, "b")
-        each(self.begin, "c0")
+        each(self.begin, "b", (0, 1))
+        self.ahead("c0", False)
         each(self.onward, "c2")
         each(self.end, "c1")
-        each(self.raw_left, "b")
+        each(self.begin, "b", (3,))
         each(self.onward, "c0")
         each(self.end, "c2")
-        each(self.raw_right, "b")
+        each(self.begin, "b", (2,))
         each(self.onward, "b")
         for p in parts:
             self.end(p, "c0")
             self.end(p, "b")
-            self.begin(p, "a")
-        each(self.onward, "a")
-        each(self.end, "a")
-        for copy in self.copies.values():
-            copy.wait_send()
+            self.direct(p)
+        for p in parts:
+            self.total(p)
+        for copies in self.copies.values():
+            for copy in copies:
+                copy.wait_send()
 
 
 EPS = 1e-05
@@ -829,6 +873,8 @@
     rows = lambda pair: twin.push(pair.at[pl.ds(0, 128), :], pair.at[pl.ds(128, 128), :])
     lanes(h1_pair)
     rows(g_pair)
+    later.wait()
+    scatter.before()
     low = lax.broadcasted_iota(jnp.int32, (128, 128), 1) < 64
     swap = lambda t: pltpu.roll(t, 64, 1)
     f32 = lambda t: t.astype(jnp.float32)
@@ -882,7 +928,6 @@
     for c in range(2):
         pl.when(scatter.core == c)(lambda c=c: weight_eighth(c, pairs, vec, flat))
     keep(0)
-    later.wait()
 
     @pl.when(scatter.core == 0)
     def _():
@@ -916,6 +961,23 @@
     )(*args[:-1], halves)
 
 
+def finish_kernel(layer_in, input_in, own_in, layer_ref, input_ref, own_ref):
+    layer_ref[...] = layer_in[...]
+    input_ref[...] = input_in[...]
+    own_ref[...] = own_in[:433, :]
+
+
+def finish(*args):
+    shapes = [(128, 768), (128, 768), (433, 128)]
+    return pl.pallas_call(
+        finish_kernel,
+        grid=(1,),
+        out_shape=[jax.ShapeDtypeStruct(s, a.dtype) for s, a in zip(shapes, args)],
+        in_specs=[const(*a.shape) for a in args],
+        out_specs=[const(*s) for s in shapes],
+    )(*args)
+
+
 def rotary_tables(positions):
     lane = jnp.arange(128) % 64
     freq = jnp.tile(10000.0 ** (-jnp.arange(8).astype(jnp.float32) * 2.0 / 16), 16)
@@ -928,15 +990,13 @@
 def body(tokens, params, out_grad):
     piece = tokens.shape[1]
     x, grad = tokens[0], out_grad[0]
-    own = jnp.pad(params.reshape(433, 128), ((0, ROWS - 433), (0, 0)))
-    gathered = gather(own).reshape(128, ROWS, 128)
+    gathered = gather(params.reshape(433, 128)).reshape(128, ROWS, 128)
     tables = rotary_tables(lax.axis_index(SEQ) * piece + jnp.arange(piece))
     w_qkv, w_out, blocks, h1t, h2, h2t, in_vec = first_part(gathered, x, grad, tables)
     mlp, dh2, bias, up_rows, halves_sum, back = middle_part(gathered, h2, grad, h2t, blocks)
-    layer_out, input_grad, own_sum = last_part(
-        back, x, grad, tables, w_qkv, w_out, mlp, dh2, bias, in_vec, h1t, up_rows, halves_sum
-    )
-    param_grad = own_sum[:433].reshape(-1)
+    results = last_part(back, x, grad, tables, w_qkv, w_out, mlp, dh2, bias, in_vec, h1t, up_rows, halves_sum)
+    layer_out, input_grad, own_sum = finish(*results)
+    param_grad = own_sum.reshape(-1)
     return layer_out[None], input_grad[None], param_grad
 
 

time: 165 us -> 154 us (0.933)
  local copies, waits for them, and re-layouts: 6.67 us -> 0.09 us
  Pallas kernels: 157 us -> 152 us
    unnamed x2 -> x0, local copies, waits for them, and re-layouts: 3.38 us -> none
    pallas_call x1, Pallas kernels: 48.7 us -> 45.8 us  [middle_part(): pl.pallas_call(middle_kernel, grid=(1,), out_shape=outs + [bf(3, 16, 448,...]
    pallas_call x1, Pallas kernels: 53.3 us -> 51.1 us  [last_part(): pl.pallas_call(last_kernel, grid=(1,), out_shape=outs, in_specs=[const(*a...]
    pallas_call x1 -> x2, Pallas kernels: 46.5 us -> 47.3 us  [the longest x1 45.3 us: gather(): pl.pallas_call(gather_kernel, grid=(1,), out_shape=jax.ShapeDtypeStruct((...]
where the time goes in v4:
time: 154 us
  Pallas kernels  152 us (99%)
    pallas_call x1, Pallas kernels, last_part(): pl.pallas_call(last_kernel, grid=(1,), out_shape=outs, in_specs=[const(*a...  51.1 us
    pallas_call x1, Pallas kernels, middle_part(): pl.pallas_call(middle_kernel, grid=(1,), out_shape=outs + [bf(3, 16, 448,...  45.8 us
    pallas_call x1, Pallas kernels, gather(): pl.pallas_call(gather_kernel, grid=(1,), out_shape=jax.ShapeDtypeStruct((...  45.3 us
    pallas_call x1, Pallas kernels, first_part(): pl.pallas_call(first_kernel, grid=(3,), out_shape=outs, in_specs=[pl.Bloc...  7.9 us

profile of v4, /device:TPU:0, one launch (start us, length us, event | category | flops | bytes accessed | tf_op | source)
XLA Modules:
  0.0 154.0 jit_solution(13926790690124692602)
XLA Ops:
  0.7 0.1 mul.41
  0.8 0.3 fusion.3
  1.1 0.7 pad_maximum_fusion.tables_ref
  1.8 45.3 %shard_map.58 = bf16[4,2,4,4,448,128]{5,4,3,2,1,0:T(8,128)(2,1)} custom-call(bf16[433,128]{1,0:T(8,128)(2,1)} %bitcast.16), custom_call_target="tpu_custom_call" | custom-call | tf_op jit(solution)/shard_map/pallas_call | solution.py:205
  47.1 7.9 %shard_map.59 = (bf16[768,2304]{1,0:T(8,128)(2,1)}, bf16[768,768]{1,0:T(8,128)(2,1)}, bf16[12,2,128,128]{3,2,1,0:T(8,128)(2,1)}, bf16[768,128]{1,0:T(8,128)(2,1)...) custom-call(bf16[128,448,128]{2,1,0:T(8,128)(2,1)} %bitcast.8, ...), custom_call_target="tpu_custom_call" | custom-call | tf_op jit(solution)/shard_map/pallas_call | solution.py:707
  55.0 45.8 %shard_map.60 = (f32[128,768]{1,0:T(8,128)}, f32[128,768]{1,0:T(8,128)}, f32[24,128]{1,0:T(8,128)}, f32[2304,128]{1,0:T(8,128)}, bf16[3,16,448,128]{3,2,1,0:T(8,128)(2,1)}, /*index=5*/bf16[12,2,128,128]{3,2,1,0:T(8,128)(2,1)}) custom-call(bf16[128,448,128]{2,1,0:T(8,128)(2,1)} %bitcast.9, bf16[128,768]{1,0:T(8,128)(2,1)} %get-tuple-element.22.h2_ref, ...), custom_call_target="tpu_custom_call" | custom-call | tf_op jit(solution)/shard_map/pallas_call | solution.py:848
  100.8 51.1 %shard_map.61 = (bf16[128,768]{1,0:T(8,128)(2,1)}, f32[128,768]{1,0:T(8,128)}, f32[448,128]{1,0:T(8,128)}) custom-call(bf16[12,2,128,128]{3,2,1,0:T(8,128)(2,1)} %get-tuple-element.25.back_ref, bf16[128,768]{1,0:T(8,128)(2,1)} %bitcast.15, bf16[128,768]{1,0:T(8,128)(2,1)} %bitcast.13, f32[3,128,128]{2,1,0:T(8,128)} %pad_maximum_fusion.tables_ref, ...), custom_call_target="tpu_custom_call" | custom-call | tf_op jit(solution)/shard_map/pallas_call | solution.py:952
  151.9 2.1 %shard_map.62 = (bf16[128,768]{1,0:T(8,128)(2,1)}, f32[128,768]{1,0:T(8,128)}, f32[433,128]{1,0:T(8,128)}) custom-call(bf16[128,768]{1,0:T(8,128)(2,1)} %get-tuple-element.35.layer_in, f32[128,768]{1,0:T(8,128)} %get-tuple-element.36.input_in, f32[448,128]{1,0:T(8,128)} %get-tuple-element.37.own_in), custom_call_target="tpu_custom_call" | custom-call | tf_op jit(solution)/shard_map/pallas_call | solution.py:972
  (5 shorter events, 0.0 us)

commit v5 on v4

--- a/solution.py
+++ b/solution.py
@@ -253,13 +253,15 @@
     def own(self):
         return pltpu.make_async_copy(self.in_ref.at[self.me], self.out_ref.at[self.me], self.local)
 
-    def greet(self):
+    def hello(self):
         barrier = pltpu.get_barrier_semaphore()
         for t in self.others:
             pl.semaphore_signal(barrier, inc=1, device_id=self.where(t), device_id_type=MESH)
         twin = (self.x, 1 - self.core, lax.div(self.me, 4), lax.rem(self.me, 4))
         pl.semaphore_signal(barrier, inc=1, device_id=twin, device_id_type=MESH)
-        pl.semaphore_wait(barrier, 16)
+
+    def meet(self):
+        pl.semaphore_wait(pltpu.get_barrier_semaphore(), 16)
 
     def start(self):
         if self.to_heads:
@@ -585,7 +587,7 @@
         for name in ("c3", "c1", "c2", "c0"):
             self.ahead(name, True)
 
-    def run(self):
+    def run(self, meanwhile):
         parts = range(3)
 
         def each(step, name, *more):
@@ -594,6 +596,7 @@
 
         self.ahead("c3", False)
         self.ahead("c1", False)
+        meanwhile()
         each(self.onward, "c3")
         self.ahead("c2", False)
         each(self.onward, "c1")
@@ -660,59 +663,8 @@
     return x * tables[0] + (pltpu.roll(x, 120, 1) * tables[1] + pltpu.roll(x, 8, 1) * tables[2]) * sign
 
 
-def first_kernel(g_ref, tokens_ref, grad_ref, tables_ref, w_qkv, w_out, blocks_ref, h1t_ref, h2_ref, h2t_ref, vec_ref, flat, wide):
-    step = pl.program_id(0)
-    widen(g_ref, flat, step)
-
-    @pl.when(step == 1)
-    def _():
-        unpack_matrix(flat, 0, W_QKV, w_qkv)
-
-    @pl.when(step == 2)
-    def _():
-        unpack_matrix(flat, 0, W_OUT, w_out)
-        vec_ref[0:24, :] = flat[0:24, :]
-        start = VECTORS["b_out"][0]
-        vec_ref[24:30, :] = flat[start:start + 6, :]
-        normal, _ = normalized(tokens_ref[...].astype(jnp.float32))
-        h1 = (normal * as_row(flat, 0, 6) + as_row(flat, 6, 6)).astype(jnp.bfloat16)
-        h2 = (normal * as_row(flat, 12, 6) + as_row(flat, 18, 6)).astype(jnp.bfloat16)
-        h1t_ref[...] = h1.T
-        h2_ref[...] = h2
-        h2t_ref[...] = h2.T
-        for n in range(9):
-            start = VECTORS["b_qkv"][0] + 2 * n
-            wide[:, 256 * n:256 * (n + 1)] = product(h1, w_qkv[:, 256 * n:256 * (n + 1)]) + as_row(flat, start, 2)
-        low = lax.broadcasted_iota(jnp.int32, (128, 128), 1) < 64
-        for m in range(6):
-            q, k, v = (wide[:, 768 * p + 128 * m:768 * p + 128 * (m + 1)] for p in range(3))
-            q = turn(q, tables_ref, 1.0)
-            k = turn(k, tables_ref, 1.0)
-            a = product(grad_ref[...], w_out[128 * m:128 * (m + 1), :], NT)
-            swap = lambda t: pltpu.roll(t, 64, 1)
-            blocks_ref[2 * m, 0] = jnp.where(low, q, swap(k)).astype(jnp.bfloat16)
-            blocks_ref[2 * m + 1, 0] = jnp.where(low, swap(q), k).astype(jnp.bfloat16)
-            blocks_ref[2 * m, 1] = jnp.where(low, v, swap(a)).astype(jnp.bfloat16)
-            blocks_ref[2 * m + 1, 1] = jnp.where(low, swap(v), a).astype(jnp.bfloat16)
-
-
 def const(*shape):
     return pl.BlockSpec(shape, lambda e: (0,) * len(shape))
-
-
-def first_part(gathered, tokens, grad, tables):
-    bf = lambda *s: jax.ShapeDtypeStruct(s, jnp.bfloat16)
-    outs = [bf(768, 2304), bf(768, 768), bf(HEADS, 2, 128, 128), bf(768, 128), bf(128, 768), bf(768, 128),
-            jax.ShapeDtypeStruct((32, 128), jnp.float32)]
-    return pl.pallas_call(
-        first_kernel,
-        grid=(3,),
-        out_shape=outs,
-        in_specs=[pl.BlockSpec((16, 448, 128), lambda e: (e, 0, 0)), const(128, 768), const(128, 768), const(3, 128, 128)],
-        out_specs=[const(*o.shape) for o in outs],
-        scratch_shapes=[pltpu.VMEM((3 * EIGHTH + 16, 128), jnp.float32), pltpu.VMEM((128, 2304), jnp.float32)],
-        compiler_params=pltpu.CompilerParams(vmem_limit_bytes=VMEM_LIMIT),
-    )(gathered, tokens, grad, tables)
 
 
 def gelu_pair(u):
@@ -738,41 +690,82 @@
             copy.wait_send()
 
 
-def middle_kernel(g_ref, h2_ref, grad_ref, h2t_ref, blocks_ref,
-                  mlp_ref, dh2_ref, bias_ref, up_ref, halves_ref, back_ref,
+def middle_kernel(g_ref, tokens_ref, grad_ref, tables_ref,
+                  mlp_ref, dh2_ref, bias_ref, h1t_ref, vec_ref, up_ref, halves_ref, back_ref, w_qkv_ref, w_out_ref,
                   gbuf, flat, w_up, w_down, act, slope, act_pair, h2_pair, g_pair, dup_pair, vec, vec2,
-                  heads_in, heads_out, *rest):
+                  heads_in, heads_out, w_qkv, w_out, wide, blocks, *rest):
     head_scratch, rest = rest[:6], rest[6:]
-    there = Exchange(True, blocks_ref, heads_in, *rest[0:3])
+    there = Exchange(True, blocks, heads_in, *rest[0:3])
     home = Exchange(False, heads_out, back_ref, *rest[3:6])
     twin = Twin(*rest[6:8])
     load, store = rest[8:10]
     core = lax.axis_index("dp_1")
-    loads = [pltpu.make_async_copy(g_ref.at[pl.ds(32 + 16 * e, 16)], gbuf.at[pl.ds(16 * (e % 3), 16)], load.at[e]) for e in range(6)]
+    there.hello()
+    loads = [pltpu.make_async_copy(g_ref.at[pl.ds(16 * e, 16)], gbuf.at[pl.ds(e % 3 * 16, 16)], load.at[e]) for e in range(8)]
     for copy in loads[:3]:
         copy.start()
-    there.greet()
+    stores = []
+
+    def keep(src, dst):
+        copy = pltpu.make_async_copy(src, dst, store.at[len(stores)])
+        copy.start()
+        stores.append(copy)
+
+    def widen(eighth, at):
+        @pl.loop(0, 16)
+        def _(k):
+            flat[pl.ds((at * 16 + k) * 433, 440), :] = gbuf[eighth % 3 * 16 + k, 0:440, :].astype(jnp.float32)
+
+    for e in range(2):
+        loads[e].wait()
+        widen(e, e)
+        loads[3 + e].start()
+    unpack_matrix(flat, 0, W_QKV, w_qkv)
+    keep(w_qkv, w_qkv_ref)
+    loads[2].wait()
+    widen(2, 2)
+    unpack_matrix(flat, 0, W_OUT, w_out)
+    keep(w_out, w_out_ref)
+    vec_ref[0:24, :] = flat[0:24, :]
+    start = VECTORS["b_out"][0]
+    vec_ref[24:30, :] = flat[start:start + 6, :]
+    normal, _ = normalized(tokens_ref[...].astype(jnp.float32))
+    h1 = (normal * as_row(flat, 0, 6) + as_row(flat, 6, 6)).astype(jnp.bfloat16)
+    h2 = (normal * as_row(flat, 12, 6) + as_row(flat, 18, 6)).astype(jnp.bfloat16)
+    h1t_ref[...] = h1.T
+    for n in range(9):
+        start = VECTORS["b_qkv"][0] + 2 * n
+        qkv = product(h1, w_qkv[:, 256 * n:256 * (n + 1)]) + as_row(flat, start, 2)
+        wide[256 * n:256 * n + 128, :] = qkv[:, :128]
+        wide[256 * n + 128:256 * (n + 1), :] = qkv[:, 128:]
+    low = lax.broadcasted_iota(jnp.int32, (128, 128), 1) < 64
+    swap = lambda t: pltpu.roll(t, 64, 1)
+    for m in range(6):
+        q, k, v = (wide[128 * (6 * p + m):128 * (6 * p + m + 1), :] for p in range(3))
+        q = turn(q, tables_ref, 1.0)
+        k = turn(k, tables_ref, 1.0)
+        a = product(grad_ref[...], w_out[128 * m:128 * (m + 1), :], NT)
+        blocks[2 * m, 0] = jnp.where(low, q, swap(k)).astype(jnp.bfloat16)
+        blocks[2 * m + 1, 0] = jnp.where(low, swap(q), k).astype(jnp.bfloat16)
+        blocks[2 * m, 1] = jnp.where(low, v, swap(a)).astype(jnp.bfloat16)
+        blocks[2 * m + 1, 1] = jnp.where(low, swap(v), a).astype(jnp.bfloat16)
+    there.meet()
     there.start()
-    h2_pair[:, :128] = h2t_ref[...]
+    h2_pair[:, :128] = h2.T
     g_pair[:128, :] = grad_ref[...]
     h2_copy = twin.push(h2_pair.at[:, pl.ds(0, 128)], h2_pair.at[:, pl.ds(128, 128)])
     g_copy = twin.push(g_pair.at[pl.ds(0, 128), :], g_pair.at[pl.ds(128, 128), :])
-
-    def widen(eighth, at):
-        @pl.loop(0, 16)
-        def _(k):
-            flat[pl.ds((at * 16 + k) * 433, 440), :] = gbuf[(eighth - 2) % 3 * 16 + k, 0:440, :].astype(jnp.float32)
-
-    for e in range(4):
-        loads[e].wait()
-        widen(2 + e, e)
-        if e < 3:
+    for e in range(2, 6):
+        if e > 2:
+            loads[e].wait()
+        widen(e, e - 2)
+        if e < 5:
             loads[3 + e].start()
     unpack_matrix(flat, 2, W_UP, w_up)
     start = VECTORS["b_up"][0] - 2 * EIGHTH
     for n in range(12):
         at = slice(256 * n, 256 * (n + 1))
-        up = product(h2_ref[...], w_up[:, at]) + as_row(flat, start + 2 * n, 2)
+        up = product(h2, w_up[:, at]) + as_row(flat, start + 2 * n, 2)
         value, slope[:, at] = gelu_pair(up)
         value = value.astype(jnp.bfloat16)
         act[:, at] = value
@@ -780,7 +773,7 @@
     act_copy = twin.push(act_pair.at[:, pl.ds(0, 128)], act_pair.at[:, pl.ds(128, 128)])
     for e in range(3):
         if e:
-            loads[3 + e].wait()
+            loads[5 + e].wait()
         widen(5 + e, e)
     unpack_matrix(flat, 5, W_DOWN, w_down, 128)
     start = VECTORS["b_down"][0] - 5 * EIGHTH
@@ -806,7 +799,6 @@
         copy.wait_recv()
     vec_copy.wait_send()
     vec[48:80, :] = vec[48:80, :] + vec2[...]
-    stores = []
     for t in (1, 2, 3):
         for c in range(2):
             if t > 1 or c == 1:
@@ -817,17 +809,17 @@
         def _(k):
             gbuf[16 * (t - 1) + k] = flat[pl.ds(MARGIN + 433 * k, 448), :].astype(jnp.bfloat16)
 
-        copy = pltpu.make_async_copy(gbuf.at[pl.ds(16 * (t - 1), 16)], halves_ref.at[t - 1], store.at[t - 1])
-        copy.start()
-        stores.append(copy)
+        keep(gbuf.at[pl.ds(16 * (t - 1), 16)], halves_ref.at[t - 1])
 
     @pl.when(core == 0)
     def _():
         @pl.loop(0, 12)
         def _(j):
             result = product(h2_pair[:96, :], dup_pair[:, pl.ds(pl.multiple_of(j * 256, 256), 256)])
-            up_ref[pl.ds(2 * j, 96, stride=24), :] = result[:, :128]
-            up_ref[pl.ds(2 * j + 1, 96, stride=24), :] = result[:, 128:]
+            wide[pl.ds(2 * j, 96, stride=24), :] = result[:, :128]
+            wide[pl.ds(2 * j + 1, 96, stride=24), :] = result[:, 128:]
+
+    keep(wide, up_ref)
 
     home.wait()
     there.wait_send()
@@ -837,33 +829,37 @@
         copy.wait()
 
 
-def middle_part(gathered, h2, grad, h2t, blocks):
+def middle_part(gathered, tokens, grad, tables):
     f32 = lambda *s: jax.ShapeDtypeStruct(s, jnp.float32)
     bf = lambda *s: jax.ShapeDtypeStruct(s, jnp.bfloat16)
     vm = lambda *s: pltpu.VMEM(s, jnp.bfloat16)
     vf = lambda *s: pltpu.VMEM(s, jnp.float32)
     anywhere = pl.BlockSpec(memory_space=pl.ANY)
-    outs = [f32(128, 768), f32(128, 768), f32(24, 128), f32(2304, 128)]
+    outs = [f32(128, 768), f32(128, 768), f32(24, 128), bf(768, 128), f32(32, 128)]
+    far = [f32(2304, 128), bf(3, 16, 448, 128), bf(HEADS, 2, 128, 128), bf(768, 2304), bf(768, 768)]
     dma = pltpu.SemaphoreType.DMA
     return pl.pallas_call(
         middle_kernel,
         grid=(1,),
-        out_shape=outs + [bf(3, 16, 448, 128), bf(HEADS, 2, 128, 128)],
-        in_specs=[anywhere, const(128, 768), const(128, 768), const(768, 128), anywhere],
-        out_specs=[const(*o.shape) for o in outs] + [anywhere, anywhere],
+        out_shape=outs + far,
+        in_specs=[anywhere, const(128, 768), const(128, 768), const(3, 128, 128)],
+        out_specs=[const(*o.shape) for o in outs] + [anywhere] * len(far),
         scratch_shapes=[vm(48, 448, 128), vf(4 * EIGHTH + 16, 128), vm(768, 3072), vm(3072, 768), vm(128, 3072),
                         vf(128, 3072), vm(3072, 256), vm(768, 256), vm(256, 768), vm(256, 3072), vf(80, 128), vf(32, 128),
-                        vm(16, 2, 128, 128), vm(16, 2, 128, 128)]
-        + HEAD_SCRATCH + Exchange.scratch + Exchange.scratch + [dma((5,)), dma((5,)), dma((6,)), dma((3,))],
+                        vm(16, 2, 128, 128), vm(16, 2, 128, 128), vm(768, 2304), vm(768, 768), vf(2304, 128),
+                        vm(HEADS, 2, 128, 128)]
+        + HEAD_SCRATCH + Exchange.scratch + Exchange.scratch + [dma((5,)), dma((5,)), dma((8,)), dma((6,))],
         compiler_params=pltpu.CompilerParams(collective_id=2, has_side_effects=True, vmem_limit_bytes=VMEM_LIMIT),
-    )(gathered, h2, grad, h2t, blocks)
-
-
-def last_kernel(back_ref, tokens_ref, grad_ref, tables_ref, w_qkv, w_out, mlp_ref, dh2_ref, bias_ref, in_vec, h1t_ref,
-                up_ref, halves_ref, layer_ref, input_ref, own_ref,
-                sums, flat, h1_pair, att_pair, dqkv_pair, g_pair, vec, vec2, twin_send, twin_recv, load, *scratch):
-    later = pltpu.make_async_copy(halves_ref, sums.at[pl.ds(1, 3)], load)
-    later.start()
+    )(gathered, tokens, grad, tables)
+
+
+def last_kernel(back_ref, tokens_ref, grad_ref, tables_ref, mlp_ref, dh2_ref, bias_ref, in_vec, h1t_ref,
+                w_qkv_ref, w_out_ref, up_in, halves_ref, layer_ref, input_ref, own_ref,
+                sums, flat, h1_pair, att_pair, dqkv_pair, g_pair, vec, vec2, w_qkv, w_out, up_ref, twin_send, twin_recv, load, *scratch):
+    pairs = ((halves_ref, sums.at[pl.ds(1, 3)]), (w_qkv_ref, w_qkv), (w_out_ref, w_out), (up_in, up_ref))
+    later, qkv_load, out_load, up_load = (pltpu.make_async_copy(a, b, load.at[n]) for n, (a, b) in enumerate(pairs))
+    for copy in (later, qkv_load, out_load, up_load):
+        copy.start()
     scatter = Scatter(sums, own_ref, *scratch)
     greet(scatter.pos, scatter.core)
     twin = Twin(twin_send, twin_recv)
@@ -895,16 +891,11 @@
     tokens = f32(tokens_ref[...])
     grad = f32(grad_ref[...])
     normal, factor = normalized(tokens)
-    total = grad
-    row = 0
-    for gain_at, dh in ((0, product(dqkv_pair[:128, :], w_qkv[...], NT)), (12, dh2_ref[...])):
-        to_rows(vec, row, jnp.sum(dh * normal, 0, keepdims=True))
-        to_rows(vec, row + 6, jnp.sum(dh, 0, keepdims=True))
-        row += 12
-        scaled = dh * as_row(in_vec, gain_at, 6)
-        inner = scaled - jnp.mean(scaled, -1, keepdims=True) - normal * jnp.mean(scaled * normal, -1, keepdims=True)
-        total = total + factor * inner
-    input_ref[...] = total
+    qkv_load.wait()
+    input_ref[...] = product(dqkv_pair[:128, :], w_qkv[...], NT)
+    for row, dh in ((0, input_ref), (12, dh2_ref)):
+        to_rows(vec, row, jnp.sum(dh[...] * normal, 0, keepdims=True))
+        to_rows(vec, row + 6, jnp.sum(dh[...], 0, keepdims=True))
     to_rows(vec, 24, jnp.sum(f32(dqkv_pair[:128, :]), 0, keepdims=True))
     shift = jnp.sum(grad, 0, keepdims=True)
     to_rows(vec, 42, shift)
@@ -912,7 +903,21 @@
     to_rows(vec, 72, shift)
     vec[78:80, :] = jnp.zeros((2, 128), jnp.float32)
     twin.push(vec, vec2)
-    layer_ref[...] = (tokens + (product(attended, w_out[...]) + as_row(in_vec, 24, 6)) + mlp_ref[...]).astype(jnp.bfloat16)
+    out_load.wait()
+    up_load.wait()
+
+    def results():
+        tokens = f32(tokens_ref[...])
+        branch = lax.dot_general(att_pair[:, :128], w_out[...], (((0,), (0,)), ((), ())), preferred_element_type=jnp.float32)
+        layer_ref[...] = (tokens + (branch + as_row(in_vec, 24, 6)) + mlp_ref[...]).astype(jnp.bfloat16)
+        normal, factor = normalized(tokens)
+        total = f32(grad_ref[...])
+        for gain_at, dh in ((0, input_ref), (12, dh2_ref)):
+            scaled = dh[...] * as_row(in_vec, gain_at, 6)
+            inner = scaled - jnp.mean(scaled, -1, keepdims=True) - normal * jnp.mean(scaled * normal, -1, keepdims=True)
+            total = total + factor * inner
+        input_ref[...] = total
+
     for copy in twin.copies:
         copy.wait_recv()
     twin.copies[-1].wait_send()
@@ -936,7 +941,7 @@
         flat[at:at + 2304, :] = up_ref[...]
         keep(1)
 
-    scatter.run()
+    scatter.run(results)
     for copy in twin.copies[:-1]:
         copy.wait_send()
 
@@ -953,10 +958,11 @@
         last_kernel,
         grid=(1,),
         out_shape=outs,
-        in_specs=[const(*a.shape) for a in args[:-1]] + [pl.BlockSpec(memory_space=pl.ANY)],
+        in_specs=[const(*a.shape) for a in args[:-4]] + [pl.BlockSpec(memory_space=pl.ANY)] * 4,
         out_specs=[const(*o.shape) for o in outs],
         scratch_shapes=[vm(4, 4, 4, 448, 128), vf(EIGHTH + 2 * MARGIN, 128), vm(768, 256), vm(768, 256), vm(256, 2304),
-                        vm(256, 768), vf(80, 128), vf(80, 128), dma((5,)), dma((5,)), dma] + Scatter.scratch(),
+                        vm(256, 768), vf(80, 128), vf(80, 128), vm(768, 2304), vm(768, 768), vf(2304, 128),
+                        dma((5,)), dma((5,)), dma((4,))] + Scatter.scratch(),
         compiler_params=pltpu.CompilerParams(collective_id=1, has_side_effects=True, vmem_limit_bytes=VMEM_LIMIT),
     )(*args[:-1], halves)
 
@@ -992,9 +998,8 @@
     x, grad = tokens[0], out_grad[0]
     gathered = gather(params.reshape(433, 128)).reshape(128, ROWS, 128)
     tables = rotary_tables(lax.axis_index(SEQ) * piece + jnp.arange(piece))
-    w_qkv, w_out, blocks, h1t, h2, h2t, in_vec = first_part(gathered, x, grad, tables)
-    mlp, dh2, bias, up_rows, halves_sum, back = middle_part(gathered, h2, grad, h2t, blocks)
-    results = last_part(back, x, grad, tables, w_qkv, w_out, mlp, dh2, bias, in_vec, h1t, up_rows, halves_sum)
+    mlp, dh2, bias, h1t, in_vec, up_rows, halves_sum, back, w_qkv, w_out = middle_part(gathered, x, grad, tables)
+    results = last_part(back, x, grad, tables, mlp, dh2, bias, in_vec, h1t, w_qkv, w_out, up_rows, halves_sum)
     layer_out, input_grad, own_sum = finish(*results)
     param_grad = own_sum.reshape(-1)
     return layer_out[None], input_grad[None], param_grad

time: 154 us -> 148 us (0.961)
  Pallas kernels: 152 us -> 146 us
    pallas_call x2 -> x1, Pallas kernels: 53.7 us -> 48.1 us  [middle_part(): pl.pallas_call(middle_kernel, grid=(1,), out_shape=outs + far, in_specs=[...]
where the time goes in v5:
time: 148 us
  Pallas kernels  146 us (99%)
    pallas_call x1, Pallas kernels, last_part(): pl.pallas_call(last_kernel, grid=(1,), out_shape=outs, in_specs=[const(*a...  50.6 us
    pallas_call x1, Pallas kernels, middle_part(): pl.pallas_call(middle_kernel, grid=(1,), out_shape=outs + far, in_specs=[...  48.1 us
    pallas_call x1, Pallas kernels, gather(): pl.pallas_call(gather_kernel, grid=(1,), out_shape=jax.ShapeDtypeStruct((...  45.3 us

profile of v5, /device:TPU:0, one launch (start us, length us, event | category | flops | bytes accessed | tf_op | source)
XLA Modules:
  0.0 147.9 jit_solution(2869981403721325924)
XLA Ops:
  0.7 0.1 mul.41
  0.8 0.3 fusion.3
  1.1 0.7 pad_maximum_fusion.tables_ref
  1.8 45.3 %shard_map.58 = bf16[4,2,4,4,448,128]{5,4,3,2,1,0:T(8,128)(2,1)} custom-call(bf16[433,128]{1,0:T(8,128)(2,1)} %bitcast.14), custom_call_target="tpu_custom_call" | custom-call | tf_op jit(solution)/shard_map/pallas_call | solution.py:205
  47.1 48.1 %shard_map.59 = (f32[128,768]{1,0:T(8,128)}, f32[128,768]{1,0:T(8,128)}, f32[24,128]{1,0:T(8,128)}, bf16[768,128]{1,0:T(8,128)(2,1)}, f32[32,128]{1,0:T(8,128)},...) custom-call(bf16[128,448,128]{2,1,0:T(8,128)(2,1)} %bitcast.8, ...), custom_call_target="tpu_custom_call" | custom-call | tf_op jit(solution)/shard_map/pallas_call | solution.py:841
  95.2 50.6 %shard_map.60 = (bf16[128,768]{1,0:T(8,128)(2,1)}, f32[128,768]{1,0:T(8,128)}, f32[448,128]{1,0:T(8,128)}) custom-call(bf16[12,2,128,128]{3,2,1,0:T(8,128)(2,1)} %get-tuple-element.19.back_ref, bf16[128,768]{1,0:T(8,128)(2,1)} %bitcast.11, bf16[128,768]{1,0:T(8,128)(2,1)} %bitcast.13, f32[3,128,128]{2,1,0:T(8,128)} %pad_maximum_fusion.tables_ref, ...), custom_call_target="tpu_custom_call" | custom-call | tf_op jit(solution)/shard_map/pallas_call | solution.py:957
  145.9 2.1 %shard_map.61 = (bf16[128,768]{1,0:T(8,128)(2,1)}, f32[128,768]{1,0:T(8,128)}, f32[433,128]{1,0:T(8,128)}) custom-call(bf16[128,768]{1,0:T(8,128)(2,1)} %get-tuple-element.29.layer_in, f32[128,768]{1,0:T(8,128)} %get-tuple-element.30.input_in, f32[448,128]{1,0:T(8,128)} %get-tuple-element.31.own_in), custom_call_target="tpu_custom_call" | custom-call | tf_op jit(solution)/shard_map/pallas_call | solution.py:978
  (5 shorter events, 0.0 us)

commit v6 on v5

--- a/solution.py
+++ b/solution.py
@@ -31,14 +31,16 @@
     return out
 
 
-def greet(pos, core, sibling=True):
+def hello(pos, core):
     barrier = pltpu.get_barrier_semaphore()
-    others = [device(moved(pos, a, by), core) for a in range(3) for by in (1, 2, 3)]
-    if sibling:
-        others.append(device(pos, 1 - core))
+    others = [device(moved(pos, a, by), core) for a in range(3) for by in (1, 2, 3)] + [device(pos, 1 - core)]
     for other in others:
         pl.semaphore_signal(barrier, inc=1, device_id=other, device_id_type=MESH)
-    pl.semaphore_wait(barrier, len(others))
+    return len(others)
+
+
+def meet(count):
+    pl.semaphore_wait(pltpu.get_barrier_semaphore(), count)
 
 
 class Gather:
@@ -138,7 +140,6 @@
         parts = range(3)
         own = pltpu.make_async_copy(self.own_ref, self.out_ref.at[self.pos[0], self.core, self.pos[1], self.pos[2]], self.local)
         own.start()
-        greet(self.pos, self.core)
         for p in parts:
             self.begin(p, "a")
         for p in parts:
@@ -194,25 +195,6 @@
                 copy.wait_recv()
 
 
-def gather_kernel(params_ref, out_ref, own_ref, *sems):
-    own_ref[0:432, :] = params_ref[0:432, :]
-    own_ref[432:448, :] = jnp.zeros((16, 128), jnp.bfloat16)
-    own_ref[432:433, :] = params_ref[432:433, :]
-    Gather(own_ref, out_ref, *sems).run()
-
-
-def gather(params):
-    return pl.pallas_call(
-        gather_kernel,
-        grid=(1,),
-        out_shape=jax.ShapeDtypeStruct((4, 2, 4, 4, ROWS, 128), jnp.bfloat16),
-        in_specs=[pl.BlockSpec((433, 128), lambda e: (0, 0))],
-        out_specs=pl.BlockSpec(memory_space=pl.ANY),
-        scratch_shapes=[pltpu.VMEM((ROWS, 128), jnp.bfloat16)] + Gather.scratch,
-        compiler_params=pltpu.CompilerParams(collective_id=0, has_side_effects=True),
-    )(params)
-
-
 EIGHTH = 16 * 433
 W_QKV = (24, 768, 18)
 W_OUT = (13866, 768, 6)
@@ -230,8 +212,8 @@
 class Exchange:
     scratch = [pltpu.SemaphoreType.DMA((16,)), pltpu.SemaphoreType.DMA((16,)), pltpu.SemaphoreType.DMA]
 
-    def __init__(self, to_heads, in_ref, out_ref, send, recv, local):
-        self.to_heads, self.in_ref, self.out_ref = to_heads, in_ref, out_ref
+    def __init__(self, in_ref, out_ref, send, recv, local):
+        self.in_ref, self.out_ref = in_ref, out_ref
         self.send, self.recv, self.local = send, recv, local
         self.x, self.core = lax.axis_index("dp_0"), lax.axis_index("dp_1")
         self.me = lax.axis_index("seq_0") * 4 + lax.axis_index("seq_1")
@@ -240,6 +222,11 @@
     def where(self, t):
         return (self.x, self.core, lax.div(t, 4), lax.rem(t, 4))
 
+    def hello(self):
+        barrier = pltpu.get_barrier_semaphore()
+        for t in self.others:
+            pl.semaphore_signal(barrier, inc=1, device_id=self.where(t), device_id_type=MESH)
+
     def copy(self, t):
         return pltpu.make_async_remote_copy(
             self.in_ref.at[t], self.out_ref.at[self.me], self.send.at[t], self.recv.at[self.me],
@@ -253,48 +240,40 @@
     def own(self):
         return pltpu.make_async_copy(self.in_ref.at[self.me], self.out_ref.at[self.me], self.local)
 
-    def hello(self):
-        barrier = pltpu.get_barrier_semaphore()
+
+class ToHeads(Exchange):
+    def start(self):
         for t in self.others:
-            pl.semaphore_signal(barrier, inc=1, device_id=self.where(t), device_id_type=MESH)
-        twin = (self.x, 1 - self.core, lax.div(self.me, 4), lax.rem(self.me, 4))
-        pl.semaphore_signal(barrier, inc=1, device_id=twin, device_id_type=MESH)
-
-    def meet(self):
-        pl.semaphore_wait(pltpu.get_barrier_semaphore(), 16)
-
-    def start(self):
-        if self.to_heads:
+            pl.when(t < HEADS)(lambda t=t: self.copy(t).start())
+        pl.when(self.me < HEADS)(lambda: self.own().start())
+
+    def wait(self):
+        @pl.when(self.me < HEADS)
+        def _():
             for t in self.others:
-                pl.when(t < HEADS)(lambda t=t: self.copy(t).start())
-            pl.when(self.me < HEADS)(lambda: self.own().start())
-        else:
-            @pl.when(self.me < HEADS)
-            def _():
-                for t in self.others:
-                    self.copy(t).start()
-                self.own().start()
-
-    def wait(self):
-        if self.to_heads:
-            @pl.when(self.me < HEADS)
-            def _():
-                for t in self.others:
-                    self.arrival(t).wait_recv()
-                self.own().wait()
-        else:
-            for t in self.others:
-                pl.when(t < HEADS)(lambda t=t: self.arrival(t).wait_recv())
-
-            @pl.when(self.me < HEADS)
-            def _():
-                for t in self.others:
-                    self.copy(t).wait_send()
-                self.own().wait()
+                self.arrival(t).wait_recv()
+            self.own().wait()
 
     def wait_send(self):
         for t in self.others:
             pl.when(t < HEADS)(lambda t=t: self.copy(t).wait_send())
+
+
+class FromHeads(Exchange):
+    def start(self, first=0, last=16):
+        for t in range(first, last):
+            pl.when((self.me < HEADS) & (self.me != t))(lambda t=t: self.copy(jnp.int32(t)).start())
+            pl.when((self.me < HEADS) & (self.me == t))(lambda: self.own().start())
+
+    def wait(self):
+        for t in self.others:
+            pl.when(t < HEADS)(lambda t=t: self.arrival(t).wait_recv())
+
+        @pl.when(self.me < HEADS)
+        def _():
+            for t in self.others:
+                self.copy(t).wait_send()
+            self.own().wait()
 
 
 NT = (((1,), (1,)), ((), ()))
@@ -310,7 +289,7 @@
     return carry
 
 
-def head_kernel(in_ref, out_ref, k, v, kt, vt, scores, dk, dv):
+def head_kernel(ready, in_ref, att_out, key_out, k, v, kt, vt, scores, dk, dv):
     blocks = 2048 // TILE
     per = TILE // 128
 
@@ -380,17 +359,18 @@
         dq = unrolled(0, last + 1, third, jnp.zeros((64, TILE), jnp.float32)) * 0.125
         both = jnp.concatenate([out, dq], 0).T.astype(jnp.bfloat16)
         for p in range(per):
-            out_ref[i * per + p, 0] = both[128 * p:128 * (p + 1)]
+            att_out[i * per + p] = both[128 * p:128 * (p + 1)]
 
     for i in range(blocks):
         block(i)
+        ready(i * per, (i + 1) * per)
 
     @pl.loop(0, blocks)
     def _(i):
         at = pl.ds(pl.multiple_of(i * TILE, TILE), TILE)
         both = jnp.concatenate([dk[at, :], dv[at, :]], 1).astype(jnp.bfloat16)
         for p in range(per):
-            out_ref[i * per + p, 1] = both[128 * p:128 * (p + 1)]
+            key_out[i * per + p] = both[128 * p:128 * (p + 1)]
 
 
 HEAD_SCRATCH = [pltpu.VMEM((2048, 64), jnp.bfloat16), pltpu.VMEM((2048, 64), jnp.bfloat16),
@@ -516,10 +496,12 @@
             if number in numbers:
                 self.push(p, name, number, self.source(p, name, which, lo, n), by)
 
-    def ahead(self, name, later):
+    def ahead(self, name, later, numbers):
         for p in range(3):
             a, b, c = PARTS[p][2]
             for number, which, lo, n, by in self.sends(p):
+                if number not in numbers:
+                    continue
                 src = self.source(p, name, which, lo, n)
                 if a == 0:
                     part = pl.ds(2 if later else 0, 2)
@@ -584,8 +566,9 @@
             self.add(name, self.source(p, name, 0, lo, n), others, put)
 
     def before(self):
-        for name in ("c3", "c1", "c2", "c0"):
-            self.ahead(name, True)
+        for numbers in ((0, 1), (2, 3)):
+            for name in ("c3", "c1", "c2", "c0"):
+                self.ahead(name, True, numbers)
 
     def run(self, meanwhile):
         parts = range(3)
@@ -594,18 +577,20 @@
             for p in parts:
                 step(p, name, *more)
 
-        self.ahead("c3", False)
-        self.ahead("c1", False)
+        for name in ("c3", "c1", "c2", "c0"):
+            self.ahead(name, False, (0, 1))
+        self.ahead("c3", False, (2, 3))
         meanwhile()
         each(self.onward, "c3")
-        self.ahead("c2", False)
+        self.ahead("c1", False, (2, 3))
         each(self.onward, "c1")
         each(self.end, "c3")
         each(self.begin, "b", (0, 1))
-        self.ahead("c0", False)
+        self.ahead("c2", False, (2, 3))
         each(self.onward, "c2")
         each(self.end, "c1")
         each(self.begin, "b", (3,))
+        self.ahead("c0", False, (2, 3))
         each(self.onward, "c0")
         each(self.end, "c2")
         each(self.begin, "b", (2,))
@@ -690,18 +675,26 @@
             copy.wait_send()
 
 
-def middle_kernel(g_ref, tokens_ref, grad_ref, tables_ref,
-                  mlp_ref, dh2_ref, bias_ref, h1t_ref, vec_ref, up_ref, halves_ref, back_ref, w_qkv_ref, w_out_ref,
+def middle_kernel(params_ref, tokens_ref, grad_ref, tables_ref,
+                  mlp_ref, dh2_ref, bias_ref, h1t_ref, vec_ref, up_ref, halves_ref, att_ref, key_ref, w_qkv_ref, w_out_ref, all_ref,
                   gbuf, flat, w_up, w_down, act, slope, act_pair, h2_pair, g_pair, dup_pair, vec, vec2,
-                  heads_in, heads_out, w_qkv, w_out, wide, blocks, *rest):
+                  heads_in, att_out, key_out, w_qkv, w_out, wide, blocks, own, *rest):
     head_scratch, rest = rest[:6], rest[6:]
-    there = Exchange(True, blocks, heads_in, *rest[0:3])
-    home = Exchange(False, heads_out, back_ref, *rest[3:6])
-    twin = Twin(*rest[6:8])
-    load, store = rest[8:10]
+    there = ToHeads(blocks, heads_in, *rest[0:3])
+    home = FromHeads(att_out, att_ref, *rest[3:6])
+    home_keys = FromHeads(key_out, key_ref, *rest[6:9])
+    twin = Twin(*rest[9:11])
+    load, store = rest[11:13]
     core = lax.axis_index("dp_1")
+    gather = Gather(own, all_ref, *rest[13:])
     there.hello()
-    loads = [pltpu.make_async_copy(g_ref.at[pl.ds(16 * e, 16)], gbuf.at[pl.ds(e % 3 * 16, 16)], load.at[e]) for e in range(8)]
+    count = hello(gather.pos, core)
+    own[0:432, :] = params_ref[0:432, :]
+    own[432:448, :] = jnp.zeros((16, 128), jnp.bfloat16)
+    own[432:433, :] = params_ref[432:433, :]
+    meet(count + 15)
+    gather.run()
+    loads = [pltpu.make_async_copy(all_ref.at[e // 2, e % 2], gbuf.at[e % 3], load.at[e]) for e in range(8)]
     for copy in loads[:3]:
         copy.start()
     stores = []
@@ -714,7 +707,7 @@
     def widen(eighth, at):
         @pl.loop(0, 16)
         def _(k):
-            flat[pl.ds((at * 16 + k) * 433, 440), :] = gbuf[eighth % 3 * 16 + k, 0:440, :].astype(jnp.float32)
+            flat[pl.ds((at * 16 + k) * 433, 440), :] = gbuf[eighth % 3, lax.div(k, 4), lax.rem(k, 4), 0:440, :].astype(jnp.float32)
 
     for e in range(2):
         loads[e].wait()
@@ -749,7 +742,6 @@
         blocks[2 * m + 1, 0] = jnp.where(low, swap(q), k).astype(jnp.bfloat16)
         blocks[2 * m, 1] = jnp.where(low, v, swap(a)).astype(jnp.bfloat16)
         blocks[2 * m + 1, 1] = jnp.where(low, swap(v), a).astype(jnp.bfloat16)
-    there.meet()
     there.start()
     h2_pair[:, :128] = h2.T
     g_pair[:128, :] = grad_ref[...]
@@ -793,8 +785,8 @@
         mlp_ref[:, at] = product(act[...], w_down[:, at]) + as_row(flat, start + 2 * n, 2)
         dh2_ref[:, at] = product(dup_pair[:128, :], w_up[at, :], NT)
     there.wait()
-    head_kernel(heads_in, heads_out, *head_scratch[:4], flat, *head_scratch[4:])
-    home.start()
+    head_kernel(home.start, heads_in, att_out, key_out, *head_scratch[:4], flat, *head_scratch[4:])
+    home_keys.start()
     for copy in (h2_copy, g_copy, act_copy, dup_copy, vec_copy):
         copy.wait_recv()
     vec_copy.wait_send()
@@ -807,9 +799,9 @@
 
         @pl.loop(0, 16)
         def _(k):
-            gbuf[16 * (t - 1) + k] = flat[pl.ds(MARGIN + 433 * k, 448), :].astype(jnp.bfloat16)
-
-        keep(gbuf.at[pl.ds(16 * (t - 1), 16)], halves_ref.at[t - 1])
+            gbuf[t - 1, lax.div(k, 4), lax.rem(k, 4)] = flat[pl.ds(MARGIN + 433 * k, 448), :].astype(jnp.bfloat16)
+
+        keep(gbuf.at[t - 1], halves_ref.at[t - 1])
 
     @pl.when(core == 0)
     def _():
@@ -822,6 +814,7 @@
     keep(wide, up_ref)
 
     home.wait()
+    home_keys.wait()
     there.wait_send()
     for copy in (h2_copy, g_copy, act_copy, dup_copy):
         copy.wait_send()
@@ -829,39 +822,39 @@
         copy.wait()
 
 
-def middle_part(gathered, tokens, grad, tables):
+def middle_part(params, tokens, grad, tables):
     f32 = lambda *s: jax.ShapeDtypeStruct(s, jnp.float32)
     bf = lambda *s: jax.ShapeDtypeStruct(s, jnp.bfloat16)
     vm = lambda *s: pltpu.VMEM(s, jnp.bfloat16)
     vf = lambda *s: pltpu.VMEM(s, jnp.float32)
     anywhere = pl.BlockSpec(memory_space=pl.ANY)
     outs = [f32(128, 768), f32(128, 768), f32(24, 128), bf(768, 128), f32(32, 128)]
-    far = [f32(2304, 128), bf(3, 16, 448, 128), bf(HEADS, 2, 128, 128), bf(768, 2304), bf(768, 768)]
+    far = [f32(2304, 128), bf(3, 4, 4, 448, 128), bf(HEADS, 128, 128), bf(HEADS, 128, 128),
+           bf(768, 2304), bf(768, 768), bf(4, 2, 4, 4, 448, 128)]
     dma = pltpu.SemaphoreType.DMA
     return pl.pallas_call(
         middle_kernel,
         grid=(1,),
         out_shape=outs + far,
-        in_specs=[anywhere, const(128, 768), const(128, 768), const(3, 128, 128)],
+        in_specs=[const(433, 128), const(128, 768), const(128, 768), const(3, 128, 128)],
         out_specs=[const(*o.shape) for o in outs] + [anywhere] * len(far),
-        scratch_shapes=[vm(48, 448, 128), vf(4 * EIGHTH + 16, 128), vm(768, 3072), vm(3072, 768), vm(128, 3072),
+        scratch_shapes=[vm(3, 4, 4, 448, 128), vf(4 * EIGHTH + 16, 128), vm(768, 3072), vm(3072, 768), vm(128, 3072),
                         vf(128, 3072), vm(3072, 256), vm(768, 256), vm(256, 768), vm(256, 3072), vf(80, 128), vf(32, 128),
-                        vm(16, 2, 128, 128), vm(16, 2, 128, 128), vm(768, 2304), vm(768, 768), vf(2304, 128),
-                        vm(HEADS, 2, 128, 128)]
-        + HEAD_SCRATCH + Exchange.scratch + Exchange.scratch + [dma((5,)), dma((5,)), dma((8,)), dma((6,))],
+                        vm(16, 2, 128, 128), vm(16, 128, 128), vm(16, 128, 128), vm(768, 2304), vm(768, 768), vf(2304, 128),
+                        vm(HEADS, 2, 128, 128), vm(448, 128)]
+        + HEAD_SCRATCH + Exchange.scratch * 3 + [dma((5,)), dma((5,)), dma((8,)), dma((6,))] + Gather.scratch,
         compiler_params=pltpu.CompilerParams(collective_id=2, has_side_effects=True, vmem_limit_bytes=VMEM_LIMIT),
-    )(gathered, tokens, grad, tables)
-
-
-def last_kernel(back_ref, tokens_ref, grad_ref, tables_ref, mlp_ref, dh2_ref, bias_ref, in_vec, h1t_ref,
+    )(params, tokens, grad, tables)
+
+
+def last_kernel(att_ref, key_ref, tokens_ref, grad_ref, tables_ref, mlp_ref, dh2_ref, bias_ref, in_vec, h1t_ref,
                 w_qkv_ref, w_out_ref, up_in, halves_ref, layer_ref, input_ref, own_ref,
                 sums, flat, h1_pair, att_pair, dqkv_pair, g_pair, vec, vec2, w_qkv, w_out, up_ref, twin_send, twin_recv, load, *scratch):
     pairs = ((halves_ref, sums.at[pl.ds(1, 3)]), (w_qkv_ref, w_qkv), (w_out_ref, w_out), (up_in, up_ref))
     later, qkv_load, out_load, up_load = (pltpu.make_async_copy(a, b, load.at[n]) for n, (a, b) in enumerate(pairs))
-    for copy in (later, qkv_load, out_load, up_load):
-        copy.start()
+    later.start()
     scatter = Scatter(sums, own_ref, *scratch)
-    greet(scatter.pos, scatter.core)
+    meet(hello(scatter.pos, scatter.core))
     twin = Twin(twin_send, twin_recv)
     h1_pair[:, :128] = h1t_ref[...]
     g_pair[:128, :] = grad_ref[...]
@@ -870,14 +863,16 @@
     lanes(h1_pair)
     rows(g_pair)
     later.wait()
+    for copy in (qkv_load, out_load, up_load):
+        copy.start()
     scatter.before()
     low = lax.broadcasted_iota(jnp.int32, (128, 128), 1) < 64
     swap = lambda t: pltpu.roll(t, 64, 1)
     f32 = lambda t: t.astype(jnp.float32)
     attended = []
     for m in range(6):
-        a, b = f32(back_ref[2 * m, 0]), f32(back_ref[2 * m + 1, 0])
-        c, d = f32(back_ref[2 * m, 1]), f32(back_ref[2 * m + 1, 1])
+        a, b = f32(att_ref[2 * m]), f32(att_ref[2 * m + 1])
+        c, d = f32(key_ref[2 * m]), f32(key_ref[2 * m + 1])
         attended.append(jnp.where(low, a, swap(b)).astype(jnp.bfloat16))
         dq = turn(jnp.where(low, swap(a), b), tables_ref, -1.0)
         dk = turn(jnp.where(low, c, swap(d)), tables_ref, -1.0)
@@ -947,7 +942,6 @@
 
 
 def last_part(*args):
-    halves = args[-1].reshape(3, 4, 4, 448, 128)
     bf = lambda *s: jax.ShapeDtypeStruct(s, jnp.bfloat16)
     f32 = lambda *s: jax.ShapeDtypeStruct(s, jnp.float32)
     vm = lambda *s: pltpu.VMEM(s, jnp.bfloat16)
@@ -964,7 +958,7 @@
                         vm(256, 768), vf(80, 128), vf(80, 128), vm(768, 2304), vm(768, 768), vf(2304, 128),
                         dma((5,)), dma((5,)), dma((4,))] + Scatter.scratch(),
         compiler_params=pltpu.CompilerParams(collective_id=1, has_side_effects=True, vmem_limit_bytes=VMEM_LIMIT),
-    )(*args[:-1], halves)
+    )(*args)
 
 
 def finish_kernel(layer_in, input_in, own_in, layer_ref, input_ref, own_ref):
@@ -996,10 +990,11 @@
 def body(tokens, params, out_grad):
     piece = tokens.shape[1]
     x, grad = tokens[0], out_grad[0]
-    gathered = gather(params.reshape(433, 128)).reshape(128, ROWS, 128)
     tables = rotary_tables(lax.axis_index(SEQ) * piece + jnp.arange(piece))
-    mlp, dh2, bias, h1t, in_vec, up_rows, halves_sum, back, w_qkv, w_out = middle_part(gathered, x, grad, tables)
-    results = last_part(back, x, grad, tables, mlp, dh2, bias, in_vec, h1t, w_qkv, w_out, up_rows, halves_sum)
+    mlp, dh2, bias, h1t, in_vec, up_rows, later, att, keys, w_qkv, w_out, _ = middle_part(
+        params.reshape(433, 128), x, grad, tables
+    )
+    results = last_part(att, keys, x, grad, tables, mlp, dh2, bias, in_vec, h1t, w_qkv, w_out, up_rows, later)
     layer_out, input_grad, own_sum = finish(*results)
     param_grad = own_sum.reshape(-1)
     return layer_out[None], input_grad[None], param_grad

time: 148 us -> 143 us (0.966)
  Pallas kernels: 146 us -> 141 us
    pallas_call x1 -> x0, Pallas kernels: 45.3 us -> none  [gather(): pl.pallas_call(gather_kernel, grid=(1,), out_shape=jax.ShapeDtypeStruct((...]
    pallas_call x1, Pallas kernels: 48.1 us -> 89.4 us  [middle_part(): pl.pallas_call(middle_kernel, grid=(1,), out_shape=outs + far, in_specs=[...]
where the time goes in v6:
time: 143 us
  Pallas kernels  141 us (99%)
    pallas_call x1, Pallas kernels, middle_part(): pl.pallas_call(middle_kernel, grid=(1,), out_shape=outs + far, in_specs=[...  89.4 us
    pallas_call x1, Pallas kernels, last_part(): pl.pallas_call(last_kernel, grid=(1,), out_shape=outs, in_specs=[const(*a...  49.6 us

profile of v6, /device:TPU:0, one launch (start us, length us, event | category | flops | bytes accessed | tf_op | source)
XLA Modules:
  0.0 142.9 jit_solution(15567325117004443252)
XLA Ops:
  0.7 0.1 mul.41
  0.8 0.3 fusion.3
  1.1 0.7 pad_maximum_fusion.tables_ref
  1.8 89.4 %shard_map.58 = (f32[128,768]{1,0:T(8,128)}, f32[128,768]{1,0:T(8,128)}, f32[24,128]{1,0:T(8,128)}, bf16[768,128]{1,0:T(8,128)(2,1)}, f32[32,128]{1,0:T(8,128)},...) custom-call(bf16[433,128]{1,0:T(8,128)(2,1)} %bitcast.10, ...), custom_call_target="tpu_custom_call" | custom-call | tf_op jit(solution)/shard_map/pallas_call | solution.py:835
  91.2 49.6 %shard_map.59 = (bf16[128,768]{1,0:T(8,128)(2,1)}, f32[128,768]{1,0:T(8,128)}, f32[448,128]{1,0:T(8,128)}) custom-call(bf16[12,128,128]{2,1,0:T(8,128)(2,1)} %get-tuple-element.20.att_ref, bf16[12,128,128]{2,1,0:T(8,128)(2,1)} %get-tuple-element.21.key_ref, bf16[128,768]{1,0:T(8,128)(2,1)} %bitcast.7, bf16[128,768]{1,0:T(8,128)(2,1)} %bitcast.9, ...), custom_call_target="tpu_custom_call" | custom-call | tf_op jit(solution)/shard_map/pallas_call | solution.py:951
  140.8 2.1 %shard_map.60 = (bf16[128,768]{1,0:T(8,128)(2,1)}, f32[128,768]{1,0:T(8,128)}, f32[433,128]{1,0:T(8,128)}) custom-call(bf16[128,768]{1,0:T(8,128)(2,1)} %get-tuple-element.31.layer_in, f32[128,768]{1,0:T(8,128)} %get-tuple-element.32.input_in, f32[448,128]{1,0:T(8,128)} %get-tuple-element.33.own_in), custom_call_target="tpu_custom_call" | custom-call | tf_op jit(solution)/shard_map/pallas_call | solution.py:972
  (5 shorter events, 0.0 us)

commit v7 on v6

--- a/solution.py
+++ b/solution.py
@@ -187,12 +187,16 @@
         for p in parts:
             self.end(p, "c3")
             self.sibling(p, self.at(p, "c3", 3))
+        for copies in self.sibs:
+            for copy in copies:
+                copy.wait_recv()
+
+    def wait_send(self):
         for copy in self.copies.values():
             copy.wait_send()
         for copies in self.sibs:
             for copy in copies:
                 copy.wait_send()
-                copy.wait_recv()
 
 
 EIGHTH = 16 * 433
@@ -811,11 +815,12 @@
             wide[pl.ds(2 * j, 96, stride=24), :] = result[:, :128]
             wide[pl.ds(2 * j + 1, 96, stride=24), :] = result[:, 128:]
 
-    keep(wide, up_ref)
+    keep(wide.at[pl.ds(0, 2304)], up_ref)
 
     home.wait()
     home_keys.wait()
     there.wait_send()
+    gather.wait_send()
     for copy in (h2_copy, g_copy, act_copy, dup_copy):
         copy.wait_send()
     for copy in stores:
@@ -840,7 +845,7 @@
         out_specs=[const(*o.shape) for o in outs] + [anywhere] * len(far),
         scratch_shapes=[vm(3, 4, 4, 448, 128), vf(4 * EIGHTH + 16, 128), vm(768, 3072), vm(3072, 768), vm(128, 3072),
                         vf(128, 3072), vm(3072, 256), vm(768, 256), vm(256, 768), vm(256, 3072), vf(80, 128), vf(32, 128),
-                        vm(16, 2, 128, 128), vm(16, 128, 128), vm(16, 128, 128), vm(768, 2304), vm(768, 768), vf(2304, 128),
+                        vm(16, 2, 128, 128), vm(16, 128, 128), vm(16, 128, 128), vm(768, 2304), vm(768, 768), vf(2336, 128),
                         vm(HEADS, 2, 128, 128), vm(448, 128)]
         + HEAD_SCRATCH + Exchange.scratch * 3 + [dma((5,)), dma((5,)), dma((8,)), dma((6,))] + Gather.scratch,
         compiler_params=pltpu.CompilerParams(collective_id=2, has_side_effects=True, vmem_limit_bytes=VMEM_LIMIT),

time: 143 us -> 142 us (level)
    pallas_call x1, Pallas kernels: 89.4 us -> 87.8 us  [middle_part(): pl.pallas_call(middle_kernel, grid=(1,), out_shape=outs + far, in_specs=[...]
where the time goes in v7:
time: 142 us
  Pallas kernels  140 us (99%)
    pallas_call x1, Pallas kernels, middle_part(): pl.pallas_call(middle_kernel, grid=(1,), out_shape=outs + far, in_specs=[...  87.8 us
    pallas_call x1, Pallas kernels, last_part(): pl.pallas_call(last_kernel, grid=(1,), out_shape=outs, in_specs=[const(*a...  50.2 us

profile of v7, /device:TPU:0, one launch (start us, length us, event | category | flops | bytes accessed | tf_op | source)
XLA Modules:
  0.0 141.9 jit_solution(12160581257960595162)
XLA Ops:
  0.7 0.1 mul.41
  0.8 0.3 fusion.3
  1.1 0.7 pad_maximum_fusion.tables_ref
  1.8 87.8 %shard_map.58 = (f32[128,768]{1,0:T(8,128)}, f32[128,768]{1,0:T(8,128)}, f32[24,128]{1,0:T(8,128)}, bf16[768,128]{1,0:T(8,128)(2,1)}, f32[32,128]{1,0:T(8,128)},...) custom-call(bf16[433,128]{1,0:T(8,128)(2,1)} %bitcast.10, ...), custom_call_target="tpu_custom_call" | custom-call | tf_op jit(solution)/shard_map/pallas_call | solution.py:840
  89.6 50.2 %shard_map.59 = (bf16[128,768]{1,0:T(8,128)(2,1)}, f32[128,768]{1,0:T(8,128)}, f32[448,128]{1,0:T(8,128)}) custom-call(bf16[12,128,128]{2,1,0:T(8,128)(2,1)} %get-tuple-element.20.att_ref, bf16[12,128,128]{2,1,0:T(8,128)(2,1)} %get-tuple-element.21.key_ref, bf16[128,768]{1,0:T(8,128)(2,1)} %bitcast.7, bf16[128,768]{1,0:T(8,128)(2,1)} %bitcast.9, ...), custom_call_target="tpu_custom_call" | custom-call | tf_op jit(solution)/shard_map/pallas_call | solution.py:956
  139.8 2.1 %shard_map.60 = (bf16[128,768]{1,0:T(8,128)(2,1)}, f32[128,768]{1,0:T(8,128)}, f32[433,128]{1,0:T(8,128)}) custom-call(bf16[128,768]{1,0:T(8,128)(2,1)} %get-tuple-element.31.layer_in, f32[128,768]{1,0:T(8,128)} %get-tuple-element.32.input_in, f32[448,128]{1,0:T(8,128)} %get-tuple-element.33.own_in), custom_call_target="tpu_custom_call" | custom-call | tf_op jit(solution)/shard_map/pallas_call | solution.py:977
  (5 shorter events, 0.0 us)
